TPU v7x, 512 devices: a whole 4x4x16 slice. The times are simulated.
512 devices in a mesh: dp: 32 (over z_lo, y, core), fsdp: 16 (over z_hi, x).
Axes of the slice: x: 4, y: 4, z: 16 (z_hi: 4, z_lo: 4; z = z_hi * 4 + z_lo), core: 2. Of those that a mesh axis runs over, the one named last changes fastest.
Arguments:
- activations: bfloat16 [8192, 4096], P('dp', 'fsdp'), may hold values from -6 to 6
- output_grads: bfloat16 [8192, 4096], P('dp', 'fsdp'), may hold values from -6 to 6
- basis: bfloat16 [4096, 1024], P('fsdp'), may hold values from -0.09375 to 0.09375
- weight: bfloat16 [4096, 4096], P('fsdp'), may hold values from -0.09375 to 0.09375
- first_moment: float32 [4096, 1024], P(('fsdp', 'dp')), may hold values from -0.06 to 0.06
- second_moment: float32 [4096, 1024], P(('fsdp', 'dp')), may hold values from 1e-07 to 1e-05
Outputs:
- new_weight: bfloat16 [4096, 4096], P('fsdp')
- new_first: float32 [4096, 1024], P(('fsdp', 'dp'))
- new_second: float32 [4096, 1024], P(('fsdp', 'dp'))
All inputs are finite; a program needn't handle non-finite values.
Results may differ from a plain program's by a relative error of at most 0.0036.
Values may be sent and summed in bfloat16 or wider, within the bound.
No kernel may reach another device: no remote copies, remote signals or barrier semaphores. Data moves between devices by JAX's collectives and lax.ppermute only.
A program may use at most 64 MiB of HBM per device.

v0:
```python
import jax
import jax.numpy as jnp
from jax import lax
from jax.sharding import PartitionSpec as P

first_decay = 0.9
second_decay = 0.999
first_fix = 1.0 - 0.9**10
second_fix = 1.0 - 0.999**10
step_rate = 0.01
tiny_eps = 1e-08


def times_basis(update, rows):
    return lax.dot_general(
        update, rows, (((1,), (1,)), ((), ())), preferred_element_type=jnp.float32
    )


def local(activations, output_grads, basis, weight, first_moment, second_moment):
    partial_product = jnp.dot(activations, basis, preferred_element_type=jnp.float32)
    projected = lax.psum(partial_product, "fsdp").astype(jnp.bfloat16)
    total_tokens = projected.shape[0] * lax.axis_size("dp")
    local_term = (
        lax.dot_general(
            output_grads, projected, (((0,), (0,)), ((), ())), preferred_element_type=jnp.float32
        )
        / total_tokens
    )
    low_grad = lax.psum_scatter(local_term, "dp", scatter_dimension=0, tiled=True)
    new_first = first_decay * first_moment + (1.0 - first_decay) * low_grad
    new_second = second_decay * second_moment + (1.0 - second_decay) * low_grad * low_grad
    update = (new_first / first_fix / (jnp.sqrt(new_second / second_fix) + tiny_eps)).astype(
        jnp.bfloat16
    )
    all_updates = lax.all_gather(update, "dp", axis=0, tiled=True)
    decoded = times_basis(all_updates, lax.all_gather(basis, "fsdp", axis=0, tiled=True))
    new_weight = (weight.astype(jnp.float32) - step_rate * decoded).astype(jnp.bfloat16)
    return (new_weight, new_first, new_second)


def solution(mesh):
    return jax.shard_map(
        local,
        mesh=mesh,
        in_specs=(
            P("dp", "fsdp"),
            P("dp", "fsdp"),
            P("fsdp", None),
            P("fsdp", None),
            P(("fsdp", "dp"), None),
            P(("fsdp", "dp"), None),
        ),
        out_specs=(P("fsdp", None), P(("fsdp", "dp"), None), P(("fsdp", "dp"), None)),
        check_vma=False,
    )
```

profile of v0, /device:TPU:137, one launch (start us, length us, event | category | flops | bytes accessed | tf_op | source)
XLA Modules:
  0.0 505.1 jit_solution(5039265580081036913)
XLA Ops:
  8.0 0.0 copy-start
  8.0 0.0 copy-start.2
  8.0 0.0 copy-start.1
  8.0 0.0 reduce-scatter.4.cloned.1.call-start
  8.1 0.8 copy-done
  8.9 1.3 fusion.6
  10.3 117.1 %all-reduce.1 = bf16[256,1024]{1,0:T(8,128)(2,1)S(1)} all-reduce(f32[256,1024]{1,0:T(8,128)S(1)} %fusion.6), channel_id=1, replica_groups=mesh['dp'=32,'fsdp'=16] {'fsdp'}, use_global_device_ids=true, to_apply=%region_0.0 | all-reduce | flops 262144 | bytes 1572864 | tf_op jit(solution)/shard_map/psum | solution.py:22
  127.4 1.3 fusion.2
  128.6 0.0 copy-start.3
  128.6 1.3 copy.26
  129.9 0.0 reduce-scatter.4.cloned.1.call-update
  130.0 0.0 all-gather.2.cloned.1.call-start
  130.0 0.5 all-gather.2.cloned.1.call-update
  130.6 307.5 %reduce-scatter.4.cloned.1.call-done = f32[8,1024]{1,0:T(8,128)} async-done(((f32[256,1024]{1,0:T(8,128)}), f32[8,1024]{1,0:T(8,128)}) %reduce-scatter.4.cloned.1.call-update) | async-done | bytes 32784 | tf_op jit(solution)/shard_map/reduce_scatter | solution.py:30
  438.1 0.0 copy-done.2
  438.1 0.0 copy-done.1
  438.1 1.4 divide_convert_fusion
  439.5 51.1 %all_gather.6 = bf16[256,1024]{1,0:T(8,128)(2,1)S(1)} all-gather(bf16[8,1024]{1,0:T(8,128)(2,1)S(1)} %get-tuple-element.9), channel_id=1, replica_groups=mesh['dp'=32,'fsdp'=16] {'dp'}, dimensions={0}, use_global_device_ids=true | all-gather | bytes 540672 | tf_op jit(solution)/shard_map/all_gather | solution.py:36
  490.5 0.0 all-gather.2.cloned.1.call-done
  490.5 0.0 copy-done.3
  490.5 7.1 %fusion.1 = bf16[256,4096]{1,0:T(8,128)(2,1)} fusion(bf16[256,1024]{1,0:T(8,128)(2,1)S(1)} %all_gather.6, bf16[4096,1024]{1,0:T(8,128)(2,1)} %all-gather.2.cloned.1.call-done, bf16[256,4096]{1,0:T(8,128)(2,1)S(1)} %copy-done.3), kind=kOutput, calls=%fused_computation.2 | convolution fusion | flops 2151677952 | bytes 13107200 | tf_op jit(solution)/shard_map/dot_general | solution.py:15
Async XLA Ops:
  8.0 0.9 copy-start
  8.0 430.1 %copy-start.2 = (f32[8,1024]{1,0:T(8,128)S(1)}, f32[8,1024]{1,0:T(8,128)}, u32[]{:S(2)}) copy-start(f32[8,1024]{1,0:T(8,128)} %param.11) | copy-start | bytes 98308
  8.0 430.1 %copy-start.1 = (f32[8,1024]{1,0:T(8,128)S(1)}, f32[8,1024]{1,0:T(8,128)}, u32[]{:S(2)}) copy-start(f32[8,1024]{1,0:T(8,128)} %param.10) | copy-start | bytes 98308
  8.0 430.0 %reduce-scatter.4.cloned.1.call-start = ((), (), s32[]{:S(2)}) async-start(), calls=%async_computation.2 | async-start | bytes 1081344 | tf_op jit(solution)/shard_map/reduce_scatter | solution.py:30
  128.6 361.9 %copy-start.3 = (bf16[256,4096]{1,0:T(8,128)(2,1)S(1)}, bf16[256,4096]{1,0:T(8,128)(2,1)}, u32[]{:S(2)}) copy-start(bf16[256,4096]{1,0:T(8,128)(2,1)} %param.9) | copy-start | bytes 6291460
  130.0 360.6 %all-gather.2.cloned.1.call-start = ((), (), s32[]{:S(2)}) async-start(), calls=%async_computation.1 | async-start | bytes 8912896 | tf_op jit(solution)/shard_map/all_gather | solution.py:37
Sparse Core Ops, SparseCore 0:
  130.1 307.9 reduce-scatter.3
Sparse Core Ops, SparseCore 1:
  133.9 238.0 all-gather.1
where the time goes:
time: 505 us
  waiting for transfers between devices  308 us (61%)
  blocking collectives  168 us (33%)
  between operations  15.5 us (3%)
  matrix products  9.7 us (2%)
    reduce_scatter x1, waiting for transfers between devices, local(): lax.psum_scatter(local_term, 'dp', scatter_dimension=0, tiled=True)  308 us
    psum x1, blocking collectives, local(): projected = lax.psum(partial_product, 'fsdp').astype(jnp.bfloat16)  117 us
    all_gather x1, blocking collectives, local(): all_updates = lax.all_gather(update, 'dp', axis=0, tiled=True)  51.1 us
  transfers between devices with their start and end apart: 2, of which 1 were waited for; matrix products, arithmetic and copies ran while one was open for 0% of the time, Pallas kernels for 0%

commit v1 on v0

v1 whole, which is shorter than its diff:
```python
import jax
import jax.numpy as jnp
from jax import lax
from jax.experimental import pallas as pl
from jax.experimental.pallas import tpu as pltpu
from jax.sharding import Mesh
from jax.sharding import PartitionSpec as P

first_decay = 0.9
second_decay = 0.999
first_fix = 1.0 - 0.9**10
second_fix = 1.0 - 0.999**10
step_rate = 0.01
tiny_eps = 1e-08

AXES = ("zl", "y", "c", "zh", "x")
SIZES = (4, 4, 2, 4, 4)
DP = ("zl", "y", "c")
FSDP = ("zh", "x")
TOKENS = 8192


def exchange_sum(value, axis):
    size = lax.axis_size(axis)
    rows, cols = value.shape
    parts = value.astype(jnp.bfloat16).reshape(size, rows // size, cols)
    parts = lax.all_to_all(parts, axis, 0, 0, tiled=True)
    return jnp.sum(parts.astype(jnp.float32), axis=0)


def gather(value, axis):
    size = lax.axis_size(axis)
    copies = jnp.broadcast_to(value[None], (size,) + value.shape)
    return lax.all_to_all(copies, axis, 0, 0, tiled=True).reshape(
        size * value.shape[0], value.shape[1]
    )


def decode_kernel(core_ref, update_ref, basis_ref, weight_ref, out_ref):
    decoded = lax.dot_general(
        update_ref[...],
        basis_ref[...],
        (((1,), (1,)), ((), ())),
        preferred_element_type=jnp.float32,
    )
    first = core_ref[0] == 0
    for g in range(2):
        left = weight_ref[:, 256 * g : 256 * g + 128]
        right = weight_ref[:, 256 * g + 128 : 256 * g + 256]
        old = jnp.where(first, left.astype(jnp.float32), right.astype(jnp.float32))
        out_ref[:, 128 * g : 128 * g + 128] = (
            old - step_rate * decoded[:, 128 * g : 128 * g + 128]
        ).astype(out_ref.dtype)


def decode_half(core, updates, basis_half, weight):
    rows, rank = updates.shape
    cols = basis_half.shape[0]
    return pl.pallas_call(
        decode_kernel,
        grid_spec=pltpu.PrefetchScalarGridSpec(
            num_scalar_prefetch=1,
            grid=(cols // 256,),
            in_specs=[
                pl.BlockSpec((rows, rank), lambda i, core: (0, 0)),
                pl.BlockSpec((256, rank), lambda i, core: (i, 0)),
                pl.BlockSpec((rows, 512), lambda i, core: (0, i)),
            ],
            out_specs=pl.BlockSpec((rows, 256), lambda i, core: (0, i)),
        ),
        out_shape=jax.ShapeDtypeStruct((rows, cols), weight.dtype),
        compiler_params=pltpu.CompilerParams(vmem_limit_bytes=24 * 1024 * 1024),
        name="decode_half",
    )(core, updates, basis_half, weight)


def merge_kernel(core_ref, mine_ref, other_ref, out_ref):
    first = core_ref[0] == 0
    for g in range(mine_ref.shape[1] // 128):
        mine = mine_ref[:, 128 * g : 128 * g + 128].astype(jnp.float32)
        other = other_ref[:, 128 * g : 128 * g + 128].astype(jnp.float32)
        out_ref[:, 256 * g : 256 * g + 128] = jnp.where(first, mine, other).astype(out_ref.dtype)
        out_ref[:, 256 * g + 128 : 256 * g + 256] = jnp.where(first, other, mine).astype(
            out_ref.dtype
        )


def merge(core, mine, other):
    rows, cols = mine.shape
    return pl.pallas_call(
        merge_kernel,
        grid_spec=pltpu.PrefetchScalarGridSpec(
            num_scalar_prefetch=1,
            grid=(cols // 512,),
            in_specs=[
                pl.BlockSpec((rows, 512), lambda i, core: (0, i)),
                pl.BlockSpec((rows, 512), lambda i, core: (0, i)),
            ],
            out_specs=pl.BlockSpec((rows, 1024), lambda i, core: (0, i)),
        ),
        out_shape=jax.ShapeDtypeStruct((rows, 2 * cols), mine.dtype),
        compiler_params=pltpu.CompilerParams(vmem_limit_bytes=24 * 1024 * 1024),
        name="merge_halves",
    )(core, mine, other)


def local(activations, output_grads, basis, weight, first_moment, second_moment):
    core = lax.axis_index("c")
    half = basis.shape[0] // 2
    my_half = lax.dynamic_slice_in_dim(basis, core * half, half, 0)
    basis_half = lax.all_gather(my_half, FSDP, axis=0, tiled=True)

    partial_product = jnp.dot(activations, basis, preferred_element_type=jnp.float32)
    shared = exchange_sum(exchange_sum(partial_product, "x"), "zh").astype(jnp.bfloat16)
    projected = gather(gather(shared, "zh"), "x")
    local_term = (
        lax.dot_general(
            output_grads, projected, (((0,), (0,)), ((), ())), preferred_element_type=jnp.float32
        )
        / TOKENS
    )
    low_grad = exchange_sum(local_term, DP)
    new_first = first_decay * first_moment + (1.0 - first_decay) * low_grad
    new_second = second_decay * second_moment + (1.0 - second_decay) * low_grad * low_grad
    update = (new_first / first_fix / (jnp.sqrt(new_second / second_fix) + tiny_eps)).astype(
        jnp.bfloat16
    )
    all_updates = gather(update, DP)
    which = jnp.full((1,), core, jnp.int32)
    mine = decode_half(which, all_updates, basis_half, weight)
    other = lax.ppermute(mine, "c", [(0, 1), (1, 0)])
    return (merge(which, mine, other), new_first, new_second)


def solution(mesh):
    named = Mesh(mesh.devices.reshape(SIZES), AXES)
    return jax.shard_map(
        local,
        mesh=named,
        in_specs=(
            P(DP, FSDP),
            P(DP, FSDP),
            P(FSDP, None),
            P(FSDP, None),
            P(FSDP + DP, None),
            P(FSDP + DP, None),
        ),
        out_specs=(P(FSDP, None), P(FSDP + DP, None), P(FSDP + DP, None)),
        check_vma=False,
    )
```

time: 505 us -> 202 us (0.40)
  the two profiles are of different devices: /device:TPU:137 before, /device:TPU:1 now
where the time goes in v1:
time: 202 us; the launch traced here: 201 us
  blocking collectives  171 us (85%)
  between operations  14.1 us (7%)
  Pallas kernels  5.22 us (3%)
  local copies, waits for them, and re-layouts  4.02 us (2%)
  waiting for transfers between devices  2.64 us (1%)
    all_to_all x3, blocking collectives, exchange_sum(): parts = lax.all_to_all(parts, axis, 0, 0, tiled=True)  119 us
    all_to_all x3, blocking collectives, gather(): lax.all_to_all(copies, axis, 0, 0, tiled=True)  51.6 us
  transfers between devices with their start and end apart: 2, of which 1 were waited for; matrix products, arithmetic and copies ran while one was open for 1% of the time, Pallas kernels for 0%

profile of v1, /device:TPU:1, one launch (start us, length us, event | category | flops | bytes accessed | tf_op | source)
XLA Modules:
  0.0 201.2 jit_solution(8561788652448590433)
XLA Ops:
  7.2 0.0 copy-start
  7.2 0.0 all-gather.2.cloned.1.call-start
  7.2 1.0 copy-done
  8.2 0.7 constant_dynamic-slice_fusion
  8.9 0.0 all-gather.2.cloned.1.call-update
  9.0 1.2 convolution_convert_fusion
  10.2 0.0 copy-start.3
  10.2 11.7 %all_to_all.30 = bf16[4,64,1024]{2,1,0:T(8,128)(2,1)S(1)} all-to-all(bf16[4,64,1024]{2,1,0:T(8,128)(2,1)S(1)} %bitcast.16), channel_id=1, replica_groups=mesh['zl'=4,'y'=4,'c'=2,'zh'=4,'x'=4] {'x'}, dimensions={0} | all-to-all | bytes 1048576 | tf_op jit(solution)/shard_map/all_to_all | solution.py:27
  21.9 0.1 reduce_sum.33
  22.0 42.4 %all_to_all.31 = bf16[4,16,1024]{2,1,0:T(8,128)(2,1)S(1)} all-to-all(bf16[4,16,1024]{2,1,0:T(8,128)(2,1)S(1)} %bitcast.18), channel_id=1, replica_groups=mesh['zl'=4,'y'=4,'c'=2,'zh'=4,'x'=4] {'zh'}, dimensions={0} | all-to-all | bytes 262144 | tf_op jit(solution)/shard_map/all_to_all | solution.py:27
  64.5 14.4 %all_to_all.32 = bf16[4,16,1024]{2,1,0:T(8,128)(2,1)S(1)} all-to-all(bf16[4,16,1024]{2,1,0:T(8,128)(2,1)S(1)} %broadcast_in_dim.11), channel_id=1, replica_groups=mesh['zl'=4,'y'=4,'c'=2,'zh'=4,'x'=4] {'zh'}, dimensions={0} | all-to-all | bytes 262144 | tf_op jit(solution)/shard_map/all_to_all | solution.py:34
  79.0 10.0 %all_to_all.33 = bf16[4,64,1024]{2,1,0:T(8,128)(2,1)S(1)} all-to-all(bf16[4,64,1024]{2,1,0:T(8,128)(2,1)S(1)} %broadcast_in_dim.25), channel_id=1, replica_groups=mesh['zl'=4,'y'=4,'c'=2,'zh'=4,'x'=4] {'x'}, dimensions={0} | all-to-all | bytes 1048576 | tf_op jit(solution)/shard_map/all_to_all | solution.py:34
  89.0 0.0 copy-done.3
  89.0 0.3 fusion.1
  89.3 65.1 %all_to_all.34 = bf16[32,8,1024]{2,1,0:T(8,128)(2,1)S(1)} all-to-all(bf16[32,8,1024]{2,1,0:T(8,128)(2,1)S(1)} %fusion.1), channel_id=1, replica_groups=mesh['zl'=4,'y'=4,'c'=2,'zh'=4,'x'=4] {'zl','y','c'}, dimensions={0} | all-to-all | bytes 1048576 | tf_op jit(solution)/shard_map/all_to_all | solution.py:27
  154.4 0.1 convert_reduce_fusion
  154.5 0.0 copy-done.4
  154.5 0.6 divide_convert_fusion
  155.2 27.2 %all_to_all.35 = bf16[32,8,1024]{2,1,0:T(8,128)(2,1)S(1)} all-to-all(bf16[32,8,1024]{2,1,0:T(8,128)(2,1)S(1)} %broadcast_in_dim.26), channel_id=1, replica_groups=mesh['zl'=4,'y'=4,'c'=2,'zh'=4,'x'=4] {'zl','y','c'}, dimensions={0} | all-to-all | bytes 1048576 | tf_op jit(solution)/shard_map/all_to_all | solution.py:34
  182.4 2.2 %copy-done.1 = bf16[2048,1024]{1,0:T(8,128)(2,1)S(1)} copy-done((bf16[2048,1024]{1,0:T(8,128)(2,1)S(1)}, bf16[2048,1024]{1,0:T(8,128)(2,1)}, u32[]{:S(2)}) %copy-start.1) | copy-done | bytes 4194328
  184.5 3.0 %decode_half.1.mine_ref = bf16[256,2048]{1,0:T(8,128)(2,1)S(1)} custom-call(s32[1]{0:T(128)} %bitcast.core_ref, bf16[256,1024]{1,0:T(8,128)(2,1)S(1)} %bitcast.14, bf16[2048,1024]{1,0:T(8,128)(2,1)S(1)} %copy-done.1, bf16[256,4096]{1,0:T(8,128)(2,1)S(1)} %copy-done.2), custom_call_target="tpu_custom_call" | custom-call | tf_op jit(solution)/shard_map/decode_half/pallas_call | solution.py:59
  187.6 1.9 collective-permute-start
  189.5 2.6 %collective-permute-done.other_ref = bf16[256,2048]{1,0:T(8,128)(2,1)S(1)} collective-permute-done((bf16[256,2048]{1,0:T(8,128)(2,1)S(1)}, bf16[256,2048]{1,0:T(8,128)(2,1)S(1)}, u32[]{:S(2)}, u32[]{:S(2)}) %collective-permute-start) | collective-permute-done | bytes 1048608 | tf_op jit(solution)/shard_map/ppermute | solution.py:131
  192.2 2.2 %merge_halves.1 = bf16[256,4096]{1,0:T(8,128)(2,1)} custom-call(s32[1]{0:T(128)} %bitcast.core_ref, bf16[256,2048]{1,0:T(8,128)(2,1)S(1)} %decode_half.1.mine_ref, bf16[256,2048]{1,0:T(8,128)(2,1)S(1)} %collective-permute-done.other_ref), custom_call_target="tpu_custom_call" | custom-call | tf_op jit(solution)/shard_map/merge_halves/pallas_call | solution.py:90
  (11 shorter events, 0.1 us)
Async XLA Ops:
  7.2 1.0 copy-start
  7.2 175.2 %all-gather.2.cloned.1.call-start = ((), (), s32[]{:S(2)}) async-start(), calls=%async_computation.6 | async-start | bytes 4456448 | tf_op jit(solution)/shard_map/all_gather | solution.py:111
  10.2 78.8 %copy-start.3 = (bf16[256,256]{1,0:T(8,128)(2,1)S(1)}, bf16[256,256]{1,0:T(8,128)(2,1)}, u32[]{:S(2)}) copy-start(bf16[256,256]{1,0:T(8,128)(2,1)} %param.7) | copy-start | bytes 393220
  78.9 75.6 %copy-start.4 = (f32[8,1024]{1,0:T(8,128)S(1)}, f32[8,1024]{1,0:T(8,128)}, u32[]{:S(2)}) copy-start(f32[8,1024]{1,0:T(8,128)} %param.10) | copy-start | bytes 98308
  78.9 75.6 %copy-start.5 = (f32[8,1024]{1,0:T(8,128)S(1)}, f32[8,1024]{1,0:T(8,128)}, u32[]{:S(2)}) copy-start(f32[8,1024]{1,0:T(8,128)} %param.11) | copy-start | bytes 98308
  89.0 93.4 %copy-start.2 = (bf16[256,4096]{1,0:T(8,128)(2,1)S(1)}, bf16[256,4096]{1,0:T(8,128)(2,1)}, u32[]{:S(2)}) copy-start(bf16[256,4096]{1,0:T(8,128)(2,1)} %weight_ref.1) | copy-start | bytes 6291460
  182.4 2.2 %copy-start.1 = (bf16[2048,1024]{1,0:T(8,128)(2,1)S(1)}, bf16[2048,1024]{1,0:T(8,128)(2,1)}, u32[]{:S(2)}) copy-start(bf16[2048,1024]{1,0:T(8,128)(2,1)} %all-gather.2.cloned.1.call-done.basis_ref) | copy-start | bytes 12582916
  187.6 4.6 %collective-permute-start = (bf16[256,2048]{1,0:T(8,128)(2,1)S(1)}, bf16[256,2048]{1,0:T(8,128)(2,1)S(1)}, u32[]{:S(2)}, u32[]{:S(2)}) collective-permute-start(bf16[256,2048]{1,0:T(8,128)(2,1)S(1)} %decode_half.1.mine_ref), channel_id=1, source_target_pairs={{0,16},{16,0},{1,17},{17,1},{2,18},{18,2},{3,19},{19,3},{4,20},{20... | collective-permute-start | bytes 3145736 | tf_op jit(solution)/shard_map/ppermute | solution.py:131
Sparse Core Ops, SparseCore 0:
  11.6 140.6 all-gather.1

commit v2 on v0

v2 whole, which is shorter than its diff:
```python
import jax
import jax.numpy as jnp
from jax import lax
from jax.experimental import pallas as pl
from jax.experimental.pallas import tpu as pltpu
from jax.sharding import Mesh
from jax.sharding import PartitionSpec as P

first_decay = 0.9
second_decay = 0.999
first_fix = 1.0 - 0.9**10
second_fix = 1.0 - 0.999**10
step_rate = 0.01
tiny_eps = 1e-08

AXES = ("zl", "y", "c", "zh", "x")
SIZES = (4, 4, 2, 4, 4)
DP = ("zl", "y", "c")
FSDP = ("zh", "x")
TOKENS = 8192


def exchange_sum(value, axis):
    size = lax.axis_size(axis)
    rows, cols = value.shape
    parts = value.astype(jnp.bfloat16).reshape(size, rows // size, cols)
    parts = lax.all_to_all(parts, axis, 0, 0, tiled=True)
    return jnp.sum(parts.astype(jnp.float32), axis=0)


def gather(value, axis):
    size = lax.axis_size(axis)
    copies = jnp.broadcast_to(value[None], (size,) + value.shape)
    return lax.all_to_all(copies, axis, 0, 0, tiled=True).reshape(
        size * value.shape[0], value.shape[1]
    )


def decode_kernel(update_ref, basis_ref, weight_ref, out_ref):
    rank = update_ref.shape[-1]
    cols = out_ref.shape[1]
    updates = update_ref[...].reshape(-1, rank)
    decoded = lax.dot_general(
        updates,
        basis_ref[...].reshape(cols, rank),
        (((1,), (1,)), ((), ())),
        preferred_element_type=jnp.float32,
    )
    decoded = decoded.reshape(2, -1, 8, cols)
    decoded = jnp.stack([decoded[0], decoded[1]], axis=1).reshape(-1, cols)
    out_ref[...] = (weight_ref[...].astype(jnp.float32) - step_rate * decoded).astype(
        out_ref.dtype
    )


def decode(updates, basis_pieces, weight):
    rows, cols = weight.shape
    two, ys, xs, zhs, piece, rank = basis_pieces.shape
    width = two * ys * piece
    return pl.pallas_call(
        decode_kernel,
        grid=(cols // width,),
        in_specs=[
            pl.BlockSpec(updates.shape, lambda i: (0, 0, 0)),
            pl.BlockSpec((two, ys, 1, 1, piece, rank), lambda i: (0, 0, i % xs, i // xs, 0, 0)),
            pl.BlockSpec((rows, width), lambda i: (0, i)),
        ],
        out_specs=pl.BlockSpec((rows, width), lambda i: (0, i)),
        out_shape=jax.ShapeDtypeStruct((rows, cols), weight.dtype),
        compiler_params=pltpu.CompilerParams(vmem_limit_bytes=56 * 1024 * 1024),
        name="decode",
    )(updates, basis_pieces, weight)


def local(activations, output_grads, basis, weight, first_moment, second_moment):
    core = lax.axis_index("c")
    piece = basis.shape[0] // 8
    mine = lax.dynamic_slice_in_dim(basis, (core * 4 + lax.axis_index("y")) * piece, piece, 0)
    mine = lax.all_gather(mine, "zh", axis=0, tiled=True)
    basis_pieces = lax.all_gather(mine, ("c", "y", "x"), axis=0, tiled=True).reshape(
        2, 4, 4, 4, piece, -1
    )

    partial_product = jnp.dot(activations, basis, preferred_element_type=jnp.float32)
    over_x = exchange_sum(partial_product, "x").astype(jnp.bfloat16)
    rows, rank = over_x.shape
    over_all = gather(over_x, "zh").reshape(4, rows, rank)
    block = jnp.sum(over_all.astype(jnp.float32), axis=0).astype(jnp.bfloat16)
    projected = gather(block, "x")
    local_term = (
        lax.dot_general(
            output_grads, projected, (((0,), (0,)), ((), ())), preferred_element_type=jnp.float32
        )
        / TOKENS
    )
    parts = local_term.reshape(-1, 2, 8, rank)
    keep = lax.dynamic_index_in_dim(parts, core, 1, keepdims=False)
    send = lax.dynamic_index_in_dim(parts, 1 - core, 1, keepdims=False).astype(jnp.bfloat16)
    sent = lax.all_gather(send, "c", axis=0)
    received = lax.dynamic_index_in_dim(sent, 1 - core, 0, keepdims=False)
    chip_term = keep + received.astype(jnp.float32)
    low_grad = exchange_sum(chip_term.reshape(-1, rank), ("zl", "y"))
    new_first = first_decay * first_moment + (1.0 - first_decay) * low_grad
    new_second = second_decay * second_moment + (1.0 - second_decay) * low_grad * low_grad
    update = (new_first / first_fix / (jnp.sqrt(new_second / second_fix) + tiny_eps)).astype(
        jnp.bfloat16
    )
    updates = lax.all_gather(gather(update, ("zl", "y")), "c", axis=0)
    return (decode(updates, basis_pieces, weight), new_first, new_second)


def solution(mesh):
    named = Mesh(mesh.devices.reshape(SIZES), AXES)
    return jax.shard_map(
        local,
        mesh=named,
        in_specs=(
            P(DP, FSDP),
            P(DP, FSDP),
            P(FSDP, None),
            P(FSDP, None),
            P(FSDP + DP, None),
            P(FSDP + DP, None),
        ),
        out_specs=(P(FSDP, None), P(FSDP + DP, None), P(FSDP + DP, None)),
        check_vma=False,
    )
```

time: 505 us -> 162 us (0.32)
  the two profiles are of different devices: /device:TPU:137 before, /device:TPU:1 now
where the time goes in v2:
time: 162 us
  blocking collectives  119 us (73%)
  between operations  14.1 us (9%)
  Pallas kernels  13.4 us (8%)
  waiting for transfers between devices  6.92 us (4%)
  starting transfers between devices  3.51 us (2%)
  local copies, waits for them, and re-layouts  1.97 us (1%)
    all_to_all x2, blocking collectives, gather(): lax.all_to_all(copies, axis, 0, 0, tiled=True)  37.6 us
    all_to_all x2, blocking collectives, exchange_sum(): parts = lax.all_to_all(parts, axis, 0, 0, tiled=True)  32.6 us
    all_gather x1, blocking collectives, local(): mine = lax.all_gather(mine, 'zh', axis=0, tiled=True)  25.6 us
    all_gather x1, blocking collectives, local(): sent = lax.all_gather(send, 'c', axis=0)  19.1 us
    pallas_call x1, Pallas kernels, decode(): pl.pallas_call(decode_kernel, grid=(cols // width,), in_specs=[pl.BlockSp...  13.4 us
    all_to_all x1, waiting for transfers between devices, gather(): lax.all_to_all(copies, axis, 0, 0, tiled=True)  6.9 us
    all_gather x1, blocking collectives, local(): updates = lax.all_gather(gather(update, ('zl', 'y')), 'c', axis=0)  4.34 us
    all_to_all x1, starting transfers between devices, gather(): lax.all_to_all(copies, axis, 0, 0, tiled=True)  3.47 us
  transfers between devices with their start and end apart: 2, of which 1 were waited for; matrix products, arithmetic and copies ran while one was open for 2% of the time, Pallas kernels for 0%

profile of v2, /device:TPU:1, one launch (start us, length us, event | category | flops | bytes accessed | tf_op | source)
XLA Modules:
  0.0 161.5 jit_solution(12663521751066063092)
XLA Ops:
  7.2 0.0 copy-start
  7.2 0.0 all-gather.3.cloned.1.call-start
  7.2 1.0 copy-done
  8.2 25.6 %all_gather.15 = bf16[128,1024]{1,0:T(8,128)(2,1)} all-gather(bf16[32,1024]{1,0:T(8,128)(2,1)S(1)} %constant_dynamic-slice_fusion), channel_id=1, replica_groups=mesh['zl'=4,'y'=4,'c'=2,'zh'=4,'x'=4] {'zh'}, dimensions={0}, use_global_device_ids=true | all-gather | bytes 327680 | tf_op jit(solution)/shard_map/all_gather | solution.py:79
  33.8 0.0 all-gather.3.cloned.1.call-update
  33.8 1.2 convolution_convert_fusion
  35.0 10.7 %all_to_all.25 = bf16[4,64,1024]{2,1,0:T(8,128)(2,1)S(1)} all-to-all(bf16[4,64,1024]{2,1,0:T(8,128)(2,1)S(1)} %bitcast.21), channel_id=1, replica_groups=mesh['zl'=4,'y'=4,'c'=2,'zh'=4,'x'=4] {'x'}, dimensions={0} | all-to-all | bytes 1048576 | tf_op jit(solution)/shard_map/all_to_all | solution.py:27
  45.8 0.1 reduce_sum.33
  45.9 0.0 copy-start.1
  45.9 0.1 broadcast_in_dim.6
  45.9 24.3 %all_to_all.26 = bf16[4,64,1024]{2,1,0:T(8,128)(2,1)S(1)} all-to-all(bf16[4,64,1024]{2,1,0:T(8,128)(2,1)S(1)} %broadcast_in_dim.6), channel_id=1, replica_groups=mesh['zl'=4,'y'=4,'c'=2,'zh'=4,'x'=4] {'zh'}, dimensions={0} | all-to-all | bytes 1048576 | tf_op jit(solution)/shard_map/all_to_all | solution.py:34
  70.3 0.1 reduce_sum.34
  70.3 0.9 broadcast_in_dim.7
  71.2 3.5 %all-to-all-start.2 = ((bf16[4,64,1024]{2,1,0:T(8,128)(2,1)}), bf16[4,64,1024]{2,1,0:T(8,128)(2,1)S(1)}, u32[]{:S(2)}, u32[]{:S(2)}) async-start(bf16[4,64,1024]{2,1,0:T(8,128)(2,1)} %broadcast_in_dim.7), calls=%async_computation.2 | async-start | bytes 1048576 | tf_op jit(solution)/shard_map/all_to_all | solution.py:34
  74.7 6.9 %all-to-all-done.2 = bf16[4,64,1024]{2,1,0:T(8,128)(2,1)S(1)} async-done(((bf16[4,64,1024]{2,1,0:T(8,128)(2,1)}), bf16[4,64,1024]{2,1,0:T(8,128)(2,1)S(1)}, u32[]{:S(2)}, u32[]{:S(2)}) %all-to-all-start.2) | async-done | bytes 524320 | tf_op jit(solution)/shard_map/all_to_all | solution.py:34
  81.6 0.0 copy-done.1
  81.6 0.3 convolution_multiply_fusion
  82.0 19.1 %all-gather = bf16[32,1,8,1024]{3,2,1,0:T(8,128)(2,1)S(1)} all-gather(bf16[16,1,8,1024]{3,2,1,0:T(8,128)(2,1)S(1)} %dynamic-slice_convert_fusion), channel_id=2, replica_groups=mesh['zl'=4,'y'=4,'c'=2,'zh'=4,'x'=4] {'c'}, dimensions={0}, use_global_device_ids=true | all-gather | bytes 786432 | tf_op jit(solution)/shard_map/all_gather | solution.py:99
  101.0 0.1 fusion
  101.1 21.8 %all_to_all.27 = bf16[16,8,1024]{2,1,0:T(8,128)(2,1)S(1)} all-to-all(bf16[16,8,1024]{2,1,0:T(8,128)(2,1)S(1)} %fusion), channel_id=1, replica_groups=mesh['zl'=4,'y'=4,'c'=2,'zh'=4,'x'=4] {'zl','y'}, dimensions={0} | all-to-all | bytes 524288 | tf_op jit(solution)/shard_map/all_to_all | solution.py:27
  123.0 0.6 divide_convert_fusion
  123.7 13.2 %all_to_all.28 = bf16[16,8,1024]{2,1,0:T(8,128)(2,1)S(1)} all-to-all(bf16[16,8,1024]{2,1,0:T(8,128)(2,1)S(1)} %broadcast_in_dim.8), channel_id=1, replica_groups=mesh['zl'=4,'y'=4,'c'=2,'zh'=4,'x'=4] {'zl','y'}, dimensions={0} | all-to-all | bytes 524288 | tf_op jit(solution)/shard_map/all_to_all | solution.py:34
  136.9 4.3 %all_gather.14.update_ref = bf16[2,128,1024]{2,1,0:T(8,128)(2,1)} all-gather(bf16[1,128,1024]{2,1,0:T(8,128)(2,1)S(1)} %bitcast.23), channel_id=1, replica_groups=mesh['zl'=4,'y'=4,'c'=2,'zh'=4,'x'=4] {'c'}, dimensions={0}, use_global_device_ids=true | all-gather | bytes 786432 | tf_op jit(solution)/shard_map/all_gather | solution.py:108
  141.2 13.4 %decode.1 = bf16[256,4096]{1,0:T(8,128)(2,1)} custom-call(bf16[2,128,1024]{2,1,0:T(8,128)(2,1)} %all_gather.14.update_ref, bf16[2,4,4,4,32,1024]{5,4,3,2,1,0:T(8,128)(2,1)} %bitcast.17, bf16[256,4096]{1,0:T(8,128)(2,1)} %weight_ref.1), custom_call_target="tpu_custom_call" | custom-call | tf_op jit(solution)/shard_map/decode/pallas_call | solution.py:60
  (9 shorter events, 0.1 us)
Async XLA Ops:
  7.2 1.0 copy-start
  7.2 134.1 %all-gather.3.cloned.1.call-start = ((), (), s32[]{:S(2)}) async-start(), calls=%async_computation.5 | async-start | bytes 8650752 | tf_op jit(solution)/shard_map/all_gather | solution.py:80
  45.9 35.7 %copy-start.1 = (bf16[256,256]{1,0:T(8,128)(2,1)S(1)}, bf16[256,256]{1,0:T(8,128)(2,1)}, u32[]{:S(2)}) copy-start(bf16[256,256]{1,0:T(8,128)(2,1)} %param.7) | copy-start | bytes 393220
  71.2 10.4 %all-to-all-start.2 = ((bf16[4,64,1024]{2,1,0:T(8,128)(2,1)}), bf16[4,64,1024]{2,1,0:T(8,128)(2,1)S(1)}, u32[]{:S(2)}, u32[]{:S(2)}) async-start(bf16[4,64,1024]{2,1,0:T(8,128)(2,1)} %broadcast_in_dim.7), calls=%async_computation.2 | async-start | bytes 1048576 | tf_op jit(solution)/shard_map/all_to_all | solution.py:34
  81.6 41.4 %copy-start.2 = (f32[8,1024]{1,0:T(8,128)S(1)}, f32[8,1024]{1,0:T(8,128)}, u32[]{:S(2)}) copy-start(f32[8,1024]{1,0:T(8,128)} %param.10) | copy-start | bytes 98308
  81.6 41.4 %copy-start.3 = (f32[8,1024]{1,0:T(8,128)S(1)}, f32[8,1024]{1,0:T(8,128)}, u32[]{:S(2)}) copy-start(f32[8,1024]{1,0:T(8,128)} %param.11) | copy-start | bytes 98308
Sparse Core Ops, SparseCore 0:
  33.9 70.1 all-gather.2

commit v3 on v2

--- a/solution.py
+++ b/solution.py
@@ -36,38 +36,52 @@
     )
 
 
-def decode_kernel(update_ref, basis_ref, weight_ref, out_ref):
-    rank = update_ref.shape[-1]
-    cols = out_ref.shape[1]
+STEP = 2
+
+
+def decode_kernel(update_ref, basis_ref, weight_ref, out_ref, new, sems):
+    two, ys, xs, zhs, piece, rank = basis_ref.shape
+    shard = two * ys * piece
+    cols = STEP * shard
+
+    def copy_out(i):
+        where = pl.ds(i * cols, cols)
+        return pltpu.make_async_copy(new.at[:, where], out_ref.at[:, where], sems.at[i])
+
     updates = update_ref[...].reshape(-1, rank)
-    decoded = lax.dot_general(
-        updates,
-        basis_ref[...].reshape(cols, rank),
-        (((1,), (1,)), ((), ())),
-        preferred_element_type=jnp.float32,
-    )
-    decoded = decoded.reshape(2, -1, 8, cols)
-    decoded = jnp.stack([decoded[0], decoded[1]], axis=1).reshape(-1, cols)
-    out_ref[...] = (weight_ref[...].astype(jnp.float32) - step_rate * decoded).astype(
-        out_ref.dtype
-    )
+    steps = xs * zhs // STEP
+    for i in range(steps):
+        shards = [
+            basis_ref[:, :, f % xs, f // xs].reshape(shard, rank)
+            for f in range(i * STEP, (i + 1) * STEP)
+        ]
+        decoded = lax.dot_general(
+            updates,
+            jnp.concatenate(shards, axis=0),
+            (((1,), (1,)), ((), ())),
+            preferred_element_type=jnp.float32,
+        )
+        decoded = decoded.reshape(2, -1, 8, cols)
+        decoded = jnp.stack([decoded[0], decoded[1]], axis=1).reshape(-1, cols)
+        old = weight_ref[:, i * cols : (i + 1) * cols].astype(jnp.float32)
+        new[:, i * cols : (i + 1) * cols] = (old - step_rate * decoded).astype(new.dtype)
+        copy_out(i).start()
+    for i in range(steps):
+        copy_out(i).wait()
 
 
 def decode(updates, basis_pieces, weight):
-    rows, cols = weight.shape
-    two, ys, xs, zhs, piece, rank = basis_pieces.shape
-    width = two * ys * piece
+    steps = basis_pieces.shape[2] * basis_pieces.shape[3] // STEP
     return pl.pallas_call(
         decode_kernel,
-        grid=(cols // width,),
-        in_specs=[
-            pl.BlockSpec(updates.shape, lambda i: (0, 0, 0)),
-            pl.BlockSpec((two, ys, 1, 1, piece, rank), lambda i: (0, 0, i % xs, i // xs, 0, 0)),
-            pl.BlockSpec((rows, width), lambda i: (0, i)),
+        in_specs=[pl.BlockSpec(memory_space=pltpu.VMEM)] * 3,
+        out_specs=pl.BlockSpec(memory_space=pl.ANY),
+        out_shape=jax.ShapeDtypeStruct(weight.shape, weight.dtype),
+        scratch_shapes=[
+            pltpu.VMEM(weight.shape, weight.dtype),
+            pltpu.SemaphoreType.DMA((steps,)),
         ],
-        out_specs=pl.BlockSpec((rows, width), lambda i: (0, i)),
-        out_shape=jax.ShapeDtypeStruct((rows, cols), weight.dtype),
-        compiler_params=pltpu.CompilerParams(vmem_limit_bytes=56 * 1024 * 1024),
+        compiler_params=pltpu.CompilerParams(vmem_limit_bytes=24 * 1024 * 1024),
         name="decode",
     )(updates, basis_pieces, weight)
 
@@ -76,17 +90,19 @@
     core = lax.axis_index("c")
     piece = basis.shape[0] // 8
     mine = lax.dynamic_slice_in_dim(basis, (core * 4 + lax.axis_index("y")) * piece, piece, 0)
-    mine = lax.all_gather(mine, "zh", axis=0, tiled=True)
-    basis_pieces = lax.all_gather(mine, ("c", "y", "x"), axis=0, tiled=True).reshape(
-        2, 4, 4, 4, piece, -1
-    )
 
     partial_product = jnp.dot(activations, basis, preferred_element_type=jnp.float32)
     over_x = exchange_sum(partial_product, "x").astype(jnp.bfloat16)
-    rows, rank = over_x.shape
-    over_all = gather(over_x, "zh").reshape(4, rows, rank)
-    block = jnp.sum(over_all.astype(jnp.float32), axis=0).astype(jnp.bfloat16)
-    projected = gather(block, "x")
+    rank = over_x.shape[1]
+    parts = over_x.reshape(4, -1, rank)
+    rows = parts.shape[1]
+    copies = jnp.broadcast_to(mine[None], (4,) + mine.shape)
+    both = lax.all_to_all(jnp.concatenate([parts, copies], axis=1), "zh", 0, 0, tiled=True)
+    basis_pieces = lax.all_gather(
+        both[:, rows:].reshape(-1, rank), ("c", "y", "x"), axis=0, tiled=True
+    ).reshape(2, 4, 4, 4, piece, rank)
+    block = jnp.sum(both[:, :rows].astype(jnp.float32), axis=0).astype(jnp.bfloat16)
+    projected = gather(gather(block, "zh"), "x")
     local_term = (
         lax.dot_general(
             output_grads, projected, (((0,), (0,)), ((), ())), preferred_element_type=jnp.float32

time: 162 us -> 146 us (0.901)
  blocking collectives: 119 us -> 95 us
  Pallas kernels: 13.4 us -> 3.14 us
  waiting for transfers between devices: 6.92 us -> 15.9 us
  starting transfers between devices: 3.51 us -> 8.32 us
  local copies, waits for them, and re-layouts: 1.97 us -> 6.13 us
    all_to_all x0 -> x1, blocking collectives: none -> 33.4 us  [local(): lax.all_to_all(jnp.concatenate([parts, copies], axis=1), 'zh', 0, 0, tile...]
    all_gather x1 -> x0, blocking collectives: 25.6 us -> none  [local(): mine = lax.all_gather(mine, 'zh', axis=0, tiled=True)]
    all_to_all x2 -> x1, blocking collectives: 32.6 us -> 16.6 us  [exchange_sum(): parts = lax.all_to_all(parts, axis, 0, 0, tiled=True)]
    pallas_call x1, Pallas kernels: 13.4 us -> 3.14 us  [decode(): pl.pallas_call(decode_kernel, in_specs=[pl.BlockSpec(memory_space=pltpu.V...]
    all_gather x1, blocking collectives: 19.1 us -> 9.12 us  [local(): sent = lax.all_gather(send, 'c', axis=0)]
    all_to_all x0 -> x1, waiting for transfers between devices: none -> 6.92 us  [exchange_sum(): parts = lax.all_to_all(parts, axis, 0, 0, tiled=True)]
    all_to_all x2, blocking collectives: 37.6 us -> 31.6 us  [gather(): lax.all_to_all(copies, axis, 0, 0, tiled=True)]
    all_to_all x0 -> x1, starting transfers between devices: none -> 4.84 us  [exchange_sum(): parts = lax.all_to_all(parts, axis, 0, 0, tiled=True)]
  transfers between devices with their start and end apart: 2 -> 3, of which waited for: 1 -> 2; matrix products, arithmetic and copies ran while one was open for 2% -> 1% of each run, Pallas kernels for 0% -> 0%
where the time goes in v3:
time: 146 us
  blocking collectives  95 us (65%)
  waiting for transfers between devices  15.9 us (11%)
  between operations  14.2 us (10%)
  starting transfers between devices  8.32 us (6%)
  local copies, waits for them, and re-layouts  6.13 us (4%)
  Pallas kernels  3.14 us (2%)
  matrix products  2.34 us (2%)
    all_to_all x1, blocking collectives, local(): lax.all_to_all(jnp.concatenate([parts, copies], axis=1), 'zh', 0, 0, tile...  33.4 us
    all_to_all x2, blocking collectives, gather(): lax.all_to_all(copies, axis, 0, 0, tiled=True)  31.6 us
    all_to_all x1, blocking collectives, exchange_sum(): parts = lax.all_to_all(parts, axis, 0, 0, tiled=True)  16.6 us
    all_gather x1, blocking collectives, local(): sent = lax.all_gather(send, 'c', axis=0)  9.12 us
    all_to_all x1, waiting for transfers between devices, gather(): lax.all_to_all(copies, axis, 0, 0, tiled=True)  8.92 us
    all_to_all x1, waiting for transfers between devices, exchange_sum(): parts = lax.all_to_all(parts, axis, 0, 0, tiled=True)  6.92 us
    all_to_all x1, starting transfers between devices, exchange_sum(): parts = lax.all_to_all(parts, axis, 0, 0, tiled=True)  4.84 us
    unnamed x12, local copies, waits for them, and re-layouts  4.44 us
  transfers between devices with their start and end apart: 3, of which 2 were waited for; matrix products, arithmetic and copies ran while one was open for 1% of the time, Pallas kernels for 0%

profile of v3, /device:TPU:1, one launch (start us, length us, event | category | flops | bytes accessed | tf_op | source)
XLA Modules:
  0.0 145.9 jit_solution(569199693964734240)
XLA Ops:
  7.2 0.0 copy-start
  7.2 1.0 copy-done
  8.2 2.0 %convolution_convert_fusion = bf16[256,1024]{1,0:T(8,128)(2,1)} fusion(bf16[256,256]{1,0:T(8,128)(2,1)} %param.6, bf16[256,1024]{1,0:T(8,128)(2,1)S(1)} %copy-done), kind=kOutput, calls=%fused_computation.1 | convolution fusion | flops 134479872 | bytes 1179648 | tf_op jit(solution)/shard_map/dot_general | solution.py:94
  10.2 4.8 %all-to-all-start = ((bf16[4,64,1024]{2,1,0:T(8,128)(2,1)}), bf16[4,64,1024]{2,1,0:T(8,128)(2,1)S(1)}, u32[]{:S(2)}, u32[]{:S(2)}) async-start(bf16[4,64,1024]{2,1,0:T(8,128)(2,1)} %bitcast), calls=%async_computation | async-start | bytes 1048576 | tf_op jit(solution)/shard_map/all_to_all | solution.py:27
  15.1 6.9 %all-to-all-done = bf16[4,64,1024]{2,1,0:T(8,128)(2,1)S(1)} async-done(((bf16[4,64,1024]{2,1,0:T(8,128)(2,1)}), bf16[4,64,1024]{2,1,0:T(8,128)(2,1)S(1)}, u32[]{:S(2)}, u32[]{:S(2)}) %all-to-all-start) | async-done | bytes 524320 | tf_op jit(solution)/shard_map/all_to_all | solution.py:27
  22.0 0.1 reduce_sum.33
  22.1 0.0 copy-start.3
  22.1 33.4 %all_to_all.30 = bf16[4,48,1024]{2,1,0:T(8,128)(2,1)S(1)} all-to-all(bf16[4,48,1024]{2,1,0:T(8,128)(2,1)S(1)} %pad_maximum_fusion), channel_id=1, replica_groups=mesh['zl'=4,'y'=4,'c'=2,'zh'=4,'x'=4] {'zh'}, dimensions={0} | all-to-all | bytes 786432 | tf_op jit(solution)/shard_map/all_to_all | solution.py:100
  55.5 0.7 slice.9
  56.3 0.0 all-gather.3.cloned.1.call-update
  56.3 18.5 %all_to_all.31 = bf16[4,16,1024]{2,1,0:T(8,128)(2,1)S(1)} all-to-all(bf16[4,16,1024]{2,1,0:T(8,128)(2,1)S(1)} %broadcast_in_dim.11), channel_id=1, replica_groups=mesh['zl'=4,'y'=4,'c'=2,'zh'=4,'x'=4] {'zh'}, dimensions={0} | all-to-all | bytes 262144 | tf_op jit(solution)/shard_map/all_to_all | solution.py:34
  74.8 0.9 broadcast_in_dim.13
  75.7 3.5 %all-to-all-start.3 = ((bf16[4,64,1024]{2,1,0:T(8,128)(2,1)}), bf16[4,64,1024]{2,1,0:T(8,128)(2,1)S(1)}, u32[]{:S(2)}, u32[]{:S(2)}) async-start(bf16[4,64,1024]{2,1,0:T(8,128)(2,1)} %broadcast_in_dim.13), calls=%async_computation.3 | async-start | bytes 1048576 | tf_op jit(solution)/shard_map/all_to_all | solution.py:34
  79.2 8.9 %all-to-all-done.3 = bf16[4,64,1024]{2,1,0:T(8,128)(2,1)S(1)} async-done(((bf16[4,64,1024]{2,1,0:T(8,128)(2,1)}), bf16[4,64,1024]{2,1,0:T(8,128)(2,1)S(1)}, u32[]{:S(2)}, u32[]{:S(2)}) %all-to-all-start.3) | async-done | bytes 524320 | tf_op jit(solution)/shard_map/all_to_all | solution.py:34
  88.1 0.3 convolution_multiply_fusion
  88.5 0.0 copy-start.2
  88.5 9.1 %all-gather = bf16[32,1,8,1024]{3,2,1,0:T(8,128)(2,1)S(1)} all-gather(bf16[16,1,8,1024]{3,2,1,0:T(8,128)(2,1)S(1)} %dynamic-slice_convert_fusion), channel_id=2, replica_groups=mesh['zl'=4,'y'=4,'c'=2,'zh'=4,'x'=4] {'c'}, dimensions={0}, use_global_device_ids=true | all-gather | bytes 786432 | tf_op jit(solution)/shard_map/all_gather | solution.py:115
  97.6 0.1 fusion
  97.7 16.6 %all_to_all.32 = bf16[16,8,1024]{2,1,0:T(8,128)(2,1)S(1)} all-to-all(bf16[16,8,1024]{2,1,0:T(8,128)(2,1)S(1)} %fusion), channel_id=1, replica_groups=mesh['zl'=4,'y'=4,'c'=2,'zh'=4,'x'=4] {'zl','y'}, dimensions={0} | all-to-all | bytes 524288 | tf_op jit(solution)/shard_map/all_to_all | solution.py:27
  114.4 0.6 divide_convert_fusion
  115.0 13.1 %all_to_all.33 = bf16[16,8,1024]{2,1,0:T(8,128)(2,1)S(1)} all-to-all(bf16[16,8,1024]{2,1,0:T(8,128)(2,1)S(1)} %broadcast_in_dim.14), channel_id=1, replica_groups=mesh['zl'=4,'y'=4,'c'=2,'zh'=4,'x'=4] {'zl','y'}, dimensions={0} | all-to-all | bytes 524288 | tf_op jit(solution)/shard_map/all_to_all | solution.py:34
  128.2 4.3 %all_gather.11.update_ref = bf16[2,128,1024]{2,1,0:T(8,128)(2,1)S(1)} all-gather(bf16[1,128,1024]{2,1,0:T(8,128)(2,1)S(1)} %bitcast.25), channel_id=1, replica_groups=mesh['zl'=4,'y'=4,'c'=2,'zh'=4,'x'=4] {'c'}, dimensions={0}, use_global_device_ids=true | all-gather | bytes 786432 | tf_op jit(solution)/shard_map/all_gather | solution.py:124
  132.5 3.4 %copy-done.1 = bf16[4096,1024]{1,0:T(8,128)(2,1)S(1)} copy-done((bf16[4096,1024]{1,0:T(8,128)(2,1)S(1)}, bf16[4096,1024]{1,0:T(8,128)(2,1)}, u32[]{:S(2)}) %copy-start.1) | copy-done | bytes 8388632
  135.9 3.1 %decode.1 = bf16[256,4096]{1,0:T(8,128)(2,1)} custom-call(bf16[2,128,1024]{2,1,0:T(8,128)(2,1)S(1)} %all_gather.11.update_ref, bf16[2,4,4,4,32,1024]{5,4,3,2,1,0:T(8,128)(2,1)S(1)} %bitcast.20, bf16[256,4096]{1,0:T(8,128)(2,1)S(1)} %copy-done.2), custom_call_target="tpu_custom_call" | custom-call | tf_op jit(solution)/shard_map/decode/pallas_call | solution.py:75
  (17 shorter events, 0.2 us)
Async XLA Ops:
  7.2 1.0 copy-start
  10.2 11.8 %all-to-all-start = ((bf16[4,64,1024]{2,1,0:T(8,128)(2,1)}), bf16[4,64,1024]{2,1,0:T(8,128)(2,1)S(1)}, u32[]{:S(2)}, u32[]{:S(2)}) async-start(bf16[4,64,1024]{2,1,0:T(8,128)(2,1)} %bitcast), calls=%async_computation | async-start | bytes 1048576 | tf_op jit(solution)/shard_map/all_to_all | solution.py:27
  15.1 117.4 %all-gather.3.cloned.1.call-start = ((), (), s32[]{:S(2)}) async-start(), calls=%async_computation.6 | async-start | bytes 8650752 | tf_op jit(solution)/shard_map/all_gather | solution.py:101
  22.1 66.0 %copy-start.3 = (bf16[256,256]{1,0:T(8,128)(2,1)S(1)}, bf16[256,256]{1,0:T(8,128)(2,1)}, u32[]{:S(2)}) copy-start(bf16[256,256]{1,0:T(8,128)(2,1)} %param.7) | copy-start | bytes 393220
  75.7 12.4 %all-to-all-start.3 = ((bf16[4,64,1024]{2,1,0:T(8,128)(2,1)}), bf16[4,64,1024]{2,1,0:T(8,128)(2,1)S(1)}, u32[]{:S(2)}, u32[]{:S(2)}) async-start(bf16[4,64,1024]{2,1,0:T(8,128)(2,1)} %broadcast_in_dim.13), calls=%async_computation.3 | async-start | bytes 1048576 | tf_op jit(solution)/shard_map/all_to_all | solution.py:34
  88.1 26.2 %copy-start.4 = (f32[8,1024]{1,0:T(8,128)S(1)}, f32[8,1024]{1,0:T(8,128)}, u32[]{:S(2)}) copy-start(f32[8,1024]{1,0:T(8,128)} %param.10) | copy-start | bytes 98308
  88.1 26.3 %copy-start.5 = (f32[8,1024]{1,0:T(8,128)S(1)}, f32[8,1024]{1,0:T(8,128)}, u32[]{:S(2)}) copy-start(f32[8,1024]{1,0:T(8,128)} %param.11) | copy-start | bytes 98308
  88.5 44.0 %copy-start.2 = (bf16[256,4096]{1,0:T(8,128)(2,1)S(1)}, bf16[256,4096]{1,0:T(8,128)(2,1)}, u32[]{:S(2)}) copy-start(bf16[256,4096]{1,0:T(8,128)(2,1)} %weight_ref.1) | copy-start | bytes 6291460
  132.5 3.4 %copy-start.1 = (bf16[4096,1024]{1,0:T(8,128)(2,1)S(1)}, bf16[4096,1024]{1,0:T(8,128)(2,1)}, u32[]{:S(2)}) copy-start(bf16[4096,1024]{1,0:T(8,128)(2,1)} %all-gather.3.cloned.1.call-done) | copy-start | bytes 25165828
Sparse Core Ops, SparseCore 0:
  56.4 75.3 all-gather.2

commit v4 on v3

--- a/solution.py
+++ b/solution.py
@@ -28,6 +28,20 @@
     return jnp.sum(parts.astype(jnp.float32), axis=0)
 
 
+def permute_sum(value, axis):
+    size = lax.axis_size(axis)
+    me = lax.axis_index(axis)
+    rows = value.shape[0] // size
+    total = lax.dynamic_slice_in_dim(value, me * rows, rows, 0)
+    for step in range(1, size):
+        block = lax.dynamic_slice_in_dim(value, lax.rem(me + step, size) * rows, rows, 0)
+        got = lax.ppermute(
+            block.astype(jnp.bfloat16), axis, [(i, (i + step) % size) for i in range(size)]
+        )
+        total += got.astype(jnp.float32)
+    return total
+
+
 def gather(value, axis):
     size = lax.axis_size(axis)
     copies = jnp.broadcast_to(value[None], (size,) + value.shape)
@@ -39,8 +53,9 @@
 STEP = 2
 
 
-def decode_kernel(update_ref, basis_ref, weight_ref, out_ref, new, sems):
-    two, ys, xs, zhs, piece, rank = basis_ref.shape
+def decode_kernel(update_ref, left_ref, right_ref, weight_ref, out_ref, new, sems):
+    two, ys, xs, zhs, piece, half = left_ref.shape
+    rank = update_ref.shape[-1]
     shard = two * ys * piece
     cols = STEP * shard
 
@@ -51,16 +66,18 @@
     updates = update_ref[...].reshape(-1, rank)
     steps = xs * zhs // STEP
     for i in range(steps):
-        shards = [
-            basis_ref[:, :, f % xs, f // xs].reshape(shard, rank)
-            for f in range(i * STEP, (i + 1) * STEP)
-        ]
-        decoded = lax.dot_general(
-            updates,
-            jnp.concatenate(shards, axis=0),
-            (((1,), (1,)), ((), ())),
-            preferred_element_type=jnp.float32,
-        )
+        decoded = 0.0
+        for k, basis_ref in enumerate((left_ref, right_ref)):
+            shards = [
+                basis_ref[:, :, f % xs, f // xs].reshape(shard, half)
+                for f in range(i * STEP, (i + 1) * STEP)
+            ]
+            decoded += lax.dot_general(
+                updates[:, k * half : (k + 1) * half],
+                jnp.concatenate(shards, axis=0),
+                (((1,), (1,)), ((), ())),
+                preferred_element_type=jnp.float32,
+            )
         decoded = decoded.reshape(2, -1, 8, cols)
         decoded = jnp.stack([decoded[0], decoded[1]], axis=1).reshape(-1, cols)
         old = weight_ref[:, i * cols : (i + 1) * cols].astype(jnp.float32)
@@ -71,10 +88,11 @@
 
 
 def decode(updates, basis_pieces, weight):
-    steps = basis_pieces.shape[2] * basis_pieces.shape[3] // STEP
+    left, right = basis_pieces
+    steps = left.shape[2] * left.shape[3] // STEP
     return pl.pallas_call(
         decode_kernel,
-        in_specs=[pl.BlockSpec(memory_space=pltpu.VMEM)] * 3,
+        in_specs=[pl.BlockSpec(memory_space=pltpu.VMEM)] * 4,
         out_specs=pl.BlockSpec(memory_space=pl.ANY),
         out_shape=jax.ShapeDtypeStruct(weight.shape, weight.dtype),
         scratch_shapes=[
@@ -83,26 +101,28 @@
         ],
         compiler_params=pltpu.CompilerParams(vmem_limit_bytes=24 * 1024 * 1024),
         name="decode",
-    )(updates, basis_pieces, weight)
+    )(updates, left, right, weight)
 
 
 def local(activations, output_grads, basis, weight, first_moment, second_moment):
     core = lax.axis_index("c")
     piece = basis.shape[0] // 8
     mine = lax.dynamic_slice_in_dim(basis, (core * 4 + lax.axis_index("y")) * piece, piece, 0)
+    mine = gather(mine, "zh")
 
     partial_product = jnp.dot(activations, basis, preferred_element_type=jnp.float32)
-    over_x = exchange_sum(partial_product, "x").astype(jnp.bfloat16)
-    rank = over_x.shape[1]
-    parts = over_x.reshape(4, -1, rank)
-    rows = parts.shape[1]
-    copies = jnp.broadcast_to(mine[None], (4,) + mine.shape)
-    both = lax.all_to_all(jnp.concatenate([parts, copies], axis=1), "zh", 0, 0, tiled=True)
-    basis_pieces = lax.all_gather(
-        both[:, rows:].reshape(-1, rank), ("c", "y", "x"), axis=0, tiled=True
-    ).reshape(2, 4, 4, 4, piece, rank)
-    block = jnp.sum(both[:, :rows].astype(jnp.float32), axis=0).astype(jnp.bfloat16)
+    over_x = permute_sum(partial_product, "x").astype(jnp.bfloat16)
+    over_x, mine = lax.optimization_barrier((over_x, mine))
+    half = mine.shape[1] // 2
+    basis_pieces = [
+        lax.all_gather(mine[:, k * half : (k + 1) * half], ("c", "y", "x"), axis=0, tiled=True)
+        .reshape(2, 4, 4, 4, piece, half)
+        for k in range(2)
+    ]
+
+    block = exchange_sum(over_x, "zh").astype(jnp.bfloat16)
     projected = gather(gather(block, "zh"), "x")
+    rank = projected.shape[1]
     local_term = (
         lax.dot_general(
             output_grads, projected, (((0,), (0,)), ((), ())), preferred_element_type=jnp.float32
@@ -121,6 +141,7 @@
     update = (new_first / first_fix / (jnp.sqrt(new_second / second_fix) + tiny_eps)).astype(
         jnp.bfloat16
     )
+    update, basis_pieces = lax.optimization_barrier((update, basis_pieces))
     updates = lax.all_gather(gather(update, ("zl", "y")), "c", axis=0)
     return (decode(updates, basis_pieces, weight), new_first, new_second)
 

time: 146 us -> 205 us (1.40)
  waiting for transfers between devices: 15.9 us -> 59 us
  starting transfers between devices: 8.32 us -> 29.1 us
  blocking collectives: 95 us -> 88.3 us
    all_gather x1 -> x2, waiting for transfers between devices: 0.01 us -> 47.3 us  [local(): lax.all_gather(mine[:, k * half:(k + 1) * half], ('c', 'y', 'x'), axis=0,...]
    all_to_all x1 -> x0, blocking collectives: 33.4 us -> none  [local(): lax.all_to_all(jnp.concatenate([parts, copies], axis=1), 'zh', 0, 0, tile...]
    all_to_all x1 -> x2, blocking collectives: 16.6 us -> 40.6 us  [exchange_sum(): parts = lax.all_to_all(parts, axis, 0, 0, tiled=True)]
    all_to_all x1 -> x2, starting transfers between devices: 3.47 us -> 19.1 us  [gather(): lax.all_to_all(copies, axis, 0, 0, tiled=True)]
    ppermute x0 -> x3, starting transfers between devices: none -> 9.93 us  [permute_sum(): lax.ppermute(block.astype(jnp.bfloat16), axis, [(i, (i + step) % size) fo...]
    all_to_all x1 -> x0, waiting for transfers between devices: 6.92 us -> none  [exchange_sum(): parts = lax.all_to_all(parts, axis, 0, 0, tiled=True)]
    all_to_all x1 -> x0, starting transfers between devices: 4.84 us -> none  [exchange_sum(): parts = lax.all_to_all(parts, axis, 0, 0, tiled=True)]
    ppermute x0 -> x3, waiting for transfers between devices: none -> 4.04 us  [permute_sum(): lax.ppermute(block.astype(jnp.bfloat16), axis, [(i, (i + step) % size) fo...]
  transfers between devices with their start and end apart: 3 -> 7, of which waited for: 2 -> 3; matrix products, arithmetic and copies ran while one was open for 1% -> 2% of each run, Pallas kernels for 0% -> 0%
where the time goes in v4:
time: 205 us; the launch traced here: 204 us
  blocking collectives  88.3 us (43%)
  waiting for transfers between devices  59 us (29%)
  starting transfers between devices  29.1 us (14%)
  between operations  14.2 us (7%)
  local copies, waits for them, and re-layouts  7.85 us (4%)
  Pallas kernels  3.15 us (2%)
    all_gather x2, waiting for transfers between devices, local(): lax.all_gather(mine[:, k * half:(k + 1) * half], ('c', 'y', 'x'), axis=0,...  47.3 us
    all_to_all x2, blocking collectives, exchange_sum(): parts = lax.all_to_all(parts, axis, 0, 0, tiled=True)  40.6 us
    all_to_all x2, blocking collectives, gather(): lax.all_to_all(copies, axis, 0, 0, tiled=True)  31.8 us
    all_to_all x2, starting transfers between devices, gather(): lax.all_to_all(copies, axis, 0, 0, tiled=True)  19.1 us
    all_gather x1, blocking collectives, local(): sent = lax.all_gather(send, 'c', axis=0)  12.4 us
    ppermute x3, starting transfers between devices, permute_sum(): lax.ppermute(block.astype(jnp.bfloat16), axis, [(i, (i + step) % size) fo...  9.93 us
    all_to_all x2, waiting for transfers between devices, gather(): lax.all_to_all(copies, axis, 0, 0, tiled=True)  6.91 us
    unnamed x14, local copies, waits for them, and re-layouts  5.42 us
  transfers between devices with their start and end apart: 7, of which 3 were waited for; matrix products, arithmetic and copies ran while one was open for 2% of the time, Pallas kernels for 0%

profile of v4, /device:TPU:1, one launch (start us, length us, event | category | flops | bytes accessed | tf_op | source)
XLA Modules:
  0.0 203.9 jit_solution(2407854308722333671)
XLA Ops:
  7.2 1.0 copy-done
  8.2 0.7 broadcast_in_dim.10
  8.9 15.6 %all-to-all-start = ((bf16[4,32,1024]{2,1,0:T(8,128)(2,1)}), bf16[4,32,1024]{2,1,0:T(8,128)(2,1)S(1)}, u32[]{:S(2)}, u32[]{:S(2)}) async-start(bf16[4,32,1024]{2,1,0:T(8,128)(2,1)} %broadcast_in_dim.10), calls=%async_computation | async-start | bytes 524288 | tf_op jit(solution)/shard_map/all_to_all | solution.py:48
  24.6 1.2 fusion.4
  25.9 3.1 %collective-permute-start = (bf16[64,1024]{1,0:T(8,128)(2,1)S(1)}, bf16[64,1024]{1,0:T(8,128)(2,1)S(1)}, u32[]{:S(2)}, u32[]{:S(2)}) collective-permute-start(bf16[64,1024]{1,0:T(8,128)(2,1)S(1)} %get-tuple-element.16), channel_id=1, source_target_pairs={{0,1},{1,2},{2,3},{3,0},{4,5},{5,6},{6,7},{7,4},{8,9},{9,10},{10,1... | collective-permute-start | bytes 393224 | tf_op jit(solution)/shard_map/ppermute | solution.py:38
  29.0 3.4 %collective-permute-start.2 = (bf16[64,1024]{1,0:T(8,128)(2,1)S(1)}, bf16[64,1024]{1,0:T(8,128)(2,1)S(1)}, u32[]{:S(2)}, u32[]{:S(2)}) collective-permute-start(bf16[64,1024]{1,0:T(8,128)(2,1)S(1)} %get-tuple-element.17), channel_id=1, source_target_pairs={{0,3},{1,0},{2,1},{3,2},{4,7},{5,4},{6,5},{7,6},{8,11},{9,8},{10,9... | collective-permute-start | bytes 393224 | tf_op jit(solution)/shard_map/ppermute | solution.py:38
  32.4 3.4 %collective-permute-start.1 = (bf16[64,1024]{1,0:T(8,128)(2,1)S(1)}, bf16[64,1024]{1,0:T(8,128)(2,1)S(1)}, u32[]{:S(2)}, u32[]{:S(2)}) collective-permute-start(bf16[64,1024]{1,0:T(8,128)(2,1)S(1)} %get-tuple-element.18), channel_id=1, source_target_pairs={{0,2},{1,3},{2,0},{3,1},{4,6},{5,7},{6,4},{7,5},{8,10},{9,11},{10,... | collective-permute-start | bytes 393224 | tf_op jit(solution)/shard_map/ppermute | solution.py:38
  35.8 4.0 %collective-permute-done.1 = bf16[64,1024]{1,0:T(8,128)(2,1)S(1)} collective-permute-done((bf16[64,1024]{1,0:T(8,128)(2,1)S(1)}, bf16[64,1024]{1,0:T(8,128)(2,1)S(1)}, u32[]{:S(2)}, u32[]{:S(2)}) %collective-permute-start.1) | collective-permute-done | bytes 131104 | tf_op jit(solution)/shard_map/ppermute | solution.py:38
  40.0 0.7 fusion.3
  40.8 0.7 all-gather.4.cloned.1.call-update
  41.5 23.2 %all_to_all.30 = bf16[4,16,1024]{2,1,0:T(8,128)(2,1)S(1)} all-to-all(bf16[4,16,1024]{2,1,0:T(8,128)(2,1)S(1)} %bitcast.29), channel_id=1, replica_groups=mesh['zl'=4,'y'=4,'c'=2,'zh'=4,'x'=4] {'zh'}, dimensions={0} | all-to-all | bytes 262144 | tf_op jit(solution)/shard_map/all_to_all | solution.py:27
  64.7 15.6 %all_to_all.31 = bf16[4,16,1024]{2,1,0:T(8,128)(2,1)S(1)} all-to-all(bf16[4,16,1024]{2,1,0:T(8,128)(2,1)S(1)} %broadcast_in_dim.11), channel_id=1, replica_groups=mesh['zl'=4,'y'=4,'c'=2,'zh'=4,'x'=4] {'zh'}, dimensions={0} | all-to-all | bytes 262144 | tf_op jit(solution)/shard_map/all_to_all | solution.py:48
  80.2 0.9 broadcast_in_dim.13
  81.1 3.5 %all-to-all-start.3 = ((bf16[4,64,1024]{2,1,0:T(8,128)(2,1)}), bf16[4,64,1024]{2,1,0:T(8,128)(2,1)S(1)}, u32[]{:S(2)}, u32[]{:S(2)}) async-start(bf16[4,64,1024]{2,1,0:T(8,128)(2,1)} %broadcast_in_dim.13), calls=%async_computation.3 | async-start | bytes 1048576 | tf_op jit(solution)/shard_map/all_to_all | solution.py:48
  84.6 6.9 %all-to-all-done.3 = bf16[4,64,1024]{2,1,0:T(8,128)(2,1)S(1)} async-done(((bf16[4,64,1024]{2,1,0:T(8,128)(2,1)}), bf16[4,64,1024]{2,1,0:T(8,128)(2,1)S(1)}, u32[]{:S(2)}, u32[]{:S(2)}) %all-to-all-start.3) | async-done | bytes 524320 | tf_op jit(solution)/shard_map/all_to_all | solution.py:48
  91.9 12.4 %all-gather = bf16[32,1,8,1024]{3,2,1,0:T(8,128)(2,1)S(1)} all-gather(bf16[16,1,8,1024]{3,2,1,0:T(8,128)(2,1)S(1)} %dynamic-slice_convert_fusion), channel_id=2, replica_groups=mesh['zl'=4,'y'=4,'c'=2,'zh'=4,'x'=4] {'c'}, dimensions={0}, use_global_device_ids=true | all-gather | bytes 786432 | tf_op jit(solution)/shard_map/all_gather | solution.py:135
  104.4 17.5 %all_to_all.32 = bf16[16,8,1024]{2,1,0:T(8,128)(2,1)S(1)} all-to-all(bf16[16,8,1024]{2,1,0:T(8,128)(2,1)S(1)} %fusion), channel_id=1, replica_groups=mesh['zl'=4,'y'=4,'c'=2,'zh'=4,'x'=4] {'zl','y'}, dimensions={0} | all-to-all | bytes 524288 | tf_op jit(solution)/shard_map/all_to_all | solution.py:27
  121.9 0.6 divide_convert_fusion
  122.5 47.3 %all-gather.4.cloned.1.call-done = bf16[4096,512]{1,0:T(8,128)(2,1)} async-done(((bf16[128,512]{1,0:T(8,128)(2,1)}), bf16[4096,512]{1,0:T(8,128)(2,1)}) %all-gather.4.cloned.1.call-update) | async-done | bytes 4194320 | tf_op jit(solution)/shard_map/all_gather | solution.py:118
  169.9 16.3 %all_to_all.33 = bf16[16,8,1024]{2,1,0:T(8,128)(2,1)S(1)} all-to-all(bf16[16,8,1024]{2,1,0:T(8,128)(2,1)S(1)} %broadcast_in_dim.14), channel_id=1, replica_groups=mesh['zl'=4,'y'=4,'c'=2,'zh'=4,'x'=4] {'zl','y'}, dimensions={0} | all-to-all | bytes 524288 | tf_op jit(solution)/shard_map/all_to_all | solution.py:48
  186.2 3.4 %all_gather.16.update_ref = bf16[2,128,1024]{2,1,0:T(8,128)(2,1)S(1)} all-gather(bf16[1,128,1024]{2,1,0:T(8,128)(2,1)S(1)} %bitcast.26), channel_id=1, replica_groups=mesh['zl'=4,'y'=4,'c'=2,'zh'=4,'x'=4] {'c'}, dimensions={0}, use_global_device_ids=true | all-gather | bytes 786432 | tf_op jit(solution)/shard_map/all_gather | solution.py:145
  189.5 2.2 %copy-done.1 = bf16[4096,512]{1,0:T(8,128)(2,1)S(1)} copy-done((bf16[4096,512]{1,0:T(8,128)(2,1)S(1)}, bf16[4096,512]{1,0:T(8,128)(2,1)}, u32[]{:S(2)}) %copy-start.1) | copy-done | bytes 4194328
  191.7 2.2 %copy-done.2 = bf16[4096,512]{1,0:T(8,128)(2,1)S(1)} copy-done((bf16[4096,512]{1,0:T(8,128)(2,1)S(1)}, bf16[4096,512]{1,0:T(8,128)(2,1)}, u32[]{:S(2)}) %copy-start.2) | copy-done | bytes 4194328
  193.9 3.1 %decode.1 = bf16[256,4096]{1,0:T(8,128)(2,1)} custom-call(bf16[2,128,1024]{2,1,0:T(8,128)(2,1)S(1)} %all_gather.16.update_ref, bf16[2,4,4,4,32,512]{5,4,3,2,1,0:T(8,128)(2,1)S(1)} %bitcast.21, bf16[2,4,4,4,32,512]{5,4,3,2,1,0:T(8,128)(2,1)S(1)} %bitcast.20, bf16[256,4096]{1,0:T(8,128)(2,1)S(1)} %copy-done.3), custom_call_target="tpu_custom_call" | custom-call | tf_op jit(solution)/shard_map/decode/pallas_call | solution.py:93
  (28 shorter events, 0.8 us)
Async XLA Ops:
  7.2 1.0 copy-start
  7.2 84.3 %copy-start.4 = (bf16[256,256]{1,0:T(8,128)(2,1)S(1)}, bf16[256,256]{1,0:T(8,128)(2,1)}, u32[]{:S(2)}) copy-start(bf16[256,256]{1,0:T(8,128)(2,1)} %param.7) | copy-start | bytes 393220
  8.9 31.0 %all-to-all-start = ((bf16[4,32,1024]{2,1,0:T(8,128)(2,1)}), bf16[4,32,1024]{2,1,0:T(8,128)(2,1)S(1)}, u32[]{:S(2)}, u32[]{:S(2)}) async-start(bf16[4,32,1024]{2,1,0:T(8,128)(2,1)} %broadcast_in_dim.10), calls=%async_computation | async-start | bytes 524288 | tf_op jit(solution)/shard_map/all_to_all | solution.py:48
  24.6 98.0 %all-gather.6.cloned.1.call-start = ((), (), s32[]{:S(2)}) async-start(), calls=%async_computation.7 | async-start | bytes 4325376 | tf_op jit(solution)/shard_map/all_gather | solution.py:118
  25.9 10.0 %collective-permute-start = (bf16[64,1024]{1,0:T(8,128)(2,1)S(1)}, bf16[64,1024]{1,0:T(8,128)(2,1)S(1)}, u32[]{:S(2)}, u32[]{:S(2)}) collective-permute-start(bf16[64,1024]{1,0:T(8,128)(2,1)S(1)} %get-tuple-element.16), channel_id=1, source_target_pairs={{0,1},{1,2},{2,3},{3,0},{4,5},{5,6},{6,7},{7,4},{8,9},{9,10},{10,1... | collective-permute-start | bytes 393224 | tf_op jit(solution)/shard_map/ppermute | solution.py:38
  29.0 6.8 %collective-permute-start.2 = (bf16[64,1024]{1,0:T(8,128)(2,1)S(1)}, bf16[64,1024]{1,0:T(8,128)(2,1)S(1)}, u32[]{:S(2)}, u32[]{:S(2)}) collective-permute-start(bf16[64,1024]{1,0:T(8,128)(2,1)S(1)} %get-tuple-element.17), channel_id=1, source_target_pairs={{0,3},{1,0},{2,1},{3,2},{4,7},{5,4},{6,5},{7,6},{8,11},{9,8},{10,9... | collective-permute-start | bytes 393224 | tf_op jit(solution)/shard_map/ppermute | solution.py:38
  32.4 7.5 %collective-permute-start.1 = (bf16[64,1024]{1,0:T(8,128)(2,1)S(1)}, bf16[64,1024]{1,0:T(8,128)(2,1)S(1)}, u32[]{:S(2)}, u32[]{:S(2)}) collective-permute-start(bf16[64,1024]{1,0:T(8,128)(2,1)S(1)} %get-tuple-element.18), channel_id=1, source_target_pairs={{0,2},{1,3},{2,0},{3,1},{4,6},{5,7},{6,4},{7,5},{8,10},{9,11},{10,... | collective-permute-start | bytes 393224 | tf_op jit(solution)/shard_map/ppermute | solution.py:38
  40.0 81.9 %copy-start.5 = (f32[8,1024]{1,0:T(8,128)S(1)}, f32[8,1024]{1,0:T(8,128)}, u32[]{:S(2)}) copy-start(f32[8,1024]{1,0:T(8,128)} %param.10) | copy-start | bytes 98308
  40.0 81.9 %copy-start.6 = (f32[8,1024]{1,0:T(8,128)S(1)}, f32[8,1024]{1,0:T(8,128)}, u32[]{:S(2)}) copy-start(f32[8,1024]{1,0:T(8,128)} %param.11) | copy-start | bytes 98308
  40.7 129.1 %all-gather.4.cloned.1.call-start = ((), (), s32[]{:S(2)}) async-start(), calls=%async_computation.6 | async-start | bytes 4325376 | tf_op jit(solution)/shard_map/all_gather | solution.py:118
  80.2 109.3 %copy-start.3 = (bf16[256,4096]{1,0:T(8,128)(2,1)S(1)}, bf16[256,4096]{1,0:T(8,128)(2,1)}, u32[]{:S(2)}) copy-start(bf16[256,4096]{1,0:T(8,128)(2,1)} %weight_ref.1) | copy-start | bytes 6291460
  81.1 10.4 %all-to-all-start.3 = ((bf16[4,64,1024]{2,1,0:T(8,128)(2,1)}), bf16[4,64,1024]{2,1,0:T(8,128)(2,1)S(1)}, u32[]{:S(2)}, u32[]{:S(2)}) async-start(bf16[4,64,1024]{2,1,0:T(8,128)(2,1)} %broadcast_in_dim.13), calls=%async_computation.3 | async-start | bytes 1048576 | tf_op jit(solution)/shard_map/all_to_all | solution.py:48
  189.5 2.2 %copy-start.1 = (bf16[4096,512]{1,0:T(8,128)(2,1)S(1)}, bf16[4096,512]{1,0:T(8,128)(2,1)}, u32[]{:S(2)}) copy-start(bf16[4096,512]{1,0:T(8,128)(2,1)} %all-gather.6.cloned.1.call-done) | copy-start | bytes 12582916
  191.7 2.2 %copy-start.2 = (bf16[4096,512]{1,0:T(8,128)(2,1)S(1)}, bf16[4096,512]{1,0:T(8,128)(2,1)}, u32[]{:S(2)}) copy-start(bf16[4096,512]{1,0:T(8,128)(2,1)} %all-gather.4.cloned.1.call-done) | copy-start | bytes 12582916
Sparse Core Ops, SparseCore 0:
  40.8 65.1 all-gather.5
  109.2 60.6 all-gather.3

commit v5 on v3

--- a/solution.py
+++ b/solution.py
@@ -88,21 +88,21 @@
 
 def local(activations, output_grads, basis, weight, first_moment, second_moment):
     core = lax.axis_index("c")
-    piece = basis.shape[0] // 8
-    mine = lax.dynamic_slice_in_dim(basis, (core * 4 + lax.axis_index("y")) * piece, piece, 0)
-
     partial_product = jnp.dot(activations, basis, preferred_element_type=jnp.float32)
     over_x = exchange_sum(partial_product, "x").astype(jnp.bfloat16)
     rank = over_x.shape[1]
-    parts = over_x.reshape(4, -1, rank)
-    rows = parts.shape[1]
-    copies = jnp.broadcast_to(mine[None], (4,) + mine.shape)
-    both = lax.all_to_all(jnp.concatenate([parts, copies], axis=1), "zh", 0, 0, tiled=True)
-    basis_pieces = lax.all_gather(
-        both[:, rows:].reshape(-1, rank), ("c", "y", "x"), axis=0, tiled=True
-    ).reshape(2, 4, 4, 4, piece, rank)
-    block = jnp.sum(both[:, :rows].astype(jnp.float32), axis=0).astype(jnp.bfloat16)
-    projected = gather(gather(block, "zh"), "x")
+
+    piece = basis.shape[0] // 8
+    mine = lax.dynamic_slice_in_dim(basis, (core * 4 + lax.axis_index("y")) * piece, piece, 0)
+    over_x, mine = lax.optimization_barrier((over_x, mine))
+    mine = lax.all_gather(mine, "zh", axis=0, tiled=True)
+    over_x, mine = lax.optimization_barrier((over_x, mine))
+    basis_pieces = lax.all_gather(mine, ("c", "y", "x"), axis=0, tiled=True)
+    basis_pieces = basis_pieces.reshape(2, 4, 4, 4, piece, rank)
+
+    over_all = lax.all_gather(over_x, "zh", axis=0)
+    block = jnp.sum(over_all.astype(jnp.float32), axis=0).astype(jnp.bfloat16)
+    projected = gather(block, "x")
     local_term = (
         lax.dot_general(
             output_grads, projected, (((0,), (0,)), ((), ())), preferred_element_type=jnp.float32

time: 146 us -> 140 us (0.959)
  blocking collectives: 95 us -> 91.3 us
  waiting for transfers between devices: 15.9 us -> 13.8 us
    all_gather x0 -> x2, blocking collectives: none -> 47.3 us  [the longest x1 27.2 us: local(): mine = lax.all_gather(mine, 'zh', axis=0, tiled=True)]
    all_to_all x1 -> x0, blocking collectives: 33.4 us -> none  [local(): lax.all_to_all(jnp.concatenate([parts, copies], axis=1), 'zh', 0, 0, tile...]
    all_to_all x2 -> x1, blocking collectives: 31.6 us -> 13.1 us  [gather(): lax.all_to_all(copies, axis, 0, 0, tiled=True)]
    all_to_all x1, waiting for transfers between devices: 8.92 us -> 6.9 us  [gather(): lax.all_to_all(copies, axis, 0, 0, tiled=True)]
where the time goes in v5:
time: 140 us; the launch traced here: 139 us
  blocking collectives  91.3 us (65%)
  between operations  14.1 us (10%)
  waiting for transfers between devices  13.8 us (10%)
  starting transfers between devices  8.32 us (6%)
  local copies, waits for them, and re-layouts  5.36 us (4%)
  Pallas kernels  3.14 us (2%)
  matrix products  2.34 us (2%)
    all_gather x1, blocking collectives, local(): mine = lax.all_gather(mine, 'zh', axis=0, tiled=True)  27.2 us
    all_gather x1, blocking collectives, local(): over_all = lax.all_gather(over_x, 'zh', axis=0)  20.1 us
    all_to_all x1, blocking collectives, exchange_sum(): parts = lax.all_to_all(parts, axis, 0, 0, tiled=True)  16.4 us
    all_to_all x1, blocking collectives, gather(): lax.all_to_all(copies, axis, 0, 0, tiled=True)  13.1 us
    all_gather x1, blocking collectives, local(): sent = lax.all_gather(send, 'c', axis=0)  10.1 us
    all_to_all x1, waiting for transfers between devices, exchange_sum(): parts = lax.all_to_all(parts, axis, 0, 0, tiled=True)  6.91 us
    all_to_all x1, waiting for transfers between devices, gather(): lax.all_to_all(copies, axis, 0, 0, tiled=True)  6.9 us
    all_to_all x1, starting transfers between devices, exchange_sum(): parts = lax.all_to_all(parts, axis, 0, 0, tiled=True)  4.84 us
  transfers between devices with their start and end apart: 3, of which 2 were waited for; matrix products, arithmetic and copies ran while one was open for 1% of the time, Pallas kernels for 0%

profile of v5, /device:TPU:1, one launch (start us, length us, event | category | flops | bytes accessed | tf_op | source)
XLA Modules:
  0.0 139.3 jit_solution(9277738898784117034)
XLA Ops:
  7.2 0.0 copy-start
  7.2 1.0 copy-done
  8.2 2.0 %convolution_convert_fusion = bf16[256,1024]{1,0:T(8,128)(2,1)} fusion(bf16[256,256]{1,0:T(8,128)(2,1)} %param.6, bf16[256,1024]{1,0:T(8,128)(2,1)S(1)} %copy-done), kind=kOutput, calls=%fused_computation.1 | convolution fusion | flops 134479872 | bytes 1179648 | tf_op jit(solution)/shard_map/dot_general | solution.py:91
  10.2 4.8 %all-to-all-start = ((bf16[4,64,1024]{2,1,0:T(8,128)(2,1)}), bf16[4,64,1024]{2,1,0:T(8,128)(2,1)S(1)}, u32[]{:S(2)}, u32[]{:S(2)}) async-start(bf16[4,64,1024]{2,1,0:T(8,128)(2,1)} %bitcast), calls=%async_computation | async-start | bytes 1048576 | tf_op jit(solution)/shard_map/all_to_all | solution.py:27
  15.1 0.0 copy-start.3
  15.1 6.9 %all-to-all-done = bf16[4,64,1024]{2,1,0:T(8,128)(2,1)S(1)} async-done(((bf16[4,64,1024]{2,1,0:T(8,128)(2,1)}), bf16[4,64,1024]{2,1,0:T(8,128)(2,1)S(1)}, u32[]{:S(2)}, u32[]{:S(2)}) %all-to-all-start) | async-done | bytes 524320 | tf_op jit(solution)/shard_map/all_to_all | solution.py:27
  22.0 0.1 reduce_sum.33
  22.1 27.2 %all_gather.19 = bf16[128,1024]{1,0:T(8,128)(2,1)} all-gather(bf16[32,1024]{1,0:T(8,128)(2,1)S(1)} %constant_dynamic-slice_fusion), channel_id=1, replica_groups=mesh['zl'=4,'y'=4,'c'=2,'zh'=4,'x'=4] {'zh'}, dimensions={0}, use_global_device_ids=true | all-gather | bytes 327680 | tf_op jit(solution)/shard_map/all_gather | solution.py:98
  49.3 0.0 all-gather.4.cloned.1.call-update
  49.3 20.1 %all-gather = bf16[256,1024]{1,0:T(8,128)(2,1)S(1)} all-gather(bf16[64,1024]{1,0:T(8,128)(2,1)S(1)} %reduce_sum.33), channel_id=2, replica_groups=mesh['zl'=4,'y'=4,'c'=2,'zh'=4,'x'=4] {'zh'}, dimensions={0}, use_global_device_ids=true | all-gather | bytes 655360 | tf_op jit(solution)/shard_map/all_gather | solution.py:103
  69.5 0.1 reduce_sum.34
  69.5 0.9 broadcast_in_dim.4
  70.4 3.5 %all-to-all-start.1 = ((bf16[4,64,1024]{2,1,0:T(8,128)(2,1)}), bf16[4,64,1024]{2,1,0:T(8,128)(2,1)S(1)}, u32[]{:S(2)}, u32[]{:S(2)}) async-start(bf16[4,64,1024]{2,1,0:T(8,128)(2,1)} %broadcast_in_dim.4), calls=%async_computation.1 | async-start | bytes 1048576 | tf_op jit(solution)/shard_map/all_to_all | solution.py:34
  73.9 6.9 %all-to-all-done.1 = bf16[4,64,1024]{2,1,0:T(8,128)(2,1)S(1)} async-done(((bf16[4,64,1024]{2,1,0:T(8,128)(2,1)}), bf16[4,64,1024]{2,1,0:T(8,128)(2,1)S(1)}, u32[]{:S(2)}, u32[]{:S(2)}) %all-to-all-start.1) | async-done | bytes 524320 | tf_op jit(solution)/shard_map/all_to_all | solution.py:34
  80.8 0.3 convolution_multiply_fusion
  81.2 0.0 copy-start.2
  81.2 10.1 %all-gather.1 = bf16[32,1,8,1024]{3,2,1,0:T(8,128)(2,1)S(1)} all-gather(bf16[16,1,8,1024]{3,2,1,0:T(8,128)(2,1)S(1)} %dynamic-slice_convert_fusion), channel_id=3, replica_groups=mesh['zl'=4,'y'=4,'c'=2,'zh'=4,'x'=4] {'c'}, dimensions={0}, use_global_device_ids=true | all-gather | bytes 786432 | tf_op jit(solution)/shard_map/all_gather | solution.py:115
  91.3 0.1 fusion
  91.4 16.4 %all_to_all.20 = bf16[16,8,1024]{2,1,0:T(8,128)(2,1)S(1)} all-to-all(bf16[16,8,1024]{2,1,0:T(8,128)(2,1)S(1)} %fusion), channel_id=1, replica_groups=mesh['zl'=4,'y'=4,'c'=2,'zh'=4,'x'=4] {'zl','y'}, dimensions={0} | all-to-all | bytes 524288 | tf_op jit(solution)/shard_map/all_to_all | solution.py:27
  107.8 0.6 divide_convert_fusion
  108.5 13.1 %all_to_all.21 = bf16[16,8,1024]{2,1,0:T(8,128)(2,1)S(1)} all-to-all(bf16[16,8,1024]{2,1,0:T(8,128)(2,1)S(1)} %broadcast_in_dim.5), channel_id=1, replica_groups=mesh['zl'=4,'y'=4,'c'=2,'zh'=4,'x'=4] {'zl','y'}, dimensions={0} | all-to-all | bytes 524288 | tf_op jit(solution)/shard_map/all_to_all | solution.py:34
  121.6 4.3 %all_gather.23.update_ref = bf16[2,128,1024]{2,1,0:T(8,128)(2,1)S(1)} all-gather(bf16[1,128,1024]{2,1,0:T(8,128)(2,1)S(1)} %bitcast.24), channel_id=1, replica_groups=mesh['zl'=4,'y'=4,'c'=2,'zh'=4,'x'=4] {'c'}, dimensions={0}, use_global_device_ids=true | all-gather | bytes 786432 | tf_op jit(solution)/shard_map/all_gather | solution.py:124
  125.9 3.4 %copy-done.1 = bf16[4096,1024]{1,0:T(8,128)(2,1)S(1)} copy-done((bf16[4096,1024]{1,0:T(8,128)(2,1)S(1)}, bf16[4096,1024]{1,0:T(8,128)(2,1)}, u32[]{:S(2)}) %copy-start.1) | copy-done | bytes 8388632
  129.3 3.1 %decode.1 = bf16[256,4096]{1,0:T(8,128)(2,1)} custom-call(bf16[2,128,1024]{2,1,0:T(8,128)(2,1)S(1)} %all_gather.23.update_ref, bf16[2,4,4,4,32,1024]{5,4,3,2,1,0:T(8,128)(2,1)S(1)} %bitcast.18, bf16[256,4096]{1,0:T(8,128)(2,1)S(1)} %copy-done.2), custom_call_target="tpu_custom_call" | custom-call | tf_op jit(solution)/shard_map/decode/pallas_call | solution.py:75
  (13 shorter events, 0.1 us)
Async XLA Ops:
  7.2 1.0 copy-start
  10.2 11.8 %all-to-all-start = ((bf16[4,64,1024]{2,1,0:T(8,128)(2,1)}), bf16[4,64,1024]{2,1,0:T(8,128)(2,1)S(1)}, u32[]{:S(2)}, u32[]{:S(2)}) async-start(bf16[4,64,1024]{2,1,0:T(8,128)(2,1)} %bitcast), calls=%async_computation | async-start | bytes 1048576 | tf_op jit(solution)/shard_map/all_to_all | solution.py:27
  15.1 110.9 %all-gather.4.cloned.1.call-start = ((), (), s32[]{:S(2)}) async-start(), calls=%async_computation.4 | async-start | bytes 8650752 | tf_op jit(solution)/shard_map/all_gather | solution.py:100
  15.1 65.7 %copy-start.3 = (bf16[256,256]{1,0:T(8,128)(2,1)S(1)}, bf16[256,256]{1,0:T(8,128)(2,1)}, u32[]{:S(2)}) copy-start(bf16[256,256]{1,0:T(8,128)(2,1)} %param.7) | copy-start | bytes 393220
  70.4 10.4 %all-to-all-start.1 = ((bf16[4,64,1024]{2,1,0:T(8,128)(2,1)}), bf16[4,64,1024]{2,1,0:T(8,128)(2,1)S(1)}, u32[]{:S(2)}, u32[]{:S(2)}) async-start(bf16[4,64,1024]{2,1,0:T(8,128)(2,1)} %broadcast_in_dim.4), calls=%async_computation.1 | async-start | bytes 1048576 | tf_op jit(solution)/shard_map/all_to_all | solution.py:34
  80.8 27.0 %copy-start.4 = (f32[8,1024]{1,0:T(8,128)S(1)}, f32[8,1024]{1,0:T(8,128)}, u32[]{:S(2)}) copy-start(f32[8,1024]{1,0:T(8,128)} %param.10) | copy-start | bytes 98308
  80.8 27.0 %copy-start.5 = (f32[8,1024]{1,0:T(8,128)S(1)}, f32[8,1024]{1,0:T(8,128)}, u32[]{:S(2)}) copy-start(f32[8,1024]{1,0:T(8,128)} %param.11) | copy-start | bytes 98308
  81.2 44.8 %copy-start.2 = (bf16[256,4096]{1,0:T(8,128)(2,1)S(1)}, bf16[256,4096]{1,0:T(8,128)(2,1)}, u32[]{:S(2)}) copy-start(bf16[256,4096]{1,0:T(8,128)(2,1)} %weight_ref.1) | copy-start | bytes 6291460
  125.9 3.4 %copy-start.1 = (bf16[4096,1024]{1,0:T(8,128)(2,1)S(1)}, bf16[4096,1024]{1,0:T(8,128)(2,1)}, u32[]{:S(2)}) copy-start(bf16[4096,1024]{1,0:T(8,128)(2,1)} %all-gather.4.cloned.1.call-done) | copy-start | bytes 25165828
Sparse Core Ops, SparseCore 0:
  49.5 69.2 all-gather.3

commit v6 on v5

--- a/solution.py
+++ b/solution.py
@@ -89,12 +89,11 @@
 def local(activations, output_grads, basis, weight, first_moment, second_moment):
     core = lax.axis_index("c")
     partial_product = jnp.dot(activations, basis, preferred_element_type=jnp.float32)
+    piece = basis.shape[0] // 8
+    mine = lax.dynamic_slice_in_dim(basis, (core * 4 + lax.axis_index("y")) * piece, piece, 0)
+    partial_product, mine = lax.optimization_barrier((partial_product.astype(jnp.bfloat16), mine))
     over_x = exchange_sum(partial_product, "x").astype(jnp.bfloat16)
     rank = over_x.shape[1]
-
-    piece = basis.shape[0] // 8
-    mine = lax.dynamic_slice_in_dim(basis, (core * 4 + lax.axis_index("y")) * piece, piece, 0)
-    over_x, mine = lax.optimization_barrier((over_x, mine))
     mine = lax.all_gather(mine, "zh", axis=0, tiled=True)
     over_x, mine = lax.optimization_barrier((over_x, mine))
     basis_pieces = lax.all_gather(mine, ("c", "y", "x"), axis=0, tiled=True)

time: 140 us -> 131 us (0.936)
  waiting for transfers between devices: 13.8 us -> 6.95 us
  blocking collectives: 91.3 us -> 88.5 us
    all_to_all x1, waiting for transfers between devices: 6.91 us -> 0.01 us  [exchange_sum(): parts = lax.all_to_all(parts, axis, 0, 0, tiled=True)]
    all_gather x1, blocking collectives: 20.1 us -> 22.5 us  [local(): over_all = lax.all_gather(over_x, 'zh', axis=0)]
    all_gather x1, blocking collectives: 10.1 us -> 7.95 us  [local(): sent = lax.all_gather(send, 'c', axis=0)]
    all_gather x1, blocking collectives: 27.2 us -> 25.1 us  [local(): mine = lax.all_gather(mine, 'zh', axis=0, tiled=True)]
  transfers between devices with their start and end apart: 3 -> 3, of which waited for: 2 -> 1; matrix products, arithmetic and copies ran while one was open for 1% -> 2% of each run, Pallas kernels for 0% -> 0%
where the time goes in v6:
time: 131 us
  blocking collectives  88.5 us (68%)
  between operations  14.1 us (11%)
  starting transfers between devices  9.29 us (7%)
  waiting for transfers between devices  6.95 us (5%)
  local copies, waits for them, and re-layouts  5.35 us (4%)
  Pallas kernels  3.14 us (2%)
  matrix products  2.34 us (2%)
    all_gather x1, blocking collectives, local(): mine = lax.all_gather(mine, 'zh', axis=0, tiled=True)  25.1 us
    all_gather x1, blocking collectives, local(): over_all = lax.all_gather(over_x, 'zh', axis=0)  22.5 us
    all_to_all x1, blocking collectives, exchange_sum(): parts = lax.all_to_all(parts, axis, 0, 0, tiled=True)  15.5 us
    all_to_all x1, blocking collectives, gather(): lax.all_to_all(copies, axis, 0, 0, tiled=True)  13.1 us
    all_gather x1, blocking collectives, local(): sent = lax.all_gather(send, 'c', axis=0)  7.95 us
    all_to_all x1, waiting for transfers between devices, gather(): lax.all_to_all(copies, axis, 0, 0, tiled=True)  6.93 us
    all_to_all x1, starting transfers between devices, exchange_sum(): parts = lax.all_to_all(parts, axis, 0, 0, tiled=True)  4.84 us
    all_to_all x1, starting transfers between devices, gather(): lax.all_to_all(copies, axis, 0, 0, tiled=True)  4.45 us
  transfers between devices with their start and end apart: 3, of which 1 were waited for; matrix products, arithmetic and copies ran while one was open for 2% of the time, Pallas kernels for 0%

profile of v6, /device:TPU:1, one launch (start us, length us, event | category | flops | bytes accessed | tf_op | source)
XLA Modules:
  0.0 130.6 jit_solution(12397232317833461031)
XLA Ops:
  7.2 0.0 copy-start
  7.2 1.0 copy-done
  8.2 2.0 %convolution_convert_fusion = bf16[256,1024]{1,0:T(8,128)(2,1)} fusion(bf16[256,256]{1,0:T(8,128)(2,1)} %param.6, bf16[256,1024]{1,0:T(8,128)(2,1)S(1)} %copy-done), kind=kOutput, calls=%fused_computation.1 | convolution fusion | flops 134479872 | bytes 1179648 | tf_op jit(solution)/shard_map/dot_general | solution.py:91
  10.2 4.8 %all-to-all-start = ((bf16[4,64,1024]{2,1,0:T(8,128)(2,1)}), bf16[4,64,1024]{2,1,0:T(8,128)(2,1)S(1)}, u32[]{:S(2)}, u32[]{:S(2)}) async-start(bf16[4,64,1024]{2,1,0:T(8,128)(2,1)} %bitcast), calls=%async_computation | async-start | bytes 1048576 | tf_op jit(solution)/shard_map/all_to_all | solution.py:27
  15.1 0.0 all-gather.4.cloned.1.call-start
  15.1 25.1 %all_gather.19 = bf16[128,1024]{1,0:T(8,128)(2,1)} all-gather(bf16[32,1024]{1,0:T(8,128)(2,1)S(1)} %constant_dynamic-slice_fusion), channel_id=1, replica_groups=mesh['zl'=4,'y'=4,'c'=2,'zh'=4,'x'=4] {'zh'}, dimensions={0}, use_global_device_ids=true | all-gather | bytes 327680 | tf_op jit(solution)/shard_map/all_gather | solution.py:97
  40.1 0.0 all-to-all-done
  40.1 0.1 reduce_sum.33
  40.2 0.0 all-gather.4.cloned.1.call-update
  40.2 22.5 %all-gather = bf16[256,1024]{1,0:T(8,128)(2,1)S(1)} all-gather(bf16[64,1024]{1,0:T(8,128)(2,1)S(1)} %reduce_sum.33), channel_id=2, replica_groups=mesh['zl'=4,'y'=4,'c'=2,'zh'=4,'x'=4] {'zh'}, dimensions={0}, use_global_device_ids=true | all-gather | bytes 655360 | tf_op jit(solution)/shard_map/all_gather | solution.py:102
  62.8 0.1 reduce_sum.34
  62.9 0.9 broadcast_in_dim.4
  63.7 4.5 %all-to-all-start.1 = ((bf16[4,64,1024]{2,1,0:T(8,128)(2,1)}), bf16[4,64,1024]{2,1,0:T(8,128)(2,1)S(1)}, u32[]{:S(2)}, u32[]{:S(2)}) async-start(bf16[4,64,1024]{2,1,0:T(8,128)(2,1)} %broadcast_in_dim.4), calls=%async_computation.1 | async-start | bytes 1048576 | tf_op jit(solution)/shard_map/all_to_all | solution.py:34
  68.2 6.9 %all-to-all-done.1 = bf16[4,64,1024]{2,1,0:T(8,128)(2,1)S(1)} async-done(((bf16[4,64,1024]{2,1,0:T(8,128)(2,1)}), bf16[4,64,1024]{2,1,0:T(8,128)(2,1)S(1)}, u32[]{:S(2)}, u32[]{:S(2)}) %all-to-all-start.1) | async-done | bytes 524320 | tf_op jit(solution)/shard_map/all_to_all | solution.py:34
  75.1 0.3 convolution_multiply_fusion
  75.5 0.0 copy-start.2
  75.5 7.9 %all-gather.1 = bf16[32,1,8,1024]{3,2,1,0:T(8,128)(2,1)S(1)} all-gather(bf16[16,1,8,1024]{3,2,1,0:T(8,128)(2,1)S(1)} %dynamic-slice_convert_fusion), channel_id=3, replica_groups=mesh['zl'=4,'y'=4,'c'=2,'zh'=4,'x'=4] {'c'}, dimensions={0}, use_global_device_ids=true | all-gather | bytes 786432 | tf_op jit(solution)/shard_map/all_gather | solution.py:114
  83.5 0.1 fusion
  83.5 15.5 %all_to_all.20 = bf16[16,8,1024]{2,1,0:T(8,128)(2,1)S(1)} all-to-all(bf16[16,8,1024]{2,1,0:T(8,128)(2,1)S(1)} %fusion), channel_id=1, replica_groups=mesh['zl'=4,'y'=4,'c'=2,'zh'=4,'x'=4] {'zl','y'}, dimensions={0} | all-to-all | bytes 524288 | tf_op jit(solution)/shard_map/all_to_all | solution.py:27
  99.1 0.6 divide_convert_fusion
  99.8 13.1 %all_to_all.21 = bf16[16,8,1024]{2,1,0:T(8,128)(2,1)S(1)} all-to-all(bf16[16,8,1024]{2,1,0:T(8,128)(2,1)S(1)} %broadcast_in_dim.5), channel_id=1, replica_groups=mesh['zl'=4,'y'=4,'c'=2,'zh'=4,'x'=4] {'zl','y'}, dimensions={0} | all-to-all | bytes 524288 | tf_op jit(solution)/shard_map/all_to_all | solution.py:34
  112.9 4.3 %all_gather.23.update_ref = bf16[2,128,1024]{2,1,0:T(8,128)(2,1)S(1)} all-gather(bf16[1,128,1024]{2,1,0:T(8,128)(2,1)S(1)} %bitcast.24), channel_id=1, replica_groups=mesh['zl'=4,'y'=4,'c'=2,'zh'=4,'x'=4] {'c'}, dimensions={0}, use_global_device_ids=true | all-gather | bytes 786432 | tf_op jit(solution)/shard_map/all_gather | solution.py:123
  117.3 3.4 %copy-done.1 = bf16[4096,1024]{1,0:T(8,128)(2,1)S(1)} copy-done((bf16[4096,1024]{1,0:T(8,128)(2,1)S(1)}, bf16[4096,1024]{1,0:T(8,128)(2,1)}, u32[]{:S(2)}) %copy-start.1) | copy-done | bytes 8388632
  120.6 3.1 %decode.1 = bf16[256,4096]{1,0:T(8,128)(2,1)} custom-call(bf16[2,128,1024]{2,1,0:T(8,128)(2,1)S(1)} %all_gather.23.update_ref, bf16[2,4,4,4,32,1024]{5,4,3,2,1,0:T(8,128)(2,1)S(1)} %bitcast.18, bf16[256,4096]{1,0:T(8,128)(2,1)S(1)} %copy-done.2), custom_call_target="tpu_custom_call" | custom-call | tf_op jit(solution)/shard_map/decode/pallas_call | solution.py:75
  (13 shorter events, 0.1 us)
Async XLA Ops:
  7.2 1.0 copy-start
  10.2 29.9 %all-to-all-start = ((bf16[4,64,1024]{2,1,0:T(8,128)(2,1)}), bf16[4,64,1024]{2,1,0:T(8,128)(2,1)S(1)}, u32[]{:S(2)}, u32[]{:S(2)}) async-start(bf16[4,64,1024]{2,1,0:T(8,128)(2,1)} %bitcast), calls=%async_computation | async-start | bytes 1048576 | tf_op jit(solution)/shard_map/all_to_all | solution.py:27
  15.1 60.1 %copy-start.3 = (bf16[256,256]{1,0:T(8,128)(2,1)S(1)}, bf16[256,256]{1,0:T(8,128)(2,1)}, u32[]{:S(2)}) copy-start(bf16[256,256]{1,0:T(8,128)(2,1)} %param.7) | copy-start | bytes 393220
  15.1 102.2 %all-gather.4.cloned.1.call-start = ((), (), s32[]{:S(2)}) async-start(), calls=%async_computation.4 | async-start | bytes 8650752 | tf_op jit(solution)/shard_map/all_gather | solution.py:99
  63.7 11.4 %all-to-all-start.1 = ((bf16[4,64,1024]{2,1,0:T(8,128)(2,1)}), bf16[4,64,1024]{2,1,0:T(8,128)(2,1)S(1)}, u32[]{:S(2)}, u32[]{:S(2)}) async-start(bf16[4,64,1024]{2,1,0:T(8,128)(2,1)} %broadcast_in_dim.4), calls=%async_computation.1 | async-start | bytes 1048576 | tf_op jit(solution)/shard_map/all_to_all | solution.py:34
  75.1 24.0 %copy-start.4 = (f32[8,1024]{1,0:T(8,128)S(1)}, f32[8,1024]{1,0:T(8,128)}, u32[]{:S(2)}) copy-start(f32[8,1024]{1,0:T(8,128)} %param.10) | copy-start | bytes 98308
  75.1 24.0 %copy-start.5 = (f32[8,1024]{1,0:T(8,128)S(1)}, f32[8,1024]{1,0:T(8,128)}, u32[]{:S(2)}) copy-start(f32[8,1024]{1,0:T(8,128)} %param.11) | copy-start | bytes 98308
  75.5 41.7 %copy-start.2 = (bf16[256,4096]{1,0:T(8,128)(2,1)S(1)}, bf16[256,4096]{1,0:T(8,128)(2,1)}, u32[]{:S(2)}) copy-start(bf16[256,4096]{1,0:T(8,128)(2,1)} %weight_ref.1) | copy-start | bytes 6291460
  117.3 3.4 %copy-start.1 = (bf16[4096,1024]{1,0:T(8,128)(2,1)S(1)}, bf16[4096,1024]{1,0:T(8,128)(2,1)}, u32[]{:S(2)}) copy-start(bf16[4096,1024]{1,0:T(8,128)(2,1)} %all-gather.4.cloned.1.call-done) | copy-start | bytes 25165828
Sparse Core Ops, SparseCore 0:
  40.4 72.8 all-gather.3

commit v7 on v6

--- a/solution.py
+++ b/solution.py
@@ -39,10 +39,11 @@
 STEP = 2
 
 
-def decode_kernel(update_ref, basis_ref, weight_ref, out_ref, new, sems):
-    two, ys, xs, zhs, piece, rank = basis_ref.shape
-    shard = two * ys * piece
-    cols = STEP * shard
+def decode_kernel(core_ref, update_ref, mine_ref, other_ref, weight_ref, out_ref, new, sems):
+    ys, xs, zhs, piece, rank = mine_ref.shape
+    half = ys * piece
+    cols = STEP * 2 * half
+    first = core_ref[0] == 0
 
     def copy_out(i):
         where = pl.ds(i * cols, cols)
@@ -51,30 +52,37 @@
     updates = update_ref[...].reshape(-1, rank)
     steps = xs * zhs // STEP
     for i in range(steps):
-        shards = [
-            basis_ref[:, :, f % xs, f // xs].reshape(shard, rank)
+        halves = [
+            ref[:, f % xs, f // xs].reshape(half, rank)
             for f in range(i * STEP, (i + 1) * STEP)
+            for ref in (mine_ref, other_ref)
         ]
         decoded = lax.dot_general(
             updates,
-            jnp.concatenate(shards, axis=0),
+            jnp.concatenate(halves, axis=0),
             (((1,), (1,)), ((), ())),
             preferred_element_type=jnp.float32,
         )
         decoded = decoded.reshape(2, -1, 8, cols)
         decoded = jnp.stack([decoded[0], decoded[1]], axis=1).reshape(-1, cols)
-        old = weight_ref[:, i * cols : (i + 1) * cols].astype(jnp.float32)
-        new[:, i * cols : (i + 1) * cols] = (old - step_rate * decoded).astype(new.dtype)
+        for k in range(0, 2 * STEP, 2):
+            own = decoded[:, k * half : (k + 1) * half]
+            other = decoded[:, (k + 1) * half : (k + 2) * half]
+            for j, part in ((k, jnp.where(first, own, other)), (k + 1, jnp.where(first, other, own))):
+                at = slice(i * cols + j * half, i * cols + (j + 1) * half)
+                old = weight_ref[:, at].astype(jnp.float32)
+                new[:, at] = (old - step_rate * part).astype(new.dtype)
         copy_out(i).start()
     for i in range(steps):
         copy_out(i).wait()
 
 
-def decode(updates, basis_pieces, weight):
-    steps = basis_pieces.shape[2] * basis_pieces.shape[3] // STEP
+def decode(core, updates, mine, other, weight):
+    steps = mine.shape[1] * mine.shape[2] // STEP
+    vmem = pl.BlockSpec(memory_space=pltpu.VMEM)
     return pl.pallas_call(
         decode_kernel,
-        in_specs=[pl.BlockSpec(memory_space=pltpu.VMEM)] * 3,
+        in_specs=[pl.BlockSpec(memory_space=pltpu.SMEM), vmem, vmem, vmem, vmem],
         out_specs=pl.BlockSpec(memory_space=pl.ANY),
         out_shape=jax.ShapeDtypeStruct(weight.shape, weight.dtype),
         scratch_shapes=[
@@ -83,7 +91,7 @@
         ],
         compiler_params=pltpu.CompilerParams(vmem_limit_bytes=24 * 1024 * 1024),
         name="decode",
-    )(updates, basis_pieces, weight)
+    )(core, updates, mine, other, weight)
 
 
 def local(activations, output_grads, basis, weight, first_moment, second_moment):
@@ -96,12 +104,11 @@
     rank = over_x.shape[1]
     mine = lax.all_gather(mine, "zh", axis=0, tiled=True)
     over_x, mine = lax.optimization_barrier((over_x, mine))
-    basis_pieces = lax.all_gather(mine, ("c", "y", "x"), axis=0, tiled=True)
-    basis_pieces = basis_pieces.reshape(2, 4, 4, 4, piece, rank)
+    basis_half = gather(mine, ("y", "x"))
 
     over_all = lax.all_gather(over_x, "zh", axis=0)
     block = jnp.sum(over_all.astype(jnp.float32), axis=0).astype(jnp.bfloat16)
-    projected = gather(block, "x")
+    projected = lax.all_gather(block, "x", axis=0, tiled=True)
     local_term = (
         lax.dot_general(
             output_grads, projected, (((0,), (0,)), ((), ())), preferred_element_type=jnp.float32
@@ -114,6 +121,8 @@
     sent = lax.all_gather(send, "c", axis=0)
     received = lax.dynamic_index_in_dim(sent, 1 - core, 0, keepdims=False)
     chip_term = keep + received.astype(jnp.float32)
+    chip_term, basis_half = lax.optimization_barrier((chip_term, basis_half))
+    other_half = lax.ppermute(basis_half, "c", [(0, 1), (1, 0)])
     low_grad = exchange_sum(chip_term.reshape(-1, rank), ("zl", "y"))
     new_first = first_decay * first_moment + (1.0 - first_decay) * low_grad
     new_second = second_decay * second_moment + (1.0 - second_decay) * low_grad * low_grad
@@ -121,7 +130,12 @@
         jnp.bfloat16
     )
     updates = lax.all_gather(gather(update, ("zl", "y")), "c", axis=0)
-    return (decode(updates, basis_pieces, weight), new_first, new_second)
+    which = jnp.full((1,), core, jnp.int32)
+    shape = (4, 4, 4, piece, rank)
+    new_weight = decode(
+        which, updates, basis_half.reshape(shape), other_half.reshape(shape), weight
+    )
+    return (new_weight, new_first, new_second)
 
 
 def solution(mesh):

time: 131 us -> 152 us (1.16)
  blocking collectives: 88.5 us -> 124 us
  between operations: 14.1 us -> 0.75 us
  waiting for transfers between devices: 6.95 us -> 0.01 us
  starting transfers between devices: 9.29 us -> 14.4 us
  Pallas kernels: 3.14 us -> 5.54 us
  local copies, waits for them, and re-layouts: 5.35 us -> 3.63 us
    all_gather x0 -> x1, blocking collectives: none -> 38.7 us  [local(): projected = lax.all_gather(block, 'x', axis=0, tiled=True)]
    all_to_all x1, waiting for transfers between devices: 6.93 us -> 0.01 us  [gather(): lax.all_to_all(copies, axis, 0, 0, tiled=True)]
    unnamed x12 -> x10, local copies, waits for them, and re-layouts: 4.43 us -> 1.05 us
    all_to_all x1, starting transfers between devices: 4.45 us -> 7.24 us  [gather(): lax.all_to_all(copies, axis, 0, 0, tiled=True)]
    pallas_call x1, Pallas kernels: 3.14 us -> 5.54 us  [decode(): pl.pallas_call(decode_kernel, in_specs=[pl.BlockSpec(memory_space=pltpu.S...]
    ppermute x0 -> x1, starting transfers between devices: none -> 2.28 us  [local(): other_half = lax.ppermute(basis_half, 'c', [(0, 1), (1, 0)])]
    broadcast_in_dim x2, local copies, waits for them, and re-layouts: 0.87 us -> 2.53 us  [gather(): copies = jnp.broadcast_to(value[None], (size,) + value.shape)]
  transfers between devices with their start and end apart: 3 -> 3, of which waited for: 1 -> 0; matrix products, arithmetic and copies ran while one was open for 2% -> 1% of each run, Pallas kernels for 0% -> 0%
where the time goes in v7:
time: 152 us
  blocking collectives  124 us (82%)
  starting transfers between devices  14.4 us (9%)
  Pallas kernels  5.54 us (4%)
  local copies, waits for them, and re-layouts  3.63 us (2%)
  matrix products  2.34 us (2%)
    all_gather x1, blocking collectives, local(): projected = lax.all_gather(block, 'x', axis=0, tiled=True)  38.7 us
    all_gather x1, blocking collectives, local(): mine = lax.all_gather(mine, 'zh', axis=0, tiled=True)  24.4 us
    all_gather x1, blocking collectives, local(): over_all = lax.all_gather(over_x, 'zh', axis=0)  21.7 us
    all_to_all x1, blocking collectives, exchange_sum(): parts = lax.all_to_all(parts, axis, 0, 0, tiled=True)  15.1 us
    all_to_all x1, blocking collectives, gather(): lax.all_to_all(copies, axis, 0, 0, tiled=True)  13.3 us
    all_to_all x1, starting transfers between devices, gather(): lax.all_to_all(copies, axis, 0, 0, tiled=True)  7.24 us
    all_gather x1, blocking collectives, local(): sent = lax.all_gather(send, 'c', axis=0)  6.88 us
    pallas_call x1, Pallas kernels, decode(): pl.pallas_call(decode_kernel, in_specs=[pl.BlockSpec(memory_space=pltpu.S...  5.54 us
  transfers between devices with their start and end apart: 3, of which 0 were waited for; matrix products, arithmetic and copies ran while one was open for 1% of the time, Pallas kernels for 0%

profile of v7, /device:TPU:1, one launch (start us, length us, event | category | flops | bytes accessed | tf_op | source)
XLA Modules:
  0.0 151.7 jit_solution(13851645428622234927)
XLA Ops:
  0.6 0.0 copy-start
  0.7 1.0 copy-done
  1.7 2.0 %convolution_convert_fusion = bf16[256,1024]{1,0:T(8,128)(2,1)} fusion(bf16[256,256]{1,0:T(8,128)(2,1)} %param.6, bf16[256,1024]{1,0:T(8,128)(2,1)S(1)} %copy-done), kind=kOutput, calls=%fused_computation.1 | convolution fusion | flops 134479872 | bytes 1179648 | tf_op jit(solution)/shard_map/dot_general | solution.py:99
  3.7 4.8 %all-to-all-start = ((bf16[4,64,1024]{2,1,0:T(8,128)(2,1)}), bf16[4,64,1024]{2,1,0:T(8,128)(2,1)S(1)}, u32[]{:S(2)}, u32[]{:S(2)}) async-start(bf16[4,64,1024]{2,1,0:T(8,128)(2,1)} %bitcast.1), calls=%async_computation | async-start | bytes 1048576 | tf_op jit(solution)/shard_map/all_to_all | solution.py:27
  8.5 24.4 %all_gather.19 = bf16[128,1024]{1,0:T(8,128)(2,1)S(1)} all-gather(bf16[32,1024]{1,0:T(8,128)(2,1)S(1)} %constant_dynamic-slice_fusion), channel_id=1, replica_groups=mesh['zl'=4,'y'=4,'c'=2,'zh'=4,'x'=4] {'zh'}, dimensions={0}, use_global_device_ids=true | all-gather | bytes 327680 | tf_op jit(solution)/shard_map/all_gather | solution.py:105
  32.9 0.1 reduce_sum.33
  33.0 2.5 %broadcast_in_dim.7 = bf16[16,128,1024]{2,1,0:T(8,128)(2,1)} broadcast(bf16[128,1024]{1,0:T(8,128)(2,1)S(1)} %all_gather.19), dimensions={1,2} | broadcast | bytes 4456448 | tf_op jit(solution)/shard_map/broadcast_in_dim | solution.py:33
  35.5 7.2 %all-to-all-start.1 = ((bf16[16,128,1024]{2,1,0:T(8,128)(2,1)}), bf16[16,128,1024]{2,1,0:T(8,128)(2,1)}, u32[]{:S(2)}, u32[]{:S(2)}) async-start(bf16[16,128,1024]{2,1,0:T(8,128)(2,1)} %broadcast_in_dim.7), calls=%async_computation.1 | async-start | bytes 8388608 | tf_op jit(solution)/shard_map/all_to_all | solution.py:34
  42.8 0.0 copy-start.3
  42.8 0.0 copy-start.4
  42.8 0.0 copy-start.1
  42.8 21.7 %all-gather = bf16[256,1024]{1,0:T(8,128)(2,1)S(1)} all-gather(bf16[64,1024]{1,0:T(8,128)(2,1)S(1)} %reduce_sum.33), channel_id=2, replica_groups=mesh['zl'=4,'y'=4,'c'=2,'zh'=4,'x'=4] {'zh'}, dimensions={0}, use_global_device_ids=true | all-gather | bytes 655360 | tf_op jit(solution)/shard_map/all_gather | solution.py:109
  64.5 0.1 reduce_sum.34
  64.6 38.7 %all_gather.22 = bf16[256,1024]{1,0:T(8,128)(2,1)S(1)} all-gather(bf16[64,1024]{1,0:T(8,128)(2,1)S(1)} %reduce_sum.34), channel_id=1, replica_groups=mesh['zl'=4,'y'=4,'c'=2,'zh'=4,'x'=4] {'x'}, dimensions={0}, use_global_device_ids=true | all-gather | bytes 655360 | tf_op jit(solution)/shard_map/all_gather | solution.py:111
  103.2 0.3 convolution_multiply_fusion
  103.6 6.9 %all-gather.1 = bf16[32,1,8,1024]{3,2,1,0:T(8,128)(2,1)S(1)} all-gather(bf16[16,1,8,1024]{3,2,1,0:T(8,128)(2,1)S(1)} %dynamic-slice_convert_fusion), channel_id=3, replica_groups=mesh['zl'=4,'y'=4,'c'=2,'zh'=4,'x'=4] {'c'}, dimensions={0}, use_global_device_ids=true | all-gather | bytes 786432 | tf_op jit(solution)/shard_map/all_gather | solution.py:121
  110.5 0.1 convert_add_fusion
  110.6 2.3 %collective-permute-start = (bf16[2048,1024]{1,0:T(8,128)(2,1)}, bf16[2048,1024]{1,0:T(8,128)(2,1)S(1)}, u32[]{:S(2)}, u32[]{:S(2)}) collective-permute-start(bf16[2048,1024]{1,0:T(8,128)(2,1)} %bitcast.9), channel_id=1, source_target_pairs={{0,16},{16,0},{1,17},{17,1},{2,18},{18,2},{3,19},{19,3},{4,20},{20... | collective-permute-start | bytes 12582920 | tf_op jit(solution)/shard_map/ppermute | solution.py:125
  112.9 15.1 %all_to_all.20 = bf16[16,8,1024]{2,1,0:T(8,128)(2,1)S(1)} all-to-all(bf16[16,8,1024]{2,1,0:T(8,128)(2,1)S(1)} %convert_add_fusion), channel_id=1, replica_groups=mesh['zl'=4,'y'=4,'c'=2,'zh'=4,'x'=4] {'zl','y'}, dimensions={0} | all-to-all | bytes 524288 | tf_op jit(solution)/shard_map/all_to_all | solution.py:27
  128.0 0.6 divide_convert_fusion
  128.7 13.3 %all_to_all.21 = bf16[16,8,1024]{2,1,0:T(8,128)(2,1)S(1)} all-to-all(bf16[16,8,1024]{2,1,0:T(8,128)(2,1)S(1)} %broadcast_in_dim.8), channel_id=1, replica_groups=mesh['zl'=4,'y'=4,'c'=2,'zh'=4,'x'=4] {'zl','y'}, dimensions={0} | all-to-all | bytes 524288 | tf_op jit(solution)/shard_map/all_to_all | solution.py:34
  142.0 4.1 %all_gather.24.update_ref = bf16[2,128,1024]{2,1,0:T(8,128)(2,1)S(1)} all-gather(bf16[1,128,1024]{2,1,0:T(8,128)(2,1)S(1)} %bitcast.25), channel_id=1, replica_groups=mesh['zl'=4,'y'=4,'c'=2,'zh'=4,'x'=4] {'c'}, dimensions={0}, use_global_device_ids=true | all-gather | bytes 786432 | tf_op jit(solution)/shard_map/all_gather | solution.py:132
  146.1 0.0 collective-permute-done
  146.1 5.5 %decode.1 = bf16[256,4096]{1,0:T(8,128)(2,1)} custom-call(s32[1]{0:T(128)} %bitcast.core_ref, bf16[2,128,1024]{2,1,0:T(8,128)(2,1)S(1)} %all_gather.24.update_ref, bf16[4,4,4,32,1024]{4,3,2,1,0:T(8,128)(2,1)} %bitcast.11.mine_ref, bf16[4,4,4,32,1024]{4,3,2,1,0:T(8,128)(2,1)S(1)} %bitcast.20, bf16[256,4096]{1,0:T(8,128)(2,1)S(1)} %copy-done.1), custom_call_target="tpu_custom_call" | custom-call | tf_op jit(solution)/shard_map/decode/pallas_call | solution.py:83
  (11 shorter events, 0.1 us)
Async XLA Ops:
  0.6 1.0 copy-start
  3.7 29.2 %all-to-all-start = ((bf16[4,64,1024]{2,1,0:T(8,128)(2,1)}), bf16[4,64,1024]{2,1,0:T(8,128)(2,1)S(1)}, u32[]{:S(2)}, u32[]{:S(2)}) async-start(bf16[4,64,1024]{2,1,0:T(8,128)(2,1)} %bitcast.1), calls=%async_computation | async-start | bytes 1048576 | tf_op jit(solution)/shard_map/all_to_all | solution.py:27
  35.5 67.7 %copy-start.2 = (bf16[256,256]{1,0:T(8,128)(2,1)S(1)}, bf16[256,256]{1,0:T(8,128)(2,1)}, u32[]{:S(2)}) copy-start(bf16[256,256]{1,0:T(8,128)(2,1)} %param.7) | copy-start | bytes 393220
  35.5 75.1 %all-to-all-start.1 = ((bf16[16,128,1024]{2,1,0:T(8,128)(2,1)}), bf16[16,128,1024]{2,1,0:T(8,128)(2,1)}, u32[]{:S(2)}, u32[]{:S(2)}) async-start(bf16[16,128,1024]{2,1,0:T(8,128)(2,1)} %broadcast_in_dim.7), calls=%async_computation.1 | async-start | bytes 8388608 | tf_op jit(solution)/shard_map/all_to_all | solution.py:34
  42.8 85.3 %copy-start.3 = (f32[8,1024]{1,0:T(8,128)S(1)}, f32[8,1024]{1,0:T(8,128)}, u32[]{:S(2)}) copy-start(f32[8,1024]{1,0:T(8,128)} %param.10) | copy-start | bytes 98308
  42.8 85.3 %copy-start.4 = (f32[8,1024]{1,0:T(8,128)S(1)}, f32[8,1024]{1,0:T(8,128)}, u32[]{:S(2)}) copy-start(f32[8,1024]{1,0:T(8,128)} %param.11) | copy-start | bytes 98308
  42.8 103.3 %copy-start.1 = (bf16[256,4096]{1,0:T(8,128)(2,1)S(1)}, bf16[256,4096]{1,0:T(8,128)(2,1)}, u32[]{:S(2)}) copy-start(bf16[256,4096]{1,0:T(8,128)(2,1)} %weight_ref.1) | copy-start | bytes 6291460
  110.6 35.5 %collective-permute-start = (bf16[2048,1024]{1,0:T(8,128)(2,1)}, bf16[2048,1024]{1,0:T(8,128)(2,1)S(1)}, u32[]{:S(2)}, u32[]{:S(2)}) collective-permute-start(bf16[2048,1024]{1,0:T(8,128)(2,1)} %bitcast.9), channel_id=1, source_target_pairs={{0,16},{16,0},{1,17},{17,1},{2,18},{18,2},{3,19},{19,3},{4,20},{20... | collective-permute-start | bytes 12582920 | tf_op jit(solution)/shard_map/ppermute | solution.py:125

commit v8 on v6

--- a/solution.py
+++ b/solution.py
@@ -34,6 +34,39 @@
     return lax.all_to_all(copies, axis, 0, 0, tiled=True).reshape(
         size * value.shape[0], value.shape[1]
     )
+
+
+def product_kernel(left_ref, right_ref, out_ref, left, right, out, sems):
+    copies = [
+        pltpu.make_async_copy(left_ref, left, sems.at[0]),
+        pltpu.make_async_copy(right_ref, right, sems.at[1]),
+    ]
+    for copy in copies:
+        copy.start()
+    for copy in copies:
+        copy.wait()
+    out[...] = jnp.dot(left[...], right[...], preferred_element_type=jnp.float32).astype(out.dtype)
+    store = pltpu.make_async_copy(out, out_ref, sems.at[2])
+    store.start()
+    store.wait()
+
+
+def product(left, right):
+    shape = (left.shape[0], right.shape[1])
+    return pl.pallas_call(
+        product_kernel,
+        in_specs=[pl.BlockSpec(memory_space=pl.ANY)] * 2,
+        out_specs=pl.BlockSpec(memory_space=pl.ANY),
+        out_shape=jax.ShapeDtypeStruct(shape, jnp.bfloat16),
+        scratch_shapes=[
+            pltpu.VMEM(left.shape, left.dtype),
+            pltpu.VMEM(right.shape, right.dtype),
+            pltpu.VMEM(shape, jnp.bfloat16),
+            pltpu.SemaphoreType.DMA((3,)),
+        ],
+        compiler_params=pltpu.CompilerParams(vmem_limit_bytes=60 * 1024 * 1024),
+        name="product",
+    )(left, right)
 
 
 STEP = 2
@@ -88,10 +121,10 @@
 
 def local(activations, output_grads, basis, weight, first_moment, second_moment):
     core = lax.axis_index("c")
-    partial_product = jnp.dot(activations, basis, preferred_element_type=jnp.float32)
+    partial_product = product(activations, basis)
     piece = basis.shape[0] // 8
     mine = lax.dynamic_slice_in_dim(basis, (core * 4 + lax.axis_index("y")) * piece, piece, 0)
-    partial_product, mine = lax.optimization_barrier((partial_product.astype(jnp.bfloat16), mine))
+    partial_product, mine, first = lax.optimization_barrier((partial_product, mine, core == 0))
     over_x = exchange_sum(partial_product, "x").astype(jnp.bfloat16)
     rank = over_x.shape[1]
     mine = lax.all_gather(mine, "zh", axis=0, tiled=True)
@@ -109,10 +142,10 @@
         / TOKENS
     )
     parts = local_term.reshape(-1, 2, 8, rank)
-    keep = lax.dynamic_index_in_dim(parts, core, 1, keepdims=False)
-    send = lax.dynamic_index_in_dim(parts, 1 - core, 1, keepdims=False).astype(jnp.bfloat16)
+    keep = jnp.where(first, parts[:, 0], parts[:, 1])
+    send = jnp.where(first, parts[:, 1], parts[:, 0]).astype(jnp.bfloat16)
     sent = lax.all_gather(send, "c", axis=0)
-    received = lax.dynamic_index_in_dim(sent, 1 - core, 0, keepdims=False)
+    received = jnp.where(first, sent[1], sent[0])
     chip_term = keep + received.astype(jnp.float32)
     low_grad = exchange_sum(chip_term.reshape(-1, rank), ("zl", "y"))
     new_first = first_decay * first_moment + (1.0 - first_decay) * low_grad

time: 131 us -> 130 us (level)
  blocking collectives: 88.5 us -> 99.5 us
  waiting for transfers between devices: 6.95 us -> 0.02 us
  starting transfers between devices: 9.29 us -> 4.86 us
  Pallas kernels: 3.14 us -> 5.38 us
  matrix products: 2.34 us -> 0.34 us
    all_to_all x1 -> x2, blocking collectives: 13.1 us -> 24.3 us  [gather(): lax.all_to_all(copies, axis, 0, 0, tiled=True)]
    all_to_all x1 -> x0, waiting for transfers between devices: 6.93 us -> none  [gather(): lax.all_to_all(copies, axis, 0, 0, tiled=True)]
    all_to_all x1 -> x0, starting transfers between devices: 4.45 us -> none  [gather(): lax.all_to_all(copies, axis, 0, 0, tiled=True)]
    pallas_call x0 -> x1, Pallas kernels: none -> 2.24 us  [product(): pl.pallas_call(product_kernel, in_specs=[pl.BlockSpec(memory_space=pl.ANY...]
    dot_general x1 -> x0, matrix products: 2 us -> none  [local(): jnp.dot(activations, basis, preferred_element_type=jnp.float32)]
    unnamed x12 -> x10, local copies, waits for them, and re-layouts: 4.43 us -> 3.41 us
  transfers between devices with their start and end apart: 3 -> 2, of which waited for: 1 -> 0; matrix products, arithmetic and copies ran while one was open for 2% -> 1% of each run, Pallas kernels for 0% -> 0%
where the time goes in v8:
time: 130 us
  blocking collectives  99.5 us (77%)
  between operations  14.1 us (11%)
  Pallas kernels  5.38 us (4%)
  starting transfers between devices  4.86 us (4%)
  local copies, waits for them, and re-layouts  4.36 us (3%)
    all_gather x1, blocking collectives, local(): mine = lax.all_gather(mine, 'zh', axis=0, tiled=True)  24.9 us
    all_to_all x2, blocking collectives, gather(): lax.all_to_all(copies, axis, 0, 0, tiled=True)  24.3 us
    all_gather x1, blocking collectives, local(): over_all = lax.all_gather(over_x, 'zh', axis=0)  22.5 us
    all_to_all x1, blocking collectives, exchange_sum(): parts = lax.all_to_all(parts, axis, 0, 0, tiled=True)  16.3 us
    all_gather x1, blocking collectives, local(): sent = lax.all_gather(send, 'c', axis=0)  7.06 us
    all_to_all x1, starting transfers between devices, exchange_sum(): parts = lax.all_to_all(parts, axis, 0, 0, tiled=True)  4.85 us
    all_gather x1, blocking collectives, local(): updates = lax.all_gather(gather(update, ('zl', 'y')), 'c', axis=0)  4.31 us
    unnamed x10, local copies, waits for them, and re-layouts  3.41 us
  transfers between devices with their start and end apart: 2, of which 0 were waited for; matrix products, arithmetic and copies ran while one was open for 1% of the time, Pallas kernels for 0%

profile of v8, /device:TPU:1, one launch (start us, length us, event | category | flops | bytes accessed | tf_op | source)
XLA Modules:
  0.0 129.6 jit_solution(16998184966909138825)
XLA Ops:
  7.2 0.0 copy-start
  7.2 0.9 constant_dynamic-slice_fusion
  8.1 2.2 %product.1 = bf16[256,1024]{1,0:T(8,128)(2,1)} custom-call(bf16[256,256]{1,0:T(8,128)(2,1)} %left_ref.1, bf16[256,1024]{1,0:T(8,128)(2,1)} %right_ref.1), custom_call_target="tpu_custom_call" | custom-call | tf_op jit(solution)/shard_map/product/pallas_call | solution.py:56
  10.3 4.9 %all-to-all-start = ((bf16[4,64,1024]{2,1,0:T(8,128)(2,1)}), bf16[4,64,1024]{2,1,0:T(8,128)(2,1)S(1)}, u32[]{:S(2)}, u32[]{:S(2)}) async-start(bf16[4,64,1024]{2,1,0:T(8,128)(2,1)} %bitcast.16), calls=%async_computation | async-start | bytes 1048576 | tf_op jit(solution)/shard_map/all_to_all | solution.py:27
  15.2 24.9 %all_gather.19 = bf16[128,1024]{1,0:T(8,128)(2,1)} all-gather(bf16[32,1024]{1,0:T(8,128)(2,1)S(1)} %constant_dynamic-slice_fusion), channel_id=1, replica_groups=mesh['zl'=4,'y'=4,'c'=2,'zh'=4,'x'=4] {'zh'}, dimensions={0}, use_global_device_ids=true | all-gather | bytes 327680 | tf_op jit(solution)/shard_map/all_gather | solution.py:130
  40.1 0.0 all-to-all-done
  40.1 0.1 reduce_sum.33
  40.2 0.0 all-gather.4.cloned.1.call-update
  40.2 22.5 %all-gather = bf16[256,1024]{1,0:T(8,128)(2,1)S(1)} all-gather(bf16[64,1024]{1,0:T(8,128)(2,1)S(1)} %reduce_sum.33), channel_id=2, replica_groups=mesh['zl'=4,'y'=4,'c'=2,'zh'=4,'x'=4] {'zh'}, dimensions={0}, use_global_device_ids=true | all-gather | bytes 655360 | tf_op jit(solution)/shard_map/all_gather | solution.py:135
  62.7 0.1 reduce_sum.34
  62.8 0.1 broadcast_in_dim.4
  62.8 11.2 %all_to_all.20 = bf16[4,64,1024]{2,1,0:T(8,128)(2,1)S(1)} all-to-all(bf16[4,64,1024]{2,1,0:T(8,128)(2,1)S(1)} %broadcast_in_dim.4), channel_id=1, replica_groups=mesh['zl'=4,'y'=4,'c'=2,'zh'=4,'x'=4] {'x'}, dimensions={0} | all-to-all | bytes 1048576 | tf_op jit(solution)/shard_map/all_to_all | solution.py:34
  74.1 0.3 convolution_multiply_fusion
  74.4 0.0 copy-start.3
  74.4 0.0 copy-start.4
  74.4 0.1 select_convert_fusion
  74.5 7.1 %all-gather.1 = bf16[32,1,8,1024]{3,2,1,0:T(8,128)(2,1)S(1)} all-gather(bf16[16,1,8,1024]{3,2,1,0:T(8,128)(2,1)S(1)} %select_convert_fusion), channel_id=3, replica_groups=mesh['zl'=4,'y'=4,'c'=2,'zh'=4,'x'=4] {'c'}, dimensions={0}, use_global_device_ids=true | all-gather | bytes 786432 | tf_op jit(solution)/shard_map/all_gather | solution.py:147
  81.6 0.1 fusion
  81.7 16.3 %all_to_all.21 = bf16[16,8,1024]{2,1,0:T(8,128)(2,1)S(1)} all-to-all(bf16[16,8,1024]{2,1,0:T(8,128)(2,1)S(1)} %fusion), channel_id=1, replica_groups=mesh['zl'=4,'y'=4,'c'=2,'zh'=4,'x'=4] {'zl','y'}, dimensions={0} | all-to-all | bytes 524288 | tf_op jit(solution)/shard_map/all_to_all | solution.py:27
  98.1 0.6 divide_convert_fusion
  98.8 13.1 %all_to_all.22 = bf16[16,8,1024]{2,1,0:T(8,128)(2,1)S(1)} all-to-all(bf16[16,8,1024]{2,1,0:T(8,128)(2,1)S(1)} %broadcast_in_dim.5), channel_id=1, replica_groups=mesh['zl'=4,'y'=4,'c'=2,'zh'=4,'x'=4] {'zl','y'}, dimensions={0} | all-to-all | bytes 524288 | tf_op jit(solution)/shard_map/all_to_all | solution.py:34
  111.9 4.3 %all_gather.23.update_ref = bf16[2,128,1024]{2,1,0:T(8,128)(2,1)S(1)} all-gather(bf16[1,128,1024]{2,1,0:T(8,128)(2,1)S(1)} %bitcast.18), channel_id=1, replica_groups=mesh['zl'=4,'y'=4,'c'=2,'zh'=4,'x'=4] {'c'}, dimensions={0}, use_global_device_ids=true | all-gather | bytes 786432 | tf_op jit(solution)/shard_map/all_gather | solution.py:156
  116.2 3.4 %copy-done.1 = bf16[4096,1024]{1,0:T(8,128)(2,1)S(1)} copy-done((bf16[4096,1024]{1,0:T(8,128)(2,1)S(1)}, bf16[4096,1024]{1,0:T(8,128)(2,1)}, u32[]{:S(2)}) %copy-start.1) | copy-done | bytes 8388632
  119.6 3.1 %decode.1 = bf16[256,4096]{1,0:T(8,128)(2,1)} custom-call(bf16[2,128,1024]{2,1,0:T(8,128)(2,1)S(1)} %all_gather.23.update_ref, bf16[2,4,4,4,32,1024]{5,4,3,2,1,0:T(8,128)(2,1)S(1)} %bitcast.12, bf16[256,4096]{1,0:T(8,128)(2,1)S(1)} %copy-done.2), custom_call_target="tpu_custom_call" | custom-call | tf_op jit(solution)/shard_map/decode/pallas_call | solution.py:108
  (10 shorter events, 0.1 us)
Async XLA Ops:
  7.2 66.9 %copy-start = (bf16[256,256]{1,0:T(8,128)(2,1)S(1)}, bf16[256,256]{1,0:T(8,128)(2,1)}, u32[]{:S(2)}) copy-start(bf16[256,256]{1,0:T(8,128)(2,1)} %param.7) | copy-start | bytes 393220
  10.3 29.8 %all-to-all-start = ((bf16[4,64,1024]{2,1,0:T(8,128)(2,1)}), bf16[4,64,1024]{2,1,0:T(8,128)(2,1)S(1)}, u32[]{:S(2)}, u32[]{:S(2)}) async-start(bf16[4,64,1024]{2,1,0:T(8,128)(2,1)} %bitcast.16), calls=%async_computation | async-start | bytes 1048576 | tf_op jit(solution)/shard_map/all_to_all | solution.py:27
  15.2 101.0 %all-gather.4.cloned.1.call-start = ((), (), s32[]{:S(2)}) async-start(), calls=%async_computation.4 | async-start | bytes 8650752 | tf_op jit(solution)/shard_map/all_gather | solution.py:132
  74.4 23.6 %copy-start.3 = (f32[8,1024]{1,0:T(8,128)S(1)}, f32[8,1024]{1,0:T(8,128)}, u32[]{:S(2)}) copy-start(f32[8,1024]{1,0:T(8,128)} %param.10) | copy-start | bytes 98308
  74.4 23.6 %copy-start.4 = (f32[8,1024]{1,0:T(8,128)S(1)}, f32[8,1024]{1,0:T(8,128)}, u32[]{:S(2)}) copy-start(f32[8,1024]{1,0:T(8,128)} %param.11) | copy-start | bytes 98308
  81.6 34.6 %copy-start.2 = (bf16[256,4096]{1,0:T(8,128)(2,1)S(1)}, bf16[256,4096]{1,0:T(8,128)(2,1)}, u32[]{:S(2)}) copy-start(bf16[256,4096]{1,0:T(8,128)(2,1)} %weight_ref.1) | copy-start | bytes 6291460
  116.2 3.4 %copy-start.1 = (bf16[4096,1024]{1,0:T(8,128)(2,1)S(1)}, bf16[4096,1024]{1,0:T(8,128)(2,1)}, u32[]{:S(2)}) copy-start(bf16[4096,1024]{1,0:T(8,128)(2,1)} %all-gather.4.cloned.1.call-done) | copy-start | bytes 25165828
Sparse Core Ops, SparseCore 0:
  40.3 74.4 all-gather.3

commit v9 on v8

--- a/solution.py
+++ b/solution.py
@@ -36,37 +36,46 @@
     )
 
 
-def product_kernel(left_ref, right_ref, out_ref, left, right, out, sems):
-    copies = [
-        pltpu.make_async_copy(left_ref, left, sems.at[0]),
-        pltpu.make_async_copy(right_ref, right, sems.at[1]),
+def product_kernel(start_ref, left_ref, right_ref, out_ref, piece_ref, left, right, out, sems):
+    rows = piece_ref.shape[0]
+    loads = [
+        pltpu.make_async_copy(right_ref, right, sems.at[0]),
+        pltpu.make_async_copy(left_ref, left, sems.at[1]),
     ]
-    for copy in copies:
-        copy.start()
-    for copy in copies:
-        copy.wait()
+    for load in loads:
+        load.start()
+    for load in loads:
+        load.wait()
+    where = pl.ds(pl.multiple_of(start_ref[0] * rows, rows), rows)
+    piece = pltpu.make_async_copy(right.at[where], piece_ref, sems.at[2])
+    piece.start()
     out[...] = jnp.dot(left[...], right[...], preferred_element_type=jnp.float32).astype(out.dtype)
-    store = pltpu.make_async_copy(out, out_ref, sems.at[2])
+    store = pltpu.make_async_copy(out, out_ref, sems.at[3])
     store.start()
+    piece.wait()
     store.wait()
 
 
-def product(left, right):
+def product(left, right, which, rows):
     shape = (left.shape[0], right.shape[1])
+    anywhere = pl.BlockSpec(memory_space=pl.ANY)
     return pl.pallas_call(
         product_kernel,
-        in_specs=[pl.BlockSpec(memory_space=pl.ANY)] * 2,
-        out_specs=pl.BlockSpec(memory_space=pl.ANY),
-        out_shape=jax.ShapeDtypeStruct(shape, jnp.bfloat16),
+        in_specs=[pl.BlockSpec(memory_space=pltpu.SMEM), anywhere, anywhere],
+        out_specs=[anywhere, anywhere],
+        out_shape=[
+            jax.ShapeDtypeStruct(shape, jnp.bfloat16),
+            jax.ShapeDtypeStruct((rows, right.shape[1]), right.dtype),
+        ],
         scratch_shapes=[
             pltpu.VMEM(left.shape, left.dtype),
             pltpu.VMEM(right.shape, right.dtype),
             pltpu.VMEM(shape, jnp.bfloat16),
-            pltpu.SemaphoreType.DMA((3,)),
+            pltpu.SemaphoreType.DMA((4,)),
         ],
         compiler_params=pltpu.CompilerParams(vmem_limit_bytes=60 * 1024 * 1024),
         name="product",
-    )(left, right)
+    )(which, left, right)
 
 
 STEP = 2
@@ -121,14 +130,17 @@
 
 def local(activations, output_grads, basis, weight, first_moment, second_moment):
     core = lax.axis_index("c")
-    partial_product = product(activations, basis)
     piece = basis.shape[0] // 8
-    mine = lax.dynamic_slice_in_dim(basis, (core * 4 + lax.axis_index("y")) * piece, piece, 0)
+    which = jnp.full((1,), core * 4 + lax.axis_index("y"), jnp.int32)
+    partial_product, mine = product(activations, basis, which, piece)
     partial_product, mine, first = lax.optimization_barrier((partial_product, mine, core == 0))
-    over_x = exchange_sum(partial_product, "x").astype(jnp.bfloat16)
-    rank = over_x.shape[1]
+    rows, rank = partial_product.shape
+    blocks = lax.all_to_all(
+        partial_product.reshape(4, rows // 4, rank), "x", 0, 0, tiled=True
+    )
     mine = lax.all_gather(mine, "zh", axis=0, tiled=True)
-    over_x, mine = lax.optimization_barrier((over_x, mine))
+    blocks, mine = lax.optimization_barrier((blocks, mine))
+    over_x = jnp.sum(blocks.astype(jnp.float32), axis=0).astype(jnp.bfloat16)
     basis_pieces = lax.all_gather(mine, ("c", "y", "x"), axis=0, tiled=True)
     basis_pieces = basis_pieces.reshape(2, 4, 4, 4, piece, rank)
 

time: 130 us -> 129 us (level)
  no operation moved by 1% of the time
where the time goes in v9:
time: 129 us
  blocking collectives  99.7 us (77%)
  between operations  14.1 us (11%)
  Pallas kernels  5.37 us (4%)
  starting transfers between devices  4.86 us (4%)
  local copies, waits for them, and re-layouts  3.48 us (3%)
    all_gather x1, blocking collectives, local(): mine = lax.all_gather(mine, 'zh', axis=0, tiled=True)  25.1 us
    all_to_all x2, blocking collectives, gather(): lax.all_to_all(copies, axis, 0, 0, tiled=True)  24.3 us
    all_gather x1, blocking collectives, local(): over_all = lax.all_gather(over_x, 'zh', axis=0)  22.5 us
    all_to_all x1, blocking collectives, exchange_sum(): parts = lax.all_to_all(parts, axis, 0, 0, tiled=True)  16.4 us
    all_gather x1, blocking collectives, local(): sent = lax.all_gather(send, 'c', axis=0)  6.98 us
    all_to_all x1, starting transfers between devices, local(): lax.all_to_all(partial_product.reshape(4, rows // 4, rank), 'x', 0, 0, ti...  4.85 us
    all_gather x1, blocking collectives, local(): updates = lax.all_gather(gather(update, ('zl', 'y')), 'c', axis=0)  4.31 us
    unnamed x10, local copies, waits for them, and re-layouts  3.41 us
  transfers between devices with their start and end apart: 2, of which 0 were waited for; matrix products, arithmetic and copies ran while one was open for 1% of the time, Pallas kernels for 0%

profile of v9, /device:TPU:1, one launch (start us, length us, event | category | flops | bytes accessed | tf_op | source)
XLA Modules:
  0.0 128.9 jit_solution(13632146563742177159)
XLA Ops:
  7.2 0.0 copy-start
  7.2 2.2 %product.1 = (bf16[256,1024]{1,0:T(8,128)(2,1)}, bf16[32,1024]{1,0:T(8,128)(2,1)}) custom-call(s32[1]{0:T(128)} %bitcast.start_ref, bf16[256,256]{1,0:T(8,128)(2,1)} %left_ref.1, bf16[256,1024]{1,0:T(8,128)(2,1)} %right_ref.1), custom_call_target="tpu_custom_call" | custom-call | tf_op jit(solution)/shard_map/product/pallas_call | solution.py:62
  9.4 4.9 %all-to-all-start = ((bf16[4,64,1024]{2,1,0:T(8,128)(2,1)}), bf16[4,64,1024]{2,1,0:T(8,128)(2,1)S(1)}, u32[]{:S(2)}, u32[]{:S(2)}) async-start(bf16[4,64,1024]{2,1,0:T(8,128)(2,1)} %bitcast.19), calls=%async_computation | async-start | bytes 1048576 | tf_op jit(solution)/shard_map/all_to_all | solution.py:138
  14.3 25.1 %all_gather.19 = bf16[128,1024]{1,0:T(8,128)(2,1)} all-gather(bf16[32,1024]{1,0:T(8,128)(2,1)} %get-tuple-element.14), channel_id=1, replica_groups=mesh['zl'=4,'y'=4,'c'=2,'zh'=4,'x'=4] {'zh'}, dimensions={0}, use_global_device_ids=true | all-gather | bytes 327680 | tf_op jit(solution)/shard_map/all_gather | solution.py:141
  39.4 0.0 all-to-all-done
  39.4 0.0 all-gather.4.cloned.1.call-update
  39.5 0.1 reduce_sum.33
  39.5 22.5 %all-gather = bf16[256,1024]{1,0:T(8,128)(2,1)S(1)} all-gather(bf16[64,1024]{1,0:T(8,128)(2,1)S(1)} %reduce_sum.33), channel_id=2, replica_groups=mesh['zl'=4,'y'=4,'c'=2,'zh'=4,'x'=4] {'zh'}, dimensions={0}, use_global_device_ids=true | all-gather | bytes 655360 | tf_op jit(solution)/shard_map/all_gather | solution.py:147
  62.1 0.1 reduce_sum.34
  62.2 0.1 broadcast_in_dim.7
  62.2 11.1 %all_to_all.20 = bf16[4,64,1024]{2,1,0:T(8,128)(2,1)S(1)} all-to-all(bf16[4,64,1024]{2,1,0:T(8,128)(2,1)S(1)} %broadcast_in_dim.7), channel_id=1, replica_groups=mesh['zl'=4,'y'=4,'c'=2,'zh'=4,'x'=4] {'x'}, dimensions={0} | all-to-all | bytes 1048576 | tf_op jit(solution)/shard_map/all_to_all | solution.py:34
  73.4 0.3 convolution_multiply_fusion
  73.7 0.0 copy-start.3
  73.7 0.0 copy-start.4
  73.7 0.1 select_convert_fusion
  73.8 7.0 %all-gather.1 = bf16[32,1,8,1024]{3,2,1,0:T(8,128)(2,1)S(1)} all-gather(bf16[16,1,8,1024]{3,2,1,0:T(8,128)(2,1)S(1)} %select_convert_fusion), channel_id=3, replica_groups=mesh['zl'=4,'y'=4,'c'=2,'zh'=4,'x'=4] {'c'}, dimensions={0}, use_global_device_ids=true | all-gather | bytes 786432 | tf_op jit(solution)/shard_map/all_gather | solution.py:159
  80.8 0.1 fusion
  80.9 16.4 %all_to_all.21 = bf16[16,8,1024]{2,1,0:T(8,128)(2,1)S(1)} all-to-all(bf16[16,8,1024]{2,1,0:T(8,128)(2,1)S(1)} %fusion), channel_id=1, replica_groups=mesh['zl'=4,'y'=4,'c'=2,'zh'=4,'x'=4] {'zl','y'}, dimensions={0} | all-to-all | bytes 524288 | tf_op jit(solution)/shard_map/all_to_all | solution.py:27
  97.4 0.0 copy-done.4
  97.4 0.6 divide_convert_fusion
  98.1 13.1 %all_to_all.22 = bf16[16,8,1024]{2,1,0:T(8,128)(2,1)S(1)} all-to-all(bf16[16,8,1024]{2,1,0:T(8,128)(2,1)S(1)} %broadcast_in_dim.8), channel_id=1, replica_groups=mesh['zl'=4,'y'=4,'c'=2,'zh'=4,'x'=4] {'zl','y'}, dimensions={0} | all-to-all | bytes 524288 | tf_op jit(solution)/shard_map/all_to_all | solution.py:34
  111.2 4.3 %all_gather.23.update_ref = bf16[2,128,1024]{2,1,0:T(8,128)(2,1)S(1)} all-gather(bf16[1,128,1024]{2,1,0:T(8,128)(2,1)S(1)} %bitcast.18), channel_id=1, replica_groups=mesh['zl'=4,'y'=4,'c'=2,'zh'=4,'x'=4] {'c'}, dimensions={0}, use_global_device_ids=true | all-gather | bytes 786432 | tf_op jit(solution)/shard_map/all_gather | solution.py:168
  115.5 3.4 %copy-done.1 = bf16[4096,1024]{1,0:T(8,128)(2,1)S(1)} copy-done((bf16[4096,1024]{1,0:T(8,128)(2,1)S(1)}, bf16[4096,1024]{1,0:T(8,128)(2,1)}, u32[]{:S(2)}) %copy-start.1) | copy-done | bytes 8388632
  118.9 3.1 %decode.1 = bf16[256,4096]{1,0:T(8,128)(2,1)} custom-call(bf16[2,128,1024]{2,1,0:T(8,128)(2,1)S(1)} %all_gather.23.update_ref, bf16[2,4,4,4,32,1024]{5,4,3,2,1,0:T(8,128)(2,1)S(1)} %bitcast.13, bf16[256,4096]{1,0:T(8,128)(2,1)S(1)} %copy-done.2), custom_call_target="tpu_custom_call" | custom-call | tf_op jit(solution)/shard_map/decode/pallas_call | solution.py:117
  (9 shorter events, 0.1 us)
Async XLA Ops:
  7.2 66.2 %copy-start = (bf16[256,256]{1,0:T(8,128)(2,1)S(1)}, bf16[256,256]{1,0:T(8,128)(2,1)}, u32[]{:S(2)}) copy-start(bf16[256,256]{1,0:T(8,128)(2,1)} %param.7) | copy-start | bytes 393220
  9.4 30.0 %all-to-all-start = ((bf16[4,64,1024]{2,1,0:T(8,128)(2,1)}), bf16[4,64,1024]{2,1,0:T(8,128)(2,1)S(1)}, u32[]{:S(2)}, u32[]{:S(2)}) async-start(bf16[4,64,1024]{2,1,0:T(8,128)(2,1)} %bitcast.19), calls=%async_computation | async-start | bytes 1048576 | tf_op jit(solution)/shard_map/all_to_all | solution.py:138
  14.3 101.2 %all-gather.4.cloned.1.call-start = ((), (), s32[]{:S(2)}) async-start(), calls=%async_computation.4 | async-start | bytes 8650752 | tf_op jit(solution)/shard_map/all_gather | solution.py:144
  73.7 23.7 %copy-start.3 = (f32[8,1024]{1,0:T(8,128)S(1)}, f32[8,1024]{1,0:T(8,128)}, u32[]{:S(2)}) copy-start(f32[8,1024]{1,0:T(8,128)} %param.10) | copy-start | bytes 98308
  73.7 23.7 %copy-start.4 = (f32[8,1024]{1,0:T(8,128)S(1)}, f32[8,1024]{1,0:T(8,128)}, u32[]{:S(2)}) copy-start(f32[8,1024]{1,0:T(8,128)} %param.11) | copy-start | bytes 98308
  80.8 34.7 %copy-start.2 = (bf16[256,4096]{1,0:T(8,128)(2,1)S(1)}, bf16[256,4096]{1,0:T(8,128)(2,1)}, u32[]{:S(2)}) copy-start(bf16[256,4096]{1,0:T(8,128)(2,1)} %weight_ref.1) | copy-start | bytes 6291460
  115.5 3.4 %copy-start.1 = (bf16[4096,1024]{1,0:T(8,128)(2,1)S(1)}, bf16[4096,1024]{1,0:T(8,128)(2,1)}, u32[]{:S(2)}) copy-start(bf16[4096,1024]{1,0:T(8,128)(2,1)} %all-gather.4.cloned.1.call-done) | copy-start | bytes 25165828
Sparse Core Ops, SparseCore 0:
  39.6 74.4 all-gather.3

commit v10 on v9

--- a/solution.py
+++ b/solution.py
@@ -82,7 +82,7 @@
 
 
 def decode_kernel(update_ref, basis_ref, weight_ref, out_ref, new, sems):
-    two, ys, xs, zhs, piece, rank = basis_ref.shape
+    ys, xs, two, zhs, piece, rank = basis_ref.shape
     shard = two * ys * piece
     cols = STEP * shard
 
@@ -94,7 +94,7 @@
     steps = xs * zhs // STEP
     for i in range(steps):
         shards = [
-            basis_ref[:, :, f % xs, f // xs].reshape(shard, rank)
+            basis_ref[:, f % xs, :, f // xs].reshape(shard, rank)
             for f in range(i * STEP, (i + 1) * STEP)
         ]
         decoded = lax.dot_general(
@@ -113,7 +113,7 @@
 
 
 def decode(updates, basis_pieces, weight):
-    steps = basis_pieces.shape[2] * basis_pieces.shape[3] // STEP
+    steps = basis_pieces.shape[1] * basis_pieces.shape[3] // STEP
     return pl.pallas_call(
         decode_kernel,
         in_specs=[pl.BlockSpec(memory_space=pltpu.VMEM)] * 3,
@@ -131,7 +131,7 @@
 def local(activations, output_grads, basis, weight, first_moment, second_moment):
     core = lax.axis_index("c")
     piece = basis.shape[0] // 8
-    which = jnp.full((1,), core * 4 + lax.axis_index("y"), jnp.int32)
+    which = jnp.full((1,), lax.axis_index("y") * 2 + core, jnp.int32)
     partial_product, mine = product(activations, basis, which, piece)
     partial_product, mine, first = lax.optimization_barrier((partial_product, mine, core == 0))
     rows, rank = partial_product.shape
@@ -141,8 +141,8 @@
     mine = lax.all_gather(mine, "zh", axis=0, tiled=True)
     blocks, mine = lax.optimization_barrier((blocks, mine))
     over_x = jnp.sum(blocks.astype(jnp.float32), axis=0).astype(jnp.bfloat16)
-    basis_pieces = lax.all_gather(mine, ("c", "y", "x"), axis=0, tiled=True)
-    basis_pieces = basis_pieces.reshape(2, 4, 4, 4, piece, rank)
+    basis_pieces = lax.all_gather(mine, ("y", "x", "c"), axis=0, tiled=True)
+    basis_pieces = basis_pieces.reshape(4, 4, 2, 4, piece, rank)
 
     over_all = lax.all_gather(over_x, "zh", axis=0)
     block = jnp.sum(over_all.astype(jnp.float32), axis=0).astype(jnp.bfloat16)

time: 129 us -> 129 us (level)
  no operation moved by 1% of the time
where the time goes in v10:
time: 129 us
  blocking collectives  99.7 us (77%)
  between operations  14.1 us (11%)
  Pallas kernels  5.37 us (4%)
  starting transfers between devices  4.86 us (4%)
  local copies, waits for them, and re-layouts  3.48 us (3%)
    all_gather x1, blocking collectives, local(): mine = lax.all_gather(mine, 'zh', axis=0, tiled=True)  25.1 us
    all_to_all x2, blocking collectives, gather(): lax.all_to_all(copies, axis, 0, 0, tiled=True)  24.3 us
    all_gather x1, blocking collectives, local(): over_all = lax.all_gather(over_x, 'zh', axis=0)  22.5 us
    all_to_all x1, blocking collectives, exchange_sum(): parts = lax.all_to_all(parts, axis, 0, 0, tiled=True)  16.4 us
    all_gather x1, blocking collectives, local(): sent = lax.all_gather(send, 'c', axis=0)  6.98 us
    all_to_all x1, starting transfers between devices, local(): lax.all_to_all(partial_product.reshape(4, rows // 4, rank), 'x', 0, 0, ti...  4.85 us
    all_gather x1, blocking collectives, local(): updates = lax.all_gather(gather(update, ('zl', 'y')), 'c', axis=0)  4.31 us
    unnamed x10, local copies, waits for them, and re-layouts  3.41 us
  transfers between devices with their start and end apart: 2, of which 0 were waited for; matrix products, arithmetic and copies ran while one was open for 1% of the time, Pallas kernels for 0%

profile of v10, /device:TPU:1, one launch (start us, length us, event | category | flops | bytes accessed | tf_op | source)
XLA Modules:
  0.0 128.9 jit_solution(13641121255545269479)
XLA Ops:
  7.2 0.0 copy-start
  7.2 2.2 %product.1 = (bf16[256,1024]{1,0:T(8,128)(2,1)}, bf16[32,1024]{1,0:T(8,128)(2,1)}) custom-call(s32[1]{0:T(128)} %bitcast.start_ref, bf16[256,256]{1,0:T(8,128)(2,1)} %left_ref.1, bf16[256,1024]{1,0:T(8,128)(2,1)} %right_ref.1), custom_call_target="tpu_custom_call" | custom-call | tf_op jit(solution)/shard_map/product/pallas_call | solution.py:62
  9.4 4.9 %all-to-all-start = ((bf16[4,64,1024]{2,1,0:T(8,128)(2,1)}), bf16[4,64,1024]{2,1,0:T(8,128)(2,1)S(1)}, u32[]{:S(2)}, u32[]{:S(2)}) async-start(bf16[4,64,1024]{2,1,0:T(8,128)(2,1)} %bitcast.19), calls=%async_computation | async-start | bytes 1048576 | tf_op jit(solution)/shard_map/all_to_all | solution.py:138
  14.3 25.1 %all_gather.19 = bf16[128,1024]{1,0:T(8,128)(2,1)} all-gather(bf16[32,1024]{1,0:T(8,128)(2,1)} %get-tuple-element.14), channel_id=1, replica_groups=mesh['zl'=4,'y'=4,'c'=2,'zh'=4,'x'=4] {'zh'}, dimensions={0}, use_global_device_ids=true | all-gather | bytes 327680 | tf_op jit(solution)/shard_map/all_gather | solution.py:141
  39.4 0.0 all-to-all-done
  39.4 0.0 all-gather.4.cloned.1.call-update
  39.5 0.1 reduce_sum.33
  39.5 22.5 %all-gather = bf16[256,1024]{1,0:T(8,128)(2,1)S(1)} all-gather(bf16[64,1024]{1,0:T(8,128)(2,1)S(1)} %reduce_sum.33), channel_id=2, replica_groups=mesh['zl'=4,'y'=4,'c'=2,'zh'=4,'x'=4] {'zh'}, dimensions={0}, use_global_device_ids=true | all-gather | bytes 655360 | tf_op jit(solution)/shard_map/all_gather | solution.py:147
  62.1 0.1 reduce_sum.34
  62.2 0.1 broadcast_in_dim.7
  62.2 11.1 %all_to_all.20 = bf16[4,64,1024]{2,1,0:T(8,128)(2,1)S(1)} all-to-all(bf16[4,64,1024]{2,1,0:T(8,128)(2,1)S(1)} %broadcast_in_dim.7), channel_id=1, replica_groups=mesh['zl'=4,'y'=4,'c'=2,'zh'=4,'x'=4] {'x'}, dimensions={0} | all-to-all | bytes 1048576 | tf_op jit(solution)/shard_map/all_to_all | solution.py:34
  73.4 0.3 convolution_multiply_fusion
  73.7 0.0 copy-start.3
  73.7 0.0 copy-start.4
  73.7 0.1 select_convert_fusion
  73.8 7.0 %all-gather.1 = bf16[32,1,8,1024]{3,2,1,0:T(8,128)(2,1)S(1)} all-gather(bf16[16,1,8,1024]{3,2,1,0:T(8,128)(2,1)S(1)} %select_convert_fusion), channel_id=3, replica_groups=mesh['zl'=4,'y'=4,'c'=2,'zh'=4,'x'=4] {'c'}, dimensions={0}, use_global_device_ids=true | all-gather | bytes 786432 | tf_op jit(solution)/shard_map/all_gather | solution.py:159
  80.8 0.1 fusion
  80.9 16.4 %all_to_all.21 = bf16[16,8,1024]{2,1,0:T(8,128)(2,1)S(1)} all-to-all(bf16[16,8,1024]{2,1,0:T(8,128)(2,1)S(1)} %fusion), channel_id=1, replica_groups=mesh['zl'=4,'y'=4,'c'=2,'zh'=4,'x'=4] {'zl','y'}, dimensions={0} | all-to-all | bytes 524288 | tf_op jit(solution)/shard_map/all_to_all | solution.py:27
  97.4 0.0 copy-done.3
  97.4 0.6 divide_convert_fusion
  98.1 13.1 %all_to_all.22 = bf16[16,8,1024]{2,1,0:T(8,128)(2,1)S(1)} all-to-all(bf16[16,8,1024]{2,1,0:T(8,128)(2,1)S(1)} %broadcast_in_dim.8), channel_id=1, replica_groups=mesh['zl'=4,'y'=4,'c'=2,'zh'=4,'x'=4] {'zl','y'}, dimensions={0} | all-to-all | bytes 524288 | tf_op jit(solution)/shard_map/all_to_all | solution.py:34
  111.2 4.3 %all_gather.23.update_ref = bf16[2,128,1024]{2,1,0:T(8,128)(2,1)S(1)} all-gather(bf16[1,128,1024]{2,1,0:T(8,128)(2,1)S(1)} %bitcast.18), channel_id=1, replica_groups=mesh['zl'=4,'y'=4,'c'=2,'zh'=4,'x'=4] {'c'}, dimensions={0}, use_global_device_ids=true | all-gather | bytes 786432 | tf_op jit(solution)/shard_map/all_gather | solution.py:168
  115.5 3.4 %copy-done.1 = bf16[4096,1024]{1,0:T(8,128)(2,1)S(1)} copy-done((bf16[4096,1024]{1,0:T(8,128)(2,1)S(1)}, bf16[4096,1024]{1,0:T(8,128)(2,1)}, u32[]{:S(2)}) %copy-start.1) | copy-done | bytes 8388632
  118.9 3.1 %decode.1 = bf16[256,4096]{1,0:T(8,128)(2,1)} custom-call(bf16[2,128,1024]{2,1,0:T(8,128)(2,1)S(1)} %all_gather.23.update_ref, bf16[4,4,2,4,32,1024]{5,4,3,2,1,0:T(8,128)(2,1)S(1)} %bitcast.13, bf16[256,4096]{1,0:T(8,128)(2,1)S(1)} %copy-done.2), custom_call_target="tpu_custom_call" | custom-call | tf_op jit(solution)/shard_map/decode/pallas_call | solution.py:117
  (9 shorter events, 0.1 us)
Async XLA Ops:
  7.2 66.2 %copy-start = (bf16[256,256]{1,0:T(8,128)(2,1)S(1)}, bf16[256,256]{1,0:T(8,128)(2,1)}, u32[]{:S(2)}) copy-start(bf16[256,256]{1,0:T(8,128)(2,1)} %param.7) | copy-start | bytes 393220
  9.4 30.0 %all-to-all-start = ((bf16[4,64,1024]{2,1,0:T(8,128)(2,1)}), bf16[4,64,1024]{2,1,0:T(8,128)(2,1)S(1)}, u32[]{:S(2)}, u32[]{:S(2)}) async-start(bf16[4,64,1024]{2,1,0:T(8,128)(2,1)} %bitcast.19), calls=%async_computation | async-start | bytes 1048576 | tf_op jit(solution)/shard_map/all_to_all | solution.py:138
  14.3 101.2 %all-gather.4.cloned.1.call-start = ((), (), s32[]{:S(2)}) async-start(), calls=%async_computation.4 | async-start | bytes 8650752 | tf_op jit(solution)/shard_map/all_gather | solution.py:144
  73.7 23.7 %copy-start.3 = (f32[8,1024]{1,0:T(8,128)S(1)}, f32[8,1024]{1,0:T(8,128)}, u32[]{:S(2)}) copy-start(f32[8,1024]{1,0:T(8,128)} %param.10) | copy-start | bytes 98308
  73.7 23.7 %copy-start.4 = (f32[8,1024]{1,0:T(8,128)S(1)}, f32[8,1024]{1,0:T(8,128)}, u32[]{:S(2)}) copy-start(f32[8,1024]{1,0:T(8,128)} %param.11) | copy-start | bytes 98308
  80.8 34.7 %copy-start.2 = (bf16[256,4096]{1,0:T(8,128)(2,1)S(1)}, bf16[256,4096]{1,0:T(8,128)(2,1)}, u32[]{:S(2)}) copy-start(bf16[256,4096]{1,0:T(8,128)(2,1)} %weight_ref.1) | copy-start | bytes 6291460
  115.5 3.4 %copy-start.1 = (bf16[4096,1024]{1,0:T(8,128)(2,1)S(1)}, bf16[4096,1024]{1,0:T(8,128)(2,1)}, u32[]{:S(2)}) copy-start(bf16[4096,1024]{1,0:T(8,128)(2,1)} %all-gather.4.cloned.1.call-done) | copy-start | bytes 25165828
Sparse Core Ops, SparseCore 0:
  39.6 74.4 all-gather.3

commit v11 on v10

--- a/solution.py
+++ b/solution.py
@@ -49,7 +49,7 @@
     where = pl.ds(pl.multiple_of(start_ref[0] * rows, rows), rows)
     piece = pltpu.make_async_copy(right.at[where], piece_ref, sems.at[2])
     piece.start()
-    out[...] = jnp.dot(left[...], right[...], preferred_element_type=jnp.float32).astype(out.dtype)
+    out[...] = jnp.dot(left[...], right[...], preferred_element_type=jnp.float32)
     store = pltpu.make_async_copy(out, out_ref, sems.at[3])
     store.start()
     piece.wait()
@@ -64,13 +64,13 @@
         in_specs=[pl.BlockSpec(memory_space=pltpu.SMEM), anywhere, anywhere],
         out_specs=[anywhere, anywhere],
         out_shape=[
-            jax.ShapeDtypeStruct(shape, jnp.bfloat16),
+            jax.ShapeDtypeStruct(shape, jnp.float32),
             jax.ShapeDtypeStruct((rows, right.shape[1]), right.dtype),
         ],
         scratch_shapes=[
             pltpu.VMEM(left.shape, left.dtype),
             pltpu.VMEM(right.shape, right.dtype),
-            pltpu.VMEM(shape, jnp.bfloat16),
+            pltpu.VMEM(shape, jnp.float32),
             pltpu.SemaphoreType.DMA((4,)),
         ],
         compiler_params=pltpu.CompilerParams(vmem_limit_bytes=60 * 1024 * 1024),
@@ -140,7 +140,7 @@
     )
     mine = lax.all_gather(mine, "zh", axis=0, tiled=True)
     blocks, mine = lax.optimization_barrier((blocks, mine))
-    over_x = jnp.sum(blocks.astype(jnp.float32), axis=0).astype(jnp.bfloat16)
+    over_x = jnp.sum(blocks, axis=0).astype(jnp.bfloat16)
     basis_pieces = lax.all_gather(mine, ("y", "x", "c"), axis=0, tiled=True)
     basis_pieces = basis_pieces.reshape(4, 4, 2, 4, piece, rank)
 

time: 129 us -> 129 us (level)
    unnamed x10 -> x12, local copies, waits for them, and re-layouts: 3.41 us -> 3.41 us
where the time goes in v11:
time: 129 us
  blocking collectives  99.5 us (77%)
  between operations  14.2 us (11%)
  Pallas kernels  5.55 us (4%)
  starting transfers between devices  4.99 us (4%)
  local copies, waits for them, and re-layouts  3.48 us (3%)
    all_gather x1, blocking collectives, local(): mine = lax.all_gather(mine, 'zh', axis=0, tiled=True)  24.9 us
    all_to_all x2, blocking collectives, gather(): lax.all_to_all(copies, axis, 0, 0, tiled=True)  24.3 us
    all_gather x1, blocking collectives, local(): over_all = lax.all_gather(over_x, 'zh', axis=0)  22.5 us
    all_to_all x1, blocking collectives, exchange_sum(): parts = lax.all_to_all(parts, axis, 0, 0, tiled=True)  16.4 us
    all_gather x1, blocking collectives, local(): sent = lax.all_gather(send, 'c', axis=0)  6.99 us
    all_to_all x1, starting transfers between devices, local(): lax.all_to_all(partial_product.reshape(4, rows // 4, rank), 'x', 0, 0, ti...  4.99 us
    all_gather x1, blocking collectives, local(): updates = lax.all_gather(gather(update, ('zl', 'y')), 'c', axis=0)  4.31 us
    unnamed x12, local copies, waits for them, and re-layouts  3.41 us
  transfers between devices with their start and end apart: 2, of which 0 were waited for; matrix products, arithmetic and copies ran while one was open for 1% of the time, Pallas kernels for 0%

profile of v11, /device:TPU:1, one launch (start us, length us, event | category | flops | bytes accessed | tf_op | source)
XLA Modules:
  0.0 129.0 jit_solution(4141892055037039905)
XLA Ops:
  7.2 0.0 copy-start
  7.2 2.4 %product.1 = (f32[256,1024]{1,0:T(8,128)}, bf16[32,1024]{1,0:T(8,128)(2,1)}) custom-call(s32[1]{0:T(128)} %bitcast.start_ref, bf16[256,256]{1,0:T(8,128)(2,1)} %left_ref.1, bf16[256,1024]{1,0:T(8,128)(2,1)} %right_ref.1), custom_call_target="tpu_custom_call" | custom-call | tf_op jit(solution)/shard_map/product/pallas_call | solution.py:62
  9.6 5.0 %all-to-all-start = ((f32[4,64,1024]{2,1,0:T(8,128)}), f32[4,64,1024]{2,1,0:T(8,128)S(1)}, u32[]{:S(2)}, u32[]{:S(2)}) async-start(f32[4,64,1024]{2,1,0:T(8,128)} %bitcast.19), calls=%async_computation | async-start | bytes 2097152 | tf_op jit(solution)/shard_map/all_to_all | solution.py:138
  14.6 24.9 %all_gather.17 = bf16[128,1024]{1,0:T(8,128)(2,1)} all-gather(bf16[32,1024]{1,0:T(8,128)(2,1)S(1)} %copy-done.3), channel_id=1, replica_groups=mesh['zl'=4,'y'=4,'c'=2,'zh'=4,'x'=4] {'zh'}, dimensions={0}, use_global_device_ids=true | all-gather | bytes 327680 | tf_op jit(solution)/shard_map/all_gather | solution.py:141
  39.5 0.0 all-to-all-done
  39.5 0.0 all-gather.4.cloned.1.call-update
  39.6 0.1 reduce_sum.30
  39.6 22.5 %all-gather = bf16[256,1024]{1,0:T(8,128)(2,1)S(1)} all-gather(bf16[64,1024]{1,0:T(8,128)(2,1)S(1)} %reduce_sum.30), channel_id=2, replica_groups=mesh['zl'=4,'y'=4,'c'=2,'zh'=4,'x'=4] {'zh'}, dimensions={0}, use_global_device_ids=true | all-gather | bytes 655360 | tf_op jit(solution)/shard_map/all_gather | solution.py:147
  62.2 0.1 reduce_sum.31
  62.3 0.1 broadcast_in_dim.7
  62.3 11.1 %all_to_all.20 = bf16[4,64,1024]{2,1,0:T(8,128)(2,1)S(1)} all-to-all(bf16[4,64,1024]{2,1,0:T(8,128)(2,1)S(1)} %broadcast_in_dim.7), channel_id=1, replica_groups=mesh['zl'=4,'y'=4,'c'=2,'zh'=4,'x'=4] {'x'}, dimensions={0} | all-to-all | bytes 1048576 | tf_op jit(solution)/shard_map/all_to_all | solution.py:34
  73.5 0.3 convolution_multiply_fusion
  73.8 0.0 copy-start.4
  73.8 0.0 copy-start.5
  73.8 0.1 select_convert_fusion
  73.9 7.0 %all-gather.1 = bf16[32,1,8,1024]{3,2,1,0:T(8,128)(2,1)S(1)} all-gather(bf16[16,1,8,1024]{3,2,1,0:T(8,128)(2,1)S(1)} %select_convert_fusion), channel_id=3, replica_groups=mesh['zl'=4,'y'=4,'c'=2,'zh'=4,'x'=4] {'c'}, dimensions={0}, use_global_device_ids=true | all-gather | bytes 786432 | tf_op jit(solution)/shard_map/all_gather | solution.py:159
  80.9 0.1 fusion
  81.0 16.4 %all_to_all.21 = bf16[16,8,1024]{2,1,0:T(8,128)(2,1)S(1)} all-to-all(bf16[16,8,1024]{2,1,0:T(8,128)(2,1)S(1)} %fusion), channel_id=1, replica_groups=mesh['zl'=4,'y'=4,'c'=2,'zh'=4,'x'=4] {'zl','y'}, dimensions={0} | all-to-all | bytes 524288 | tf_op jit(solution)/shard_map/all_to_all | solution.py:27
  97.5 0.0 copy-done.5
  97.5 0.6 divide_convert_fusion
  98.2 13.1 %all_to_all.22 = bf16[16,8,1024]{2,1,0:T(8,128)(2,1)S(1)} all-to-all(bf16[16,8,1024]{2,1,0:T(8,128)(2,1)S(1)} %broadcast_in_dim.8), channel_id=1, replica_groups=mesh['zl'=4,'y'=4,'c'=2,'zh'=4,'x'=4] {'zl','y'}, dimensions={0} | all-to-all | bytes 524288 | tf_op jit(solution)/shard_map/all_to_all | solution.py:34
  111.3 4.3 %all_gather.20.update_ref = bf16[2,128,1024]{2,1,0:T(8,128)(2,1)S(1)} all-gather(bf16[1,128,1024]{2,1,0:T(8,128)(2,1)S(1)} %bitcast.18), channel_id=1, replica_groups=mesh['zl'=4,'y'=4,'c'=2,'zh'=4,'x'=4] {'c'}, dimensions={0}, use_global_device_ids=true | all-gather | bytes 786432 | tf_op jit(solution)/shard_map/all_gather | solution.py:168
  115.6 3.4 %copy-done.1 = bf16[4096,1024]{1,0:T(8,128)(2,1)S(1)} copy-done((bf16[4096,1024]{1,0:T(8,128)(2,1)S(1)}, bf16[4096,1024]{1,0:T(8,128)(2,1)}, u32[]{:S(2)}) %copy-start.1) | copy-done | bytes 8388632
  119.0 3.1 %decode.1 = bf16[256,4096]{1,0:T(8,128)(2,1)} custom-call(bf16[2,128,1024]{2,1,0:T(8,128)(2,1)S(1)} %all_gather.20.update_ref, bf16[4,4,2,4,32,1024]{5,4,3,2,1,0:T(8,128)(2,1)S(1)} %bitcast.13, bf16[256,4096]{1,0:T(8,128)(2,1)S(1)} %copy-done.2), custom_call_target="tpu_custom_call" | custom-call | tf_op jit(solution)/shard_map/decode/pallas_call | solution.py:117
  (11 shorter events, 0.1 us)
Async XLA Ops:
  7.2 66.3 %copy-start = (bf16[256,256]{1,0:T(8,128)(2,1)S(1)}, bf16[256,256]{1,0:T(8,128)(2,1)}, u32[]{:S(2)}) copy-start(bf16[256,256]{1,0:T(8,128)(2,1)} %param.7) | copy-start | bytes 393220
  9.6 5.0 %copy-start.3 = (bf16[32,1024]{1,0:T(8,128)(2,1)S(1)}, bf16[32,1024]{1,0:T(8,128)(2,1)}, u32[]{:S(2)}) copy-start(bf16[32,1024]{1,0:T(8,128)(2,1)} %get-tuple-element.14) | copy-start | bytes 196612
  9.6 29.9 %all-to-all-start = ((f32[4,64,1024]{2,1,0:T(8,128)}), f32[4,64,1024]{2,1,0:T(8,128)S(1)}, u32[]{:S(2)}, u32[]{:S(2)}) async-start(f32[4,64,1024]{2,1,0:T(8,128)} %bitcast.19), calls=%async_computation | async-start | bytes 2097152 | tf_op jit(solution)/shard_map/all_to_all | solution.py:138
  14.6 101.0 %all-gather.4.cloned.1.call-start = ((), (), s32[]{:S(2)}) async-start(), calls=%async_computation.4 | async-start | bytes 8650752 | tf_op jit(solution)/shard_map/all_gather | solution.py:144
  73.8 23.7 %copy-start.4 = (f32[8,1024]{1,0:T(8,128)S(1)}, f32[8,1024]{1,0:T(8,128)}, u32[]{:S(2)}) copy-start(f32[8,1024]{1,0:T(8,128)} %param.10) | copy-start | bytes 98308
  73.8 23.7 %copy-start.5 = (f32[8,1024]{1,0:T(8,128)S(1)}, f32[8,1024]{1,0:T(8,128)}, u32[]{:S(2)}) copy-start(f32[8,1024]{1,0:T(8,128)} %param.11) | copy-start | bytes 98308
  80.9 34.7 %copy-start.2 = (bf16[256,4096]{1,0:T(8,128)(2,1)S(1)}, bf16[256,4096]{1,0:T(8,128)(2,1)}, u32[]{:S(2)}) copy-start(bf16[256,4096]{1,0:T(8,128)(2,1)} %weight_ref.1) | copy-start | bytes 6291460
  115.6 3.4 %copy-start.1 = (bf16[4096,1024]{1,0:T(8,128)(2,1)S(1)}, bf16[4096,1024]{1,0:T(8,128)(2,1)}, u32[]{:S(2)}) copy-start(bf16[4096,1024]{1,0:T(8,128)(2,1)} %all-gather.4.cloned.1.call-done) | copy-start | bytes 25165828
Sparse Core Ops, SparseCore 0:
  39.7 74.4 all-gather.3

commit v12 on v11

--- a/solution.py
+++ b/solution.py
@@ -81,49 +81,67 @@
 STEP = 2
 
 
-def decode_kernel(update_ref, basis_ref, weight_ref, out_ref, new, sems):
+def decode_kernel(update_ref, basis_ref, weight_ref, out_ref, held, new, in_sems, out_sems):
     ys, xs, two, zhs, piece, rank = basis_ref.shape
     shard = two * ys * piece
-    cols = STEP * shard
-
-    def copy_out(i):
-        where = pl.ds(i * cols, cols)
-        return pltpu.make_async_copy(new.at[:, where], out_ref.at[:, where], sems.at[i])
-
+    parts = [(x, z) for x in range(xs) for z in range(0, zhs, STEP)]
+
+    def copy_in(i):
+        x, z = parts[i]
+        return pltpu.make_async_copy(
+            basis_ref.at[:, x, :, pl.ds(z, STEP)], held.at[i], in_sems.at[i]
+        )
+
+    def copy_out(i, k):
+        x, z = parts[i]
+        where = pl.ds(((z + k) * xs + x) * shard, shard)
+        return pltpu.make_async_copy(
+            new.at[:, where], out_ref.at[:, where], out_sems.at[i * STEP + k]
+        )
+
+    for i in range(len(parts)):
+        copy_in(i).start()
     updates = update_ref[...].reshape(-1, rank)
-    steps = xs * zhs // STEP
-    for i in range(steps):
-        shards = [
-            basis_ref[:, f % xs, :, f // xs].reshape(shard, rank)
-            for f in range(i * STEP, (i + 1) * STEP)
-        ]
+    for i, (x, z) in enumerate(parts):
+        copy_in(i).wait()
+        shards = [held[i, :, :, k].reshape(shard, rank) for k in range(STEP)]
         decoded = lax.dot_general(
             updates,
             jnp.concatenate(shards, axis=0),
             (((1,), (1,)), ((), ())),
             preferred_element_type=jnp.float32,
         )
-        decoded = decoded.reshape(2, -1, 8, cols)
-        decoded = jnp.stack([decoded[0], decoded[1]], axis=1).reshape(-1, cols)
-        old = weight_ref[:, i * cols : (i + 1) * cols].astype(jnp.float32)
-        new[:, i * cols : (i + 1) * cols] = (old - step_rate * decoded).astype(new.dtype)
-        copy_out(i).start()
-    for i in range(steps):
-        copy_out(i).wait()
+        decoded = decoded.reshape(2, -1, 8, STEP * shard)
+        decoded = jnp.stack([decoded[0], decoded[1]], axis=1).reshape(-1, STEP * shard)
+        for k in range(STEP):
+            start = ((z + k) * xs + x) * shard
+            old = weight_ref[:, start : start + shard].astype(jnp.float32)
+            new[:, start : start + shard] = (
+                old - step_rate * decoded[:, k * shard : (k + 1) * shard]
+            ).astype(new.dtype)
+            copy_out(i, k).start()
+    for i in range(len(parts)):
+        for k in range(STEP):
+            copy_out(i, k).wait()
 
 
 def decode(updates, basis_pieces, weight):
-    steps = basis_pieces.shape[1] * basis_pieces.shape[3] // STEP
+    ys, xs, two, zhs, piece, rank = basis_pieces.shape
+    steps = xs * zhs // STEP
+    vmem = pl.BlockSpec(memory_space=pltpu.VMEM)
+    anywhere = pl.BlockSpec(memory_space=pl.ANY)
     return pl.pallas_call(
         decode_kernel,
-        in_specs=[pl.BlockSpec(memory_space=pltpu.VMEM)] * 3,
-        out_specs=pl.BlockSpec(memory_space=pl.ANY),
+        in_specs=[vmem, anywhere, vmem],
+        out_specs=anywhere,
         out_shape=jax.ShapeDtypeStruct(weight.shape, weight.dtype),
         scratch_shapes=[
+            pltpu.VMEM((steps, ys, two, STEP, piece, rank), basis_pieces.dtype),
             pltpu.VMEM(weight.shape, weight.dtype),
             pltpu.SemaphoreType.DMA((steps,)),
+            pltpu.SemaphoreType.DMA((steps * STEP,)),
         ],
-        compiler_params=pltpu.CompilerParams(vmem_limit_bytes=24 * 1024 * 1024),
+        compiler_params=pltpu.CompilerParams(vmem_limit_bytes=46 * 1024 * 1024),
         name="decode",
     )(updates, basis_pieces, weight)
 

time: 129 us -> 129 us (level)
  local copies, waits for them, and re-layouts: 3.48 us -> 0.1 us
  Pallas kernels: 5.55 us -> 8.46 us
    unnamed x12 -> x10, local copies, waits for them, and re-layouts: 3.41 us -> 0.03 us
    pallas_call x1, Pallas kernels: 3.14 us -> 6.06 us  [decode(): pl.pallas_call(decode_kernel, in_specs=[vmem, anywhere, vmem], out_specs=...]
where the time goes in v12:
time: 129 us
  blocking collectives  99.5 us (77%)
  between operations  14.2 us (11%)
  Pallas kernels  8.46 us (7%)
  starting transfers between devices  4.99 us (4%)
    all_gather x1, blocking collectives, local(): mine = lax.all_gather(mine, 'zh', axis=0, tiled=True)  24.9 us
    all_to_all x2, blocking collectives, gather(): lax.all_to_all(copies, axis, 0, 0, tiled=True)  24.3 us
    all_gather x1, blocking collectives, local(): over_all = lax.all_gather(over_x, 'zh', axis=0)  22.5 us
    all_to_all x1, blocking collectives, exchange_sum(): parts = lax.all_to_all(parts, axis, 0, 0, tiled=True)  16.4 us
    all_gather x1, blocking collectives, local(): sent = lax.all_gather(send, 'c', axis=0)  6.99 us
    pallas_call x1, Pallas kernels, decode(): pl.pallas_call(decode_kernel, in_specs=[vmem, anywhere, vmem], out_specs=...  6.06 us
    all_to_all x1, starting transfers between devices, local(): lax.all_to_all(partial_product.reshape(4, rows // 4, rank), 'x', 0, 0, ti...  4.99 us
    all_gather x1, blocking collectives, local(): updates = lax.all_gather(gather(update, ('zl', 'y')), 'c', axis=0)  4.31 us
  transfers between devices with their start and end apart: 2, of which 0 were waited for; matrix products, arithmetic and copies ran while one was open for 1% of the time, Pallas kernels for 0%

profile of v12, /device:TPU:1, one launch (start us, length us, event | category | flops | bytes accessed | tf_op | source)
XLA Modules:
  0.0 128.5 jit_solution(3133684745072620628)
XLA Ops:
  7.2 0.0 copy-start
  7.2 2.4 %product.1 = (f32[256,1024]{1,0:T(8,128)}, bf16[32,1024]{1,0:T(8,128)(2,1)}) custom-call(s32[1]{0:T(128)} %bitcast.start_ref, bf16[256,256]{1,0:T(8,128)(2,1)} %left_ref.1, bf16[256,1024]{1,0:T(8,128)(2,1)} %right_ref.1), custom_call_target="tpu_custom_call" | custom-call | tf_op jit(solution)/shard_map/product/pallas_call | solution.py:62
  9.6 5.0 %all-to-all-start = ((f32[4,64,1024]{2,1,0:T(8,128)}), f32[4,64,1024]{2,1,0:T(8,128)S(1)}, u32[]{:S(2)}, u32[]{:S(2)}) async-start(f32[4,64,1024]{2,1,0:T(8,128)} %bitcast.19), calls=%async_computation | async-start | bytes 2097152 | tf_op jit(solution)/shard_map/all_to_all | solution.py:156
  14.6 0.0 all-gather.4.cloned.1.call-start
  14.6 24.9 %all_gather.17 = bf16[128,1024]{1,0:T(8,128)(2,1)} all-gather(bf16[32,1024]{1,0:T(8,128)(2,1)S(1)} %copy-done.2), channel_id=1, replica_groups=mesh['zl'=4,'y'=4,'c'=2,'zh'=4,'x'=4] {'zh'}, dimensions={0}, use_global_device_ids=true | all-gather | bytes 327680 | tf_op jit(solution)/shard_map/all_gather | solution.py:159
  39.5 0.0 all-to-all-done
  39.5 0.0 all-gather.4.cloned.1.call-update
  39.6 0.1 reduce_sum.30
  39.6 22.5 %all-gather = bf16[256,1024]{1,0:T(8,128)(2,1)S(1)} all-gather(bf16[64,1024]{1,0:T(8,128)(2,1)S(1)} %reduce_sum.30), channel_id=2, replica_groups=mesh['zl'=4,'y'=4,'c'=2,'zh'=4,'x'=4] {'zh'}, dimensions={0}, use_global_device_ids=true | all-gather | bytes 655360 | tf_op jit(solution)/shard_map/all_gather | solution.py:165
  62.2 0.1 reduce_sum.31
  62.3 0.1 broadcast_in_dim.7
  62.3 11.1 %all_to_all.20 = bf16[4,64,1024]{2,1,0:T(8,128)(2,1)S(1)} all-to-all(bf16[4,64,1024]{2,1,0:T(8,128)(2,1)S(1)} %broadcast_in_dim.7), channel_id=1, replica_groups=mesh['zl'=4,'y'=4,'c'=2,'zh'=4,'x'=4] {'x'}, dimensions={0} | all-to-all | bytes 1048576 | tf_op jit(solution)/shard_map/all_to_all | solution.py:34
  73.5 0.3 convolution_multiply_fusion
  73.8 0.0 copy-start.3
  73.8 0.0 copy-start.4
  73.8 0.1 select_convert_fusion
  73.9 7.0 %all-gather.1 = bf16[32,1,8,1024]{3,2,1,0:T(8,128)(2,1)S(1)} all-gather(bf16[16,1,8,1024]{3,2,1,0:T(8,128)(2,1)S(1)} %select_convert_fusion), channel_id=3, replica_groups=mesh['zl'=4,'y'=4,'c'=2,'zh'=4,'x'=4] {'c'}, dimensions={0}, use_global_device_ids=true | all-gather | bytes 786432 | tf_op jit(solution)/shard_map/all_gather | solution.py:177
  80.9 0.1 fusion
  81.0 16.4 %all_to_all.21 = bf16[16,8,1024]{2,1,0:T(8,128)(2,1)S(1)} all-to-all(bf16[16,8,1024]{2,1,0:T(8,128)(2,1)S(1)} %fusion), channel_id=1, replica_groups=mesh['zl'=4,'y'=4,'c'=2,'zh'=4,'x'=4] {'zl','y'}, dimensions={0} | all-to-all | bytes 524288 | tf_op jit(solution)/shard_map/all_to_all | solution.py:27
  97.5 0.0 copy-done.3
  97.5 0.6 divide_convert_fusion
  98.2 13.1 %all_to_all.22 = bf16[16,8,1024]{2,1,0:T(8,128)(2,1)S(1)} all-to-all(bf16[16,8,1024]{2,1,0:T(8,128)(2,1)S(1)} %broadcast_in_dim.8), channel_id=1, replica_groups=mesh['zl'=4,'y'=4,'c'=2,'zh'=4,'x'=4] {'zl','y'}, dimensions={0} | all-to-all | bytes 524288 | tf_op jit(solution)/shard_map/all_to_all | solution.py:34
  111.3 4.3 %all_gather.20.update_ref = bf16[2,128,1024]{2,1,0:T(8,128)(2,1)S(1)} all-gather(bf16[1,128,1024]{2,1,0:T(8,128)(2,1)S(1)} %bitcast.18), channel_id=1, replica_groups=mesh['zl'=4,'y'=4,'c'=2,'zh'=4,'x'=4] {'c'}, dimensions={0}, use_global_device_ids=true | all-gather | bytes 786432 | tf_op jit(solution)/shard_map/all_gather | solution.py:186
  115.6 6.1 %decode.1 = bf16[256,4096]{1,0:T(8,128)(2,1)} custom-call(bf16[2,128,1024]{2,1,0:T(8,128)(2,1)S(1)} %all_gather.20.update_ref, bf16[4,4,2,4,32,1024]{5,4,3,2,1,0:T(8,128)(2,1)} %bitcast.13, bf16[256,4096]{1,0:T(8,128)(2,1)S(1)} %copy-done.1), custom_call_target="tpu_custom_call" | custom-call | tf_op jit(solution)/shard_map/decode/pallas_call | solution.py:133
  (9 shorter events, 0.1 us)
Async XLA Ops:
  7.2 66.3 %copy-start = (bf16[256,256]{1,0:T(8,128)(2,1)S(1)}, bf16[256,256]{1,0:T(8,128)(2,1)}, u32[]{:S(2)}) copy-start(bf16[256,256]{1,0:T(8,128)(2,1)} %param.7) | copy-start | bytes 393220
  9.6 5.0 %copy-start.2 = (bf16[32,1024]{1,0:T(8,128)(2,1)S(1)}, bf16[32,1024]{1,0:T(8,128)(2,1)}, u32[]{:S(2)}) copy-start(bf16[32,1024]{1,0:T(8,128)(2,1)} %get-tuple-element.14) | copy-start | bytes 196612
  9.6 29.9 %all-to-all-start = ((f32[4,64,1024]{2,1,0:T(8,128)}), f32[4,64,1024]{2,1,0:T(8,128)S(1)}, u32[]{:S(2)}, u32[]{:S(2)}) async-start(f32[4,64,1024]{2,1,0:T(8,128)} %bitcast.19), calls=%async_computation | async-start | bytes 2097152 | tf_op jit(solution)/shard_map/all_to_all | solution.py:156
  14.6 101.0 %all-gather.4.cloned.1.call-start = ((), (), s32[]{:S(2)}) async-start(), calls=%async_computation.4 | async-start | bytes 8650752 | tf_op jit(solution)/shard_map/all_gather | solution.py:162
  73.8 23.7 %copy-start.3 = (f32[8,1024]{1,0:T(8,128)S(1)}, f32[8,1024]{1,0:T(8,128)}, u32[]{:S(2)}) copy-start(f32[8,1024]{1,0:T(8,128)} %param.10) | copy-start | bytes 98308
  73.8 23.7 %copy-start.4 = (f32[8,1024]{1,0:T(8,128)S(1)}, f32[8,1024]{1,0:T(8,128)}, u32[]{:S(2)}) copy-start(f32[8,1024]{1,0:T(8,128)} %param.11) | copy-start | bytes 98308
  80.9 34.7 %copy-start.1 = (bf16[256,4096]{1,0:T(8,128)(2,1)S(1)}, bf16[256,4096]{1,0:T(8,128)(2,1)}, u32[]{:S(2)}) copy-start(bf16[256,4096]{1,0:T(8,128)(2,1)} %weight_ref.1) | copy-start | bytes 6291460
Sparse Core Ops, SparseCore 0:
  39.7 74.4 all-gather.3

commit v13 on v12

--- a/solution.py
+++ b/solution.py
@@ -34,6 +34,9 @@
     return lax.all_to_all(copies, axis, 0, 0, tiled=True).reshape(
         size * value.shape[0], value.shape[1]
     )
+
+
+BLOCKS = 4
 
 
 def product_kernel(start_ref, left_ref, right_ref, out_ref, piece_ref, left, right, out, sems):
@@ -49,11 +52,17 @@
     where = pl.ds(pl.multiple_of(start_ref[0] * rows, rows), rows)
     piece = pltpu.make_async_copy(right.at[where], piece_ref, sems.at[2])
     piece.start()
-    out[...] = jnp.dot(left[...], right[...], preferred_element_type=jnp.float32)
-    store = pltpu.make_async_copy(out, out_ref, sems.at[3])
-    store.start()
+    stores = []
+    step = out.shape[0] // BLOCKS
+    for i in range(BLOCKS):
+        block = pl.ds(i * step, step)
+        out[block] = jnp.dot(left[block], right[...], preferred_element_type=jnp.float32)
+        store = pltpu.make_async_copy(out.at[block], out_ref.at[block], sems.at[3 + i])
+        store.start()
+        stores.append(store)
     piece.wait()
-    store.wait()
+    for store in stores:
+        store.wait()
 
 
 def product(left, right, which, rows):
@@ -71,7 +80,7 @@
             pltpu.VMEM(left.shape, left.dtype),
             pltpu.VMEM(right.shape, right.dtype),
             pltpu.VMEM(shape, jnp.float32),
-            pltpu.SemaphoreType.DMA((4,)),
+            pltpu.SemaphoreType.DMA((3 + BLOCKS,)),
         ],
         compiler_params=pltpu.CompilerParams(vmem_limit_bytes=60 * 1024 * 1024),
         name="product",

time: 129 us -> 129 us (level)
  no operation moved by 1% of the time
where the time goes in v13:
time: 129 us; the launch traced here: 128 us
  blocking collectives  99.5 us (77%)
  between operations  14.2 us (11%)
  Pallas kernels  8.43 us (7%)
  starting transfers between devices  4.99 us (4%)
    all_gather x1, blocking collectives, local(): mine = lax.all_gather(mine, 'zh', axis=0, tiled=True)  24.9 us
    all_to_all x2, blocking collectives, gather(): lax.all_to_all(copies, axis, 0, 0, tiled=True)  24.3 us
    all_gather x1, blocking collectives, local(): over_all = lax.all_gather(over_x, 'zh', axis=0)  22.6 us
    all_to_all x1, blocking collectives, exchange_sum(): parts = lax.all_to_all(parts, axis, 0, 0, tiled=True)  16.4 us
    all_gather x1, blocking collectives, local(): sent = lax.all_gather(send, 'c', axis=0)  6.96 us
    pallas_call x1, Pallas kernels, decode(): pl.pallas_call(decode_kernel, in_specs=[vmem, anywhere, vmem], out_specs=...  6.06 us
    all_to_all x1, starting transfers between devices, local(): lax.all_to_all(partial_product.reshape(4, rows // 4, rank), 'x', 0, 0, ti...  4.99 us
    all_gather x1, blocking collectives, local(): updates = lax.all_gather(gather(update, ('zl', 'y')), 'c', axis=0)  4.3 us
  transfers between devices with their start and end apart: 2, of which 0 were waited for; matrix products, arithmetic and copies ran while one was open for 1% of the time, Pallas kernels for 0%

profile of v13, /device:TPU:1, one launch (start us, length us, event | category | flops | bytes accessed | tf_op | source)
XLA Modules:
  0.0 128.5 jit_solution(5675609923350972580)
XLA Ops:
  7.2 0.0 copy-start
  7.2 2.4 %product.1 = (f32[256,1024]{1,0:T(8,128)}, bf16[32,1024]{1,0:T(8,128)(2,1)}) custom-call(s32[1]{0:T(128)} %bitcast.start_ref, bf16[256,256]{1,0:T(8,128)(2,1)} %left_ref.1, bf16[256,1024]{1,0:T(8,128)(2,1)} %right_ref.1), custom_call_target="tpu_custom_call" | custom-call | tf_op jit(solution)/shard_map/product/pallas_call | solution.py:71
  9.6 0.0 copy-start.2
  9.6 5.0 %all-to-all-start = ((f32[4,64,1024]{2,1,0:T(8,128)}), f32[4,64,1024]{2,1,0:T(8,128)S(1)}, u32[]{:S(2)}, u32[]{:S(2)}) async-start(f32[4,64,1024]{2,1,0:T(8,128)} %bitcast.19), calls=%async_computation | async-start | bytes 2097152 | tf_op jit(solution)/shard_map/all_to_all | solution.py:165
  14.6 0.0 all-gather.4.cloned.1.call-start
  14.6 24.9 %all_gather.17 = bf16[128,1024]{1,0:T(8,128)(2,1)} all-gather(bf16[32,1024]{1,0:T(8,128)(2,1)S(1)} %copy-done.2), channel_id=1, replica_groups=mesh['zl'=4,'y'=4,'c'=2,'zh'=4,'x'=4] {'zh'}, dimensions={0}, use_global_device_ids=true | all-gather | bytes 327680 | tf_op jit(solution)/shard_map/all_gather | solution.py:168
  39.5 0.0 all-to-all-done
  39.5 0.0 all-gather.4.cloned.1.call-update
  39.5 0.1 reduce_sum.30
  39.6 22.6 %all-gather = bf16[256,1024]{1,0:T(8,128)(2,1)S(1)} all-gather(bf16[64,1024]{1,0:T(8,128)(2,1)S(1)} %reduce_sum.30), channel_id=2, replica_groups=mesh['zl'=4,'y'=4,'c'=2,'zh'=4,'x'=4] {'zh'}, dimensions={0}, use_global_device_ids=true | all-gather | bytes 655360 | tf_op jit(solution)/shard_map/all_gather | solution.py:174
  62.2 0.1 reduce_sum.31
  62.3 0.1 broadcast_in_dim.7
  62.3 11.2 %all_to_all.20 = bf16[4,64,1024]{2,1,0:T(8,128)(2,1)S(1)} all-to-all(bf16[4,64,1024]{2,1,0:T(8,128)(2,1)S(1)} %broadcast_in_dim.7), channel_id=1, replica_groups=mesh['zl'=4,'y'=4,'c'=2,'zh'=4,'x'=4] {'x'}, dimensions={0} | all-to-all | bytes 1048576 | tf_op jit(solution)/shard_map/all_to_all | solution.py:34
  73.5 0.3 convolution_multiply_fusion
  73.8 0.0 copy-start.3
  73.8 0.0 copy-start.4
  73.9 0.1 select_convert_fusion
  73.9 7.0 %all-gather.1 = bf16[32,1,8,1024]{3,2,1,0:T(8,128)(2,1)S(1)} all-gather(bf16[16,1,8,1024]{3,2,1,0:T(8,128)(2,1)S(1)} %select_convert_fusion), channel_id=3, replica_groups=mesh['zl'=4,'y'=4,'c'=2,'zh'=4,'x'=4] {'c'}, dimensions={0}, use_global_device_ids=true | all-gather | bytes 786432 | tf_op jit(solution)/shard_map/all_gather | solution.py:186
  80.9 0.1 fusion
  81.0 16.4 %all_to_all.21 = bf16[16,8,1024]{2,1,0:T(8,128)(2,1)S(1)} all-to-all(bf16[16,8,1024]{2,1,0:T(8,128)(2,1)S(1)} %fusion), channel_id=1, replica_groups=mesh['zl'=4,'y'=4,'c'=2,'zh'=4,'x'=4] {'zl','y'}, dimensions={0} | all-to-all | bytes 524288 | tf_op jit(solution)/shard_map/all_to_all | solution.py:27
  97.5 0.6 divide_convert_fusion
  98.1 13.1 %all_to_all.22 = bf16[16,8,1024]{2,1,0:T(8,128)(2,1)S(1)} all-to-all(bf16[16,8,1024]{2,1,0:T(8,128)(2,1)S(1)} %broadcast_in_dim.8), channel_id=1, replica_groups=mesh['zl'=4,'y'=4,'c'=2,'zh'=4,'x'=4] {'zl','y'}, dimensions={0} | all-to-all | bytes 524288 | tf_op jit(solution)/shard_map/all_to_all | solution.py:34
  111.3 4.3 %all_gather.20.update_ref = bf16[2,128,1024]{2,1,0:T(8,128)(2,1)S(1)} all-gather(bf16[1,128,1024]{2,1,0:T(8,128)(2,1)S(1)} %bitcast.18), channel_id=1, replica_groups=mesh['zl'=4,'y'=4,'c'=2,'zh'=4,'x'=4] {'c'}, dimensions={0}, use_global_device_ids=true | all-gather | bytes 786432 | tf_op jit(solution)/shard_map/all_gather | solution.py:195
  115.6 6.1 %decode.1 = bf16[256,4096]{1,0:T(8,128)(2,1)} custom-call(bf16[2,128,1024]{2,1,0:T(8,128)(2,1)S(1)} %all_gather.20.update_ref, bf16[4,4,2,4,32,1024]{5,4,3,2,1,0:T(8,128)(2,1)} %bitcast.13, bf16[256,4096]{1,0:T(8,128)(2,1)S(1)} %copy-done.1), custom_call_target="tpu_custom_call" | custom-call | tf_op jit(solution)/shard_map/decode/pallas_call | solution.py:142
  (9 shorter events, 0.1 us)
Async XLA Ops:
  7.2 66.3 %copy-start = (bf16[256,256]{1,0:T(8,128)(2,1)S(1)}, bf16[256,256]{1,0:T(8,128)(2,1)}, u32[]{:S(2)}) copy-start(bf16[256,256]{1,0:T(8,128)(2,1)} %param.7) | copy-start | bytes 393220
  9.6 5.0 %copy-start.2 = (bf16[32,1024]{1,0:T(8,128)(2,1)S(1)}, bf16[32,1024]{1,0:T(8,128)(2,1)}, u32[]{:S(2)}) copy-start(bf16[32,1024]{1,0:T(8,128)(2,1)} %get-tuple-element.14) | copy-start | bytes 196612
  9.6 29.9 %all-to-all-start = ((f32[4,64,1024]{2,1,0:T(8,128)}), f32[4,64,1024]{2,1,0:T(8,128)S(1)}, u32[]{:S(2)}, u32[]{:S(2)}) async-start(f32[4,64,1024]{2,1,0:T(8,128)} %bitcast.19), calls=%async_computation | async-start | bytes 2097152 | tf_op jit(solution)/shard_map/all_to_all | solution.py:165
  14.6 101.0 %all-gather.4.cloned.1.call-start = ((), (), s32[]{:S(2)}) async-start(), calls=%async_computation.4 | async-start | bytes 8650752 | tf_op jit(solution)/shard_map/all_gather | solution.py:171
  73.8 23.6 %copy-start.3 = (f32[8,1024]{1,0:T(8,128)S(1)}, f32[8,1024]{1,0:T(8,128)}, u32[]{:S(2)}) copy-start(f32[8,1024]{1,0:T(8,128)} %param.10) | copy-start | bytes 98308
  73.8 23.6 %copy-start.4 = (f32[8,1024]{1,0:T(8,128)S(1)}, f32[8,1024]{1,0:T(8,128)}, u32[]{:S(2)}) copy-start(f32[8,1024]{1,0:T(8,128)} %param.11) | copy-start | bytes 98308
  80.9 34.7 %copy-start.1 = (bf16[256,4096]{1,0:T(8,128)(2,1)S(1)}, bf16[256,4096]{1,0:T(8,128)(2,1)}, u32[]{:S(2)}) copy-start(bf16[256,4096]{1,0:T(8,128)(2,1)} %weight_ref.1) | copy-start | bytes 6291460
Sparse Core Ops, SparseCore 0:
  39.7 74.3 all-gather.3
